TPU v7x, 32 devices: a whole 2x2x4 slice. The times are simulated.
32 devices in a mesh: groups: 2 (over x), role: 2 (over core), seq: 8 (over z, y).
Axes of the slice: x: 2, y: 2, z: 4, core: 2. Of those that a mesh axis runs over, the one named last changes fastest.
Arguments:
- kv_store: bfloat16 [2, 8192, 1024], P('role', ('groups', 'seq')), parts along dimension 1, may hold values from -6 to 6
- queries: bfloat16 [2, 256, 2, 4096], P('role', ('groups', 'seq')), parts along dimension 1, may hold values from -100 to 100
- step_kv: bfloat16 [256, 2, 1024], P(('groups', 'seq')), parts along dimension 0, may hold values from -6 to 6
- suffix_pages: int32 [256, 2], P(('groups', 'seq')), parts along dimension 0, may hold values from 0 to 31, as said below
- suffix_len: int32 [256], P(('groups', 'seq')), parts along dimension 0, may hold values from 2 to 32, as said below
- owner: int32 [256, 1], P(('groups', 'seq')), parts along dimension 0, may hold values from 0 to 7; in each aligned block of 16 rows (0 to 15, 16 to 31, ...) at most 4 rows name the same one
- parent_id: int32 [256], P(('groups', 'seq')), parts along dimension 0, may hold values from 0 to 1
- parent_pages: int32 [32, 16], P(('groups', 'seq')), parts along dimension 0, may hold values from 0 to 31, as said below
- parent_len: int32 [32], P(('groups', 'seq')), parts along dimension 0, may hold values from 1 to 256, as said below
Outputs:
- served: bfloat16 [2, 256, 2, 4096], P('role', ('groups', 'seq')), parts along dimension 1
There are 2 independent parts, one for each index of `groups`. A program takes and returns all parts, laid end to end along the dimension named above; each array names one. Nothing has to cross between parts.
Inputs may be any that keep to these rules, and one draw needn't show every extreme that they name: `suffix_pages`: on each device the page lists of its 16 requests are disjoint and together name every page of its store once. `suffix_len`: the first request of every device has the full 32 tokens. Of the requests of one device at most 4 go to one owner, and some device sends 4 to one owner. `parent_pages`: on each device the page tables of its 2 parent slots are disjoint and together name every page of its store once. `parent_len`: the first parent slot of every device has the full 256 tokens.
All inputs are finite; a program needn't handle non-finite values.
Results may differ from a plain program's by a relative error of at most 0.0025.
Values may be sent and summed in bfloat16 or wider, within the bound.
No kernel may reach another device: no remote copies, remote signals or barrier semaphores. Data moves between devices by JAX's collectives and lax.ppermute only.
A program may use at most 128 MiB of HBM per device.

v0:
```python
import jax
import jax.numpy as jnp
from jax import lax
from jax.sharding import PartitionSpec as P

HEAD_DIM = 128
KV_HEADS = 4
GROUP = 8
PAGE = 16


MASKED_SCORE = -1e30


def as_sent(shard):

    def short(part):
        return part.astype(jnp.bfloat16) if part.dtype == jnp.float32 else part

    return jax.tree.map(short, shard)


def passed_along(block, axis, distance):
    devices = range(lax.axis_size(axis))
    route = [(i - distance, i) for i in devices if i - distance in devices]
    return lax.ppermute(block, axis, route)


def split_heads(kv_rows):
    key_width = KV_HEADS * HEAD_DIM
    shape_head = kv_rows.shape[:-1] + (KV_HEADS, HEAD_DIM)
    return (
        kv_rows[..., :key_width].reshape(shape_head),
        kv_rows[..., key_width:].reshape(shape_head),
    )


def prefill_rows(query_rows, suffix_kv, lengths):
    request_count = query_rows.shape[0]
    query_heads = query_rows.reshape(request_count, 2, KV_HEADS, GROUP, HEAD_DIM)
    key_rows, value_rows = split_heads(suffix_kv)
    scores = jnp.einsum(
        "rtgqh,rugh->rtgqu", query_heads, key_rows, preferred_element_type=jnp.float32
    ) * HEAD_DIM ** (-0.5)
    positions = jnp.arange(suffix_kv.shape[1])
    last_seen = lengths[:, None] - 2 + jnp.arange(2)[None, :]
    keep_mask = positions[None, None, :] <= last_seen[:, :, None]
    scores = jnp.where(keep_mask[:, :, None, None, :], scores, MASKED_SCORE)
    row_max = jnp.max(scores, axis=-1, keepdims=True)
    exp_terms = jnp.exp(scores - row_max)
    row_total = jnp.sum(exp_terms, axis=-1)
    blended = jnp.einsum(
        "rtgqu,rugh->rtgqh",
        exp_terms.astype(jnp.bfloat16),
        value_rows,
        preferred_element_type=jnp.float32,
    )
    return (blended / row_total[..., None]).astype(jnp.bfloat16).reshape(request_count, 2, -1)


def decode_rows(
    page_slots, query_slots, step_slots, meta_slots, parent_kv, parent_of, parent_pos, parent_cut
):
    slot_count = page_slots.shape[0]
    kv_width = parent_kv.shape[1]
    query_heads = query_slots.reshape(slot_count, 2, KV_HEADS, GROUP, HEAD_DIM)
    suffix_keys, suffix_values = split_heads(page_slots.reshape(slot_count, -1, kv_width))
    step_keys, step_values = split_heads(step_slots.reshape(slot_count, 2, kv_width))
    parent_keys, parent_values = split_heads(parent_kv)
    keep_parent = (parent_of[None, :] == meta_slots[:, 0:1]) & (
        parent_pos[None, :] < parent_cut[None, :]
    )
    keep_suffix = jnp.arange(suffix_keys.shape[1])[None, :] < meta_slots[:, 1:2]
    keep_step = jnp.arange(2)[None, :] <= jnp.arange(2)[:, None]
    scale = HEAD_DIM ** (-0.5)
    results = []
    for kv_head in range(KV_HEADS):
        query_one = query_heads[:, :, kv_head]
        score_parent = (
            jnp.einsum(
                "rtqh,ph->rtqp",
                query_one,
                parent_keys[:, kv_head],
                preferred_element_type=jnp.float32,
            )
            * scale
        )
        score_parent = jnp.where(keep_parent[:, None, None, :], score_parent, MASKED_SCORE)
        score_suffix = (
            jnp.einsum(
                "rtqh,ruh->rtqu",
                query_one,
                suffix_keys[:, :, kv_head],
                preferred_element_type=jnp.float32,
            )
            * scale
        )
        score_suffix = jnp.where(keep_suffix[:, None, None, :], score_suffix, MASKED_SCORE)
        score_step = (
            jnp.einsum(
                "rtqh,rnh->rtqn",
                query_one,
                step_keys[:, :, kv_head],
                preferred_element_type=jnp.float32,
            )
            * scale
        )
        score_step = jnp.where(keep_step[None, :, None, :], score_step, MASKED_SCORE)
        row_max = jnp.maximum(
            jnp.maximum(jnp.max(score_parent, axis=-1), jnp.max(score_suffix, axis=-1)),
            jnp.max(score_step, axis=-1),
        )[..., None]
        exp_parent = jnp.exp(score_parent - row_max)
        exp_suffix = jnp.exp(score_suffix - row_max)
        exp_step = jnp.exp(score_step - row_max)
        row_total = (
            jnp.sum(exp_parent, axis=-1) + jnp.sum(exp_suffix, axis=-1) + jnp.sum(exp_step, axis=-1)
        )
        blended = jnp.einsum(
            "rtqp,ph->rtqh",
            exp_parent.astype(jnp.bfloat16),
            parent_values[:, kv_head],
            preferred_element_type=jnp.float32,
        )
        blended = blended + jnp.einsum(
            "rtqu,ruh->rtqh",
            exp_suffix.astype(jnp.bfloat16),
            suffix_values[:, :, kv_head],
            preferred_element_type=jnp.float32,
        )
        blended = blended + jnp.einsum(
            "rtqn,rnh->rtqh",
            exp_step.astype(jnp.bfloat16),
            step_values[:, :, kv_head],
            preferred_element_type=jnp.float32,
        )
        results.append((blended / row_total[..., None]).astype(jnp.bfloat16))
    return jnp.stack(results, axis=2).reshape(slot_count, -1)


def pack_rows(pick_rows, row_values):
    return jnp.dot(
        pick_rows.astype(jnp.bfloat16), row_values, preferred_element_type=jnp.float32
    ).astype(jnp.bfloat16)


def local(
    kv_store, queries, step_kv, suffix_pages, suffix_len, owner, parent_id, parent_pages, parent_len
):
    role_index = lax.axis_index("role")
    seq_count = lax.axis_size("seq")
    page_store = kv_store[0]
    query_rows = queries[0]
    kv_width = page_store.shape[1]
    request_count = query_rows.shape[0]
    page_table = page_store.reshape(-1, PAGE * kv_width)
    suffix_flat = jnp.take(page_table, suffix_pages.reshape(-1), axis=0).reshape(request_count, -1)
    prefilled = prefill_rows(
        query_rows, suffix_flat.reshape(request_count, -1, kv_width), suffix_len
    )
    owner_col = owner[:, 0]
    ordinal = jnp.arange(request_count)
    earlier = (owner_col[:, None] == owner_col[None, :]) & (ordinal[None, :] < ordinal[:, None])
    slot_rank = jnp.sum(earlier, axis=1)
    capacity = max(2, 2 * request_count // seq_count)
    slot_total = seq_count * capacity
    placement = owner_col * capacity + slot_rank
    pick_rows = jnp.arange(slot_total)[:, None] == placement[None, :]
    meta_rows = jnp.stack([parent_id, suffix_len], axis=1)
    meta_slots = jnp.sum(
        jnp.where(pick_rows[:, :, None], meta_rows[None, :, :], 0), axis=1
    ).reshape(seq_count, capacity, 2)
    query_slots = pack_rows(pick_rows, query_rows.reshape(request_count, -1)).reshape(
        seq_count, capacity, -1
    )
    step_slots = pack_rows(pick_rows, step_kv.reshape(request_count, -1)).reshape(
        seq_count, capacity, -1
    )
    parent_kv = jnp.take(page_table, parent_pages.reshape(-1), axis=0).reshape(-1, kv_width)
    parent_span = parent_kv.shape[0] // parent_pages.shape[0]
    token_index = jnp.arange(parent_kv.shape[0])
    parent_of = token_index // parent_span
    parent_pos = token_index % parent_span
    parent_cut = jnp.sum(
        jnp.where(
            parent_of[:, None] == jnp.arange(parent_len.shape[0])[None, :], parent_len[None, :], 0
        ),
        axis=1,
    )
    page_slots = pack_rows(pick_rows, suffix_flat).reshape(seq_count, capacity, -1)
    page_width = page_slots.shape[2]
    query_width = query_slots.shape[2]
    step_width = step_slots.shape[2]
    combined = jnp.concatenate([query_slots, step_slots], axis=2)
    padded_rows = jnp.pad(combined, ((0, 0), (0, 0), (0, page_width - query_width - step_width)))
    payload = jnp.where(role_index == 0, page_slots, padded_rows)
    carried = lax.all_to_all(payload, "seq", split_axis=0, concat_axis=0, tiled=True)
    shifted = passed_along(carried, "role", 1)
    query_part = carried[:, :, :query_width]
    step_part = carried[:, :, query_width : query_width + step_width]
    serve_exchanged = (
        shifted,
        query_part,
        step_part,
        lax.all_to_all(meta_slots, "seq", split_axis=0, concat_axis=0, tiled=True),
    )
    source_count = serve_exchanged[0].shape[0]
    item_count = serve_exchanged[0].shape[1]
    operands = tuple(
        (
            member.reshape((source_count * item_count,) + member.shape[2:])
            for member in serve_exchanged
        )
    )
    finished = lax.cond(
        role_index == 1,
        lambda inputs: decode_rows(
            inputs[0], inputs[1], inputs[2], inputs[3], parent_kv, parent_of, parent_pos, parent_cut
        ),
        lambda inputs: jnp.zeros((inputs[1].shape[0], inputs[1].shape[1]), jnp.bfloat16),
        operands,
    )
    finished = finished.reshape(source_count, item_count, -1)
    returned = lax.all_to_all(
        as_sent(finished), "seq", split_axis=0, concat_axis=0, tiled=True
    ).astype(finished.dtype)
    decoded = jnp.take(returned.reshape(slot_total, -1), placement, axis=0).reshape(
        request_count, 2, -1
    )
    served = jnp.where(role_index == 0, prefilled, decoded)
    return served[None]


def solution(mesh):
    in_specs = (
        P("role", ("groups", "seq"), None),
        P("role", ("groups", "seq"), None, None),
        P(("groups", "seq"), None, None),
        P(("groups", "seq"), None),
        P(("groups", "seq")),
        P(("groups", "seq"), None),
        P(("groups", "seq")),
        P(("groups", "seq"), None),
        P(("groups", "seq")),
    )
    out_specs = P("role", ("groups", "seq"), None, None)
    return jax.shard_map(local, mesh=mesh, in_specs=in_specs, out_specs=out_specs, check_vma=False)
```

profile of v0, /device:TPU:1, one launch (start us, length us, event | category | flops | bytes accessed | tf_op | source)
XLA Modules:
  0.0 139.6 jit_solution(12882593423701290201)
XLA Ops:
  7.4 1.2 gather_fusion.1
  9.2 2.1 %convolution_convert_fusion = bf16[32,32768]{1,0:T(8,128)(2,1)} fusion(bf16[16,32768]{1,0:T(8,128)(2,1)S(1)} %reshape.359, s32[16]{0:T(128)S(1)} %multiply_add_fusion), kind=kOutput, calls=%fused_computation.157 | convolution fusion | flops 34603520 | bytes 3145792 | tf_op jit(solution)/shard_map/dot_general | solution.py:142
  11.3 4.2 %reshape.360 = bf16[8,4,32768]{2,1,0:T(4,128)(2,1)} reshape(bf16[32,32768]{1,0:T(8,128)(2,1)} %convolution_convert_fusion) | data formatting | bytes 4194304 | tf_op jit(solution)/shard_map/reshape | solution.py:190
  15.5 1.1 fusion.90
  16.6 53.5 %all_to_all.15 = bf16[8,4,32768]{2,1,0:T(4,128)(2,1)} all-to-all(bf16[8,4,32768]{2,1,0:T(4,128)(2,1)S(1)} %fusion.90), channel_id=1, replica_groups=mesh['groups'=2,'role'=2,'seq'=8] {'seq'}, dimensions={0} | all-to-all | bytes 4194304 | tf_op jit(solution)/shard_map/all_to_all | solution.py:197
  70.1 1.4 %collective-permute-start = (bf16[8,4,32768]{2,1,0:T(4,128)(2,1)}, bf16[8,4,32768]{2,1,0:T(4,128)(2,1)}, u32[]{:S(2)}, u32[]{:S(2)}) collective-permute-start(bf16[8,4,32768]{2,1,0:T(4,128)(2,1)} %all_to_all.15), channel_id=1, source_target_pairs={{0,8},{1,9},{2,10},{3,11},{4,12},{5,13},{6,14},{7,15},{16,24},{17,... | collective-permute-start | bytes 6291464 | tf_op jit(solution)/shard_map/ppermute | solution.py:26
  72.4 4.2 %all-to-all-start = ((s32[8,4,2]{1,2,0:T(2,128)}), s32[8,4,2]{1,2,0:T(2,128)S(1)}, u32[]{:S(2)}, u32[]{:S(2)}) async-start(s32[8,4,2]{1,2,0:T(2,128)} %copy.175), calls=%async_computation | async-start | bytes 16384 | tf_op jit(solution)/shard_map/all_to_all | solution.py:205
  79.2 1.2 gather_fusion.2
  83.0 39.2 %conditional.1 = (bf16[32,8192]{1,0:T(8,128)(2,1)S(1)}) conditional(s32[]{:T(128)} %convert_element_type.125, () %tuple.45, (s32[512]{0:T(512)S(1)}, s32[8,4,2]{1,2,0:T(2,128)S(1)}, s32[512]{0:T(512)S(1)}, s32[512,1]{0,1:T(1,128)S(1)}, s32[512,2]{0,1:T(2,128)S(1)}, /*index=5*/s32[2]{0:T(128)S(1)}, bf16[8,4,32768]{2,1,0:T(4,128)(2,1)}, ...), branch_computations={%region_4.6_spmd, %region_5.32_spmd} | conditional | flops 582753408 | bytes 65777132 | solution.py:215
  83.0 3.3 %reshape_reshape.18 = bf16[32,32,1024]{2,1,0:T(8,128)(2,1)S(1)} reshape(bf16[8,4,32768]{2,1,0:T(4,128)(2,1)} %get-tuple-element.258) | data formatting | bytes 4194304 | tf_op jit(solution)/shard_map/cond/branch_1_fun/reshape;reshape | solution.py:67
  86.3 1.6 %fusion.107 = (bf16[32,32,512]{2,1,0:T(8,128)(2,1)}, bf16[32,32,512]{2,1,0:T(8,128)(2,1)}) fusion(bf16[32,32,1024]{2,1,0:T(8,128)(2,1)S(1)} %reshape_reshape.18), kind=kLoop, calls=%fused_computation.203 | loop fusion | bytes 4194304 | tf_op jit(solution)/shard_map/cond/branch_1_fun/slice | solution.py:34
  87.9 1.4 %reshape.338 = bf16[32,32,4,128]{3,2,1,0:T(4,128)(2,1)S(1)} reshape(bf16[32,32,512]{2,1,0:T(8,128)(2,1)} %get-tuple-element.292) | data formatting | bytes 2097152 | tf_op jit(solution)/shard_map/cond/branch_1_fun/reshape | solution.py:34
  89.5 1.2 broadcast_select_fusion
  90.7 1.6 %reshape.333 = bf16[512,1024]{1,0:T(8,128)(2,1)S(1)} reshape(bf16[32,16384]{1,0:T(8,128)(2,1)} %broadcast_select_fusion) | data formatting | bytes 2097152 | tf_op jit(solution)/shard_map/reshape | solution.py:179
  94.7 1.2 slice.197
  97.6 1.3 fusion.123
  98.9 1.3 fusion.117
  100.2 1.9 %fusion.120 = (f32[32,2,8]{2,1,0:T(2,128)}, f32[32,2,8,2]{2,3,1,0:T(2,128)S(1)}) fusion(bf16[32,2,1,128]{3,2,1,0:T(2,128)(2,1)S(1)} %get-tuple-element.312, bf16[32,2,4,8,128]{4,3,2,1,0:T(8,128)(2,1)S(1)} %reshape_reshape.17, pred[2,2]{1,0:T(4,128)(4,1)} %copy-done.21), kind=kOutput, calls=%fused_computation.216 | convolution fusion | flops 264704 | bytes 169988 | tf_op jit(solution)/shard_map/cond/branch_1_fun/rtqh,rnh->rtqn/dot_general | solution.py:100
  102.1 1.9 %fusion.114 = (f32[32,2,8]{2,1,0:T(2,128)}, f32[32,2,8,2]{2,3,1,0:T(2,128)S(1)}) fusion(bf16[32,2,1,128]{3,2,1,0:T(2,128)(2,1)S(1)} %get-tuple-element.313, bf16[32,2,4,8,128]{4,3,2,1,0:T(8,128)(2,1)S(1)} %reshape_reshape.17, pred[2,2]{1,0:T(4,128)(4,1)} %copy-done.21), kind=kOutput, calls=%fused_computation.210 | convolution fusion | flops 264704 | bytes 169988 | tf_op jit(solution)/shard_map/cond/branch_1_fun/rtqh,rnh->rtqn/dot_general | solution.py:100
  105.1 1.3 reshape.335
  106.4 2.3 %fusion.109 = (bf16[32,32,1,128]{3,2,1,0:T(2,128)(2,1)S(1)}, bf16[32,32,1,128]{3,2,1,0:T(2,128)(2,1)S(1)}, bf16[32,32,1,128]{3,2,1,0:T(2,128)(2,1)S(1)}, bf16[32,32,1,128]{3,2,1,0:T(2,128)(2,1)S(1)}) fusion(bf16[32,32,4,128]{3,2,1,0:T(4,128)(2,1)S(1)} %reshape.335), kind=kLoop, calls=%fused_computation.205 | loop fusion | bytes 2097152 | tf_op jit(solution)/shard_map/cond/branch_1_fun/slice | solution.py:93
  110.2 2.5 %fusion.108 = (bf16[32,32,1,128]{3,2,1,0:T(2,128)(2,1)S(1)}, bf16[32,32,1,128]{3,2,1,0:T(2,128)(2,1)S(1)}, bf16[32,32,1,128]{3,2,1,0:T(2,128)(2,1)S(1)}, bf16[32,32,1,128]{3,2,1,0:T(2,128)(2,1)S(1)}) fusion(bf16[32,32,4,128]{3,2,1,0:T(4,128)(2,1)S(1)} %reshape.338), kind=kLoop, calls=%fused_computation.204 | loop fusion | bytes 2097152 | tf_op jit(solution)/shard_map/cond/branch_1_fun/slice | solution.py:128
  123.3 4.9 %all-to-all-start.2 = ((bf16[8,4,8192]{2,1,0:T(4,128)(2,1)}), bf16[8,4,8192]{2,1,0:T(4,128)(2,1)S(1)}, u32[]{:S(2)}, u32[]{:S(2)}) async-start(bf16[8,4,8192]{2,1,0:T(4,128)(2,1)} %reshape.365), calls=%async_computation.2 | async-start | bytes 1048576 | tf_op jit(solution)/shard_map/all_to_all | solution.py:224
  129.9 7.3 %all-to-all-done.2 = bf16[8,4,8192]{2,1,0:T(4,128)(2,1)S(1)} async-done(((bf16[8,4,8192]{2,1,0:T(4,128)(2,1)}), bf16[8,4,8192]{2,1,0:T(4,128)(2,1)S(1)}, u32[]{:S(2)}, u32[]{:S(2)}) %all-to-all-start.2) | async-done | bytes 524320 | tf_op jit(solution)/shard_map/all_to_all | solution.py:224
  (161 shorter events, 34.6 us)
Async XLA Ops:
  0.0 6.8 %copy-start.4 = (bf16[1,512,1024]{2,1,0:T(8,128)(2,1)S(1)}, bf16[1,512,1024]{2,1,0:T(8,128)(2,1)}, u32[]{:S(2)}) copy-start(bf16[1,512,1024]{2,1,0:T(8,128)(2,1)} %param.13) | copy-start | bytes 3145732
  11.3 4.2 %copy-start.1 = (bf16[8,4,8192]{2,1,0:T(4,128)(2,1)S(1)}, bf16[8,4,8192]{2,1,0:T(4,128)(2,1)}, u32[]{:S(2)}) copy-start(bf16[8,4,8192]{2,1,0:T(4,128)(2,1)} %reshape.361) | copy-start | bytes 1572868
  16.6 54.9 %copy-start.15 = (s32[16]{0:T(128)S(1)}, s32[16]{0:T(128)}, u32[]{:S(2)}) copy-start(s32[16]{0:T(128)} %param.19) | copy-start | bytes 196
  16.6 54.9 %copy-start.16 = (s32[16]{0:T(128)S(1)}, s32[16]{0:T(128)}, u32[]{:S(2)}) copy-start(s32[16]{0:T(128)} %param.17) | copy-start | bytes 196
  70.1 7.0 %copy-start.20 = (s32[2,16]{1,0:T(2,128)S(1)}, s32[2,16]{1,0:T(2,128)}, u32[]{:S(2)}) copy-start(s32[2,16]{1,0:T(2,128)} %param.20) | copy-start | bytes 388
  70.1 11.8 %collective-permute-start = (bf16[8,4,32768]{2,1,0:T(4,128)(2,1)}, bf16[8,4,32768]{2,1,0:T(4,128)(2,1)}, u32[]{:S(2)}, u32[]{:S(2)}) collective-permute-start(bf16[8,4,32768]{2,1,0:T(4,128)(2,1)} %all_to_all.15), channel_id=1, source_target_pairs={{0,8},{1,9},{2,10},{3,11},{4,12},{5,13},{6,14},{7,15},{16,24},{17,... | collective-permute-start | bytes 6291464 | tf_op jit(solution)/shard_map/ppermute | solution.py:26
  72.4 9.5 %all-to-all-start = ((s32[8,4,2]{1,2,0:T(2,128)}), s32[8,4,2]{1,2,0:T(2,128)S(1)}, u32[]{:S(2)}, u32[]{:S(2)}) async-start(s32[8,4,2]{1,2,0:T(2,128)} %copy.175), calls=%async_computation | async-start | bytes 16384 | tf_op jit(solution)/shard_map/all_to_all | solution.py:205
  76.6 1.7 %copy-start.5 = (bf16[1,16,2,4096]{3,2,1,0:T(2,128)(2,1)S(1)}, bf16[1,16,2,4096]{3,2,1,0:T(2,128)(2,1)}, u32[]{:S(2)}) copy-start(bf16[1,16,2,4096]{3,2,1,0:T(2,128)(2,1)} %param.14) | copy-start | bytes 786436
  80.4 2.6 %copy-start.14 = (s32[2]{0:T(128)S(1)}, s32[2]{0:T(128)}, u32[]{:S(2)}) copy-start(s32[2]{0:T(128)} %param.21) | copy-start | bytes 28
  87.9 1.5 %copy-start = (bf16[32,16384]{1,0:T(8,128)(2,1)S(1)}, bf16[32,16384]{1,0:T(8,128)(2,1)}, u32[]{:S(2)}) copy-start(bf16[32,16384]{1,0:T(8,128)(2,1)} %get-tuple-element.281) | copy-start | bytes 3145732 | tf_op jit(solution)/shard_map/cond
  89.4 9.5 %copy-start.21 = (pred[2,2]{1,0:T(4,128)(4,1)}, pred[2,2]{1,0:T(4,128)(4,1)S(1)}, u32[]{:S(2)}) copy-start(pred[2,2]{1,0:T(4,128)(4,1)S(1)} %iota_compare_fusion.1) | copy-start | bytes 16 | tf_op jit(solution)/shard_map/cond
  110.2 2.6 %copy-start.3 = (bf16[512,512]{0,1:T(8,128)(2,1)S(1)}, bf16[512,512]{0,1:T(8,128)(2,1)}, u32[]{:S(2)}) copy-start(bf16[512,512]{0,1:T(8,128)(2,1)} %copy.138) | copy-start | bytes 1572868 | tf_op jit(solution)/shard_map/cond
  110.2 3.0 %copy-start.13 = (f32[32,2,8]{2,1,0:T(2,128)S(1)}, f32[32,2,8]{2,1,0:T(2,128)}, u32[]{:S(2)}) copy-start(f32[32,2,8]{2,1,0:T(2,128)} %get-tuple-element.322) | copy-start | bytes 6148 | tf_op jit(solution)/shard_map/cond
  112.8 1.3 copy-start.7
  113.2 1.2 copy-start.9
  114.7 0.8 copy-start.12
  116.8 0.8 copy-start.10
  117.1 0.9 copy-start.11
  122.2 5.9 %copy-start.6 = (bf16[16,32,4,128]{3,2,1,0:T(4,128)(2,1)S(1)}, bf16[16,32,4,128]{3,2,1,0:T(4,128)(2,1)}, u32[]{:S(2)}) copy-start(bf16[16,32,4,128]{3,2,1,0:T(4,128)(2,1)} %reshape.356) | copy-start | bytes 1572868
  122.3 5.9 %copy-start.8 = (bf16[16,2,4,8,128]{4,3,2,1,0:T(8,128)(2,1)S(1)}, bf16[16,2,4,8,128]{4,3,2,1,0:T(8,128)(2,1)}, u32[]{:S(2)}) copy-start(bf16[16,2,4,8,128]{4,3,2,1,0:T(8,128)(2,1)} %reshape_squeeze.10) | copy-start | bytes 786436
  122.3 6.4 %copy-start.2 = (bf16[16,32,512]{2,1,0:T(8,128)(2,1)S(1)}, bf16[16,32,512]{2,1,0:T(8,128)(2,1)}, u32[]{:S(2)}) copy-start(bf16[16,32,512]{2,1,0:T(8,128)(2,1)} %get-tuple-element.341) | copy-start | bytes 1572868
  123.3 14.0 %all-to-all-start.2 = ((bf16[8,4,8192]{2,1,0:T(4,128)(2,1)}), bf16[8,4,8192]{2,1,0:T(4,128)(2,1)S(1)}, u32[]{:S(2)}, u32[]{:S(2)}) async-start(bf16[8,4,8192]{2,1,0:T(4,128)(2,1)} %reshape.365), calls=%async_computation.2 | async-start | bytes 1048576 | tf_op jit(solution)/shard_map/all_to_all | solution.py:224
  129.2 0.7 copy-start.17
  129.3 0.7 copy-start.19
  (1 other events, 0.6 us)
where the time goes:
time: 140 us
  blocking collectives  53.5 us (38%)
  local copies, waits for them, and re-layouts  41.4 us (30%)
  matrix products  16.8 us (12%)
  starting transfers between devices  10.4 us (7%)
  other arithmetic  8.64 us (6%)
  waiting for transfers between devices  7.87 us (6%)
    all_to_all x1, blocking collectives, local(): lax.all_to_all(payload, 'seq', split_axis=0, concat_axis=0, tiled=True)  53.5 us
    all_to_all x1, waiting for transfers between devices, local(): lax.all_to_all(as_sent(finished), 'seq', split_axis=0, concat_axis=0, til...  7.3 us
    dot_general x4, matrix products, decode_rows(): jnp.einsum('rtqh,rnh->rtqn', query_one, step_keys[:, :, kv_head], preferr...  6.47 us
    all_to_all x1, starting transfers between devices, local(): lax.all_to_all(as_sent(finished), 'seq', split_axis=0, concat_axis=0, til...  4.86 us
    all_to_all x1, starting transfers between devices, local(): lax.all_to_all(meta_slots, 'seq', split_axis=0, concat_axis=0, tiled=True)  4.16 us
    reshape x1, local copies, waits for them, and re-layouts, local(): pack_rows(pick_rows, suffix_flat).reshape(seq_count, capacity, -1)  4.16 us
    unnamed x29, local copies, waits for them, and re-layouts  3.55 us
    another operation x1, local copies, waits for them, and re-layouts, decode_rows(): page_slots.reshape(slot_count, -1, kv_width)  3.27 us
  transfers between devices with their start and end apart: 3, of which 2 were waited for; matrix products, arithmetic and copies ran while one was open for 5% of the time, Pallas kernels for 0%

commit v1 on v0

v1 whole, which is shorter than its diff:
```python
import functools

import jax
import jax.numpy as jnp
from jax import lax
from jax.experimental import pallas as pl
from jax.experimental.pallas import tpu as pltpu
from jax.sharding import PartitionSpec as P

HEAD_DIM = 128
KV_HEADS = 4
GROUP = 8
PAGE = 16
HEAD_ROWS = 2 * GROUP
KEY_WIDTH = KV_HEADS * HEAD_DIM
SCALE = HEAD_DIM ** (-0.5)
MASKED = -1e30
STAT_ROWS = 8
VMEM_BYTES = 48 * 1024 * 1024

NT = (((1,), (1,)), ((), ()))


def iota(shape, dim):
    return lax.broadcasted_iota(jnp.int32, shape, dim)


def slot_ranks(owner_ref, count):
    names = [owner_ref[r] for r in range(count)]
    ranks = []
    for r in range(count):
        rank = jnp.int32(0)
        for earlier in range(r):
            rank = rank + jnp.where(names[earlier] == names[r], 1, 0)
        ranks.append(rank)
    return names, ranks


def pack_kernel(cap, owner_ref, parent_ref, query_ref, out_ref, meta_ref):
    count = query_ref.shape[0]
    head_span = cap * HEAD_ROWS
    out_ref[...] = jnp.zeros_like(out_ref)
    meta_ref[...] = jnp.zeros_like(meta_ref)
    names, ranks = slot_ranks(owner_ref, count)
    row, lane = iota((16, HEAD_DIM), 0), iota((16, HEAD_DIM), 1)
    for r in range(count):
        d, rank = names[r], ranks[r]
        for g in range(KV_HEADS):
            start = pl.multiple_of(g * head_span + rank * HEAD_ROWS, HEAD_ROWS)
            out_ref[d, pl.ds(start, HEAD_ROWS), :] = query_ref[r, pl.ds(g * HEAD_ROWS, HEAD_ROWS), :]
        hit = (row == rank) & (lane == parent_ref[r])
        meta_ref[d] = jnp.where(hit, 1.0, meta_ref[d])
    out_ref[:, pl.ds(KV_HEADS * head_span, 16), :] = meta_ref[...].astype(jnp.bfloat16)


def parent_kernel(
    cap, chunk, pages_ref, len_ref, recv_ref, store_ref, out_ref, bias_ref
):
    parents, page_count = pages_ref.shape
    sources = recv_ref.shape[0]
    head_span = cap * HEAD_ROWS
    row, lane = iota((PAGE, HEAD_DIM), 0), iota((PAGE, HEAD_DIM), 1)
    for p in range(parents):
        for i in range(page_count):
            keep = (lane == p) & (row + i * PAGE < len_ref[p])
            start = pl.multiple_of(pages_ref[p, i] * PAGE, PAGE)
            bias_ref[pl.ds(start, PAGE), :] = jnp.where(keep, 0.0, MASKED).astype(jnp.bfloat16)

    def body(c, carry):
        base = c * chunk
        rows = chunk * head_span
        meta = recv_ref[pl.ds(base, chunk), pl.ds(KV_HEADS * head_span, 16), :].astype(jnp.float32)
        picks = [
            jnp.broadcast_to(meta[:, s : s + 1, :], (chunk, HEAD_ROWS, HEAD_DIM)) for s in range(cap)
        ]
        pick = jnp.concatenate(picks, axis=1).reshape(rows, HEAD_DIM).astype(jnp.bfloat16)
        stats = jnp.zeros((rows, HEAD_DIM), jnp.float32)
        lanes = iota((rows, HEAD_DIM), 1)
        for g in range(KV_HEADS):
            query = recv_ref[pl.ds(base, chunk), pl.ds(g * head_span, head_span), :].reshape(rows, HEAD_DIM)
            keys = store_ref[:, pl.ds(g * HEAD_DIM, HEAD_DIM)]
            values = store_ref[:, pl.ds(KEY_WIDTH + g * HEAD_DIM, HEAD_DIM)]
            scores = lax.dot_general(
                jnp.concatenate([query, pick], axis=1),
                jnp.concatenate([keys, bias_ref[...]], axis=1),
                NT,
                preferred_element_type=jnp.float32,
            ) * SCALE
            top = jnp.max(scores, axis=1, keepdims=True)
            terms = jnp.exp(scores - top)
            total = jnp.sum(terms, axis=1, keepdims=True)
            blended = jnp.dot(terms.astype(jnp.bfloat16), values, preferred_element_type=jnp.float32)
            out_ref[pl.ds(base, chunk), pl.ds(g * head_span, head_span), :] = blended.reshape(
                chunk, head_span, HEAD_DIM
            )
            stats = jnp.where(lanes == g, top, stats)
            stats = jnp.where(lanes == KV_HEADS + g, total, stats)
        flat = stats.T[:STAT_ROWS, :]
        for j in range(chunk):
            piece = flat[:, j * head_span : (j + 1) * head_span]
            if head_span < HEAD_DIM:
                piece = jnp.concatenate(
                    [piece, jnp.zeros((STAT_ROWS, HEAD_DIM - head_span), jnp.float32)], axis=1
                )
            out_ref[base + j, pl.ds(KV_HEADS * head_span, STAT_ROWS), :] = piece
        return carry

    lax.fori_loop(0, sources // chunk, body, 0, unroll=min(2, sources // chunk))


def fill_suffix_bias(pages_ref, len_ref, bias_ref, last_of):
    page_count, count = pages_ref.shape
    row, lane = iota((PAGE, HEAD_DIM), 0), iota((PAGE, HEAD_DIM), 1)
    for r in range(count):
        for i in range(page_count):
            keep = (lane // 2 == r) & (row + i * PAGE <= last_of(len_ref[r], lane % 2))
            start = pl.multiple_of(pages_ref[i, r] * PAGE, PAGE)
            bias_ref[pl.ds(start, PAGE), :] = jnp.where(keep, 0.0, MASKED).astype(jnp.bfloat16)


def own_pick(count):
    rows = count * HEAD_ROWS
    row, lane = iota((rows, HEAD_DIM), 0), iota((rows, HEAD_DIM), 1)
    return jnp.where(lane == (row // HEAD_ROWS) * 2 + row % 2, 1.0, 0.0).astype(jnp.bfloat16)


def prefill_kernel(pages_ref, len_ref, query_ref, store_ref, out_ref, bias_ref):
    count = query_ref.shape[0]
    rows = count * HEAD_ROWS
    fill_suffix_bias(pages_ref, len_ref, bias_ref, lambda length, t: length - 2 + t)
    pick = own_pick(count)
    for g in range(KV_HEADS):
        query = query_ref[:, pl.ds(g * HEAD_ROWS, HEAD_ROWS), :].reshape(rows, HEAD_DIM)
        keys = store_ref[:, pl.ds(g * HEAD_DIM, HEAD_DIM)]
        values = store_ref[:, pl.ds(KEY_WIDTH + g * HEAD_DIM, HEAD_DIM)]
        scores = lax.dot_general(
            jnp.concatenate([query, pick], axis=1),
            jnp.concatenate([keys, bias_ref[...]], axis=1),
            NT,
            preferred_element_type=jnp.float32,
        ) * SCALE
        terms = jnp.exp(scores - jnp.max(scores, axis=1, keepdims=True))
        total = jnp.sum(terms, axis=1, keepdims=True)
        blended = jnp.dot(terms.astype(jnp.bfloat16), values, preferred_element_type=jnp.float32)
        out_ref[:, pl.ds(g * HEAD_ROWS, HEAD_ROWS), :] = (
            (blended / total).astype(jnp.bfloat16).reshape(count, HEAD_ROWS, HEAD_DIM)
        )


def merge_kernel(
    cap, owner_ref, pages_ref, len_ref, back_ref, query_ref, store_ref, step_ref, out_ref,
    bias_ref, part_ref, stat_ref,
):
    count = query_ref.shape[0]
    rows = count * HEAD_ROWS
    head_span = cap * HEAD_ROWS
    fill_suffix_bias(pages_ref, len_ref, bias_ref, lambda length, t: length - 1)
    steps = 2 * count
    step_pad = -steps % HEAD_DIM
    key_row, lane = iota((steps + step_pad, HEAD_DIM), 0), iota((steps + step_pad, HEAD_DIM), 1)
    seen = (key_row // 2 == lane // 2) & (key_row % 2 <= lane % 2) & (key_row < steps)
    step_bias = jnp.where(seen, 0.0, MASKED).astype(jnp.bfloat16)
    pad = jnp.zeros((step_pad, HEAD_DIM), jnp.bfloat16)

    names, ranks = slot_ranks(owner_ref, count)
    for r in range(count):
        d, rank = names[r], ranks[r]
        for g in range(KV_HEADS):
            start = pl.multiple_of(g * head_span + rank * HEAD_ROWS, HEAD_ROWS)
            part_ref[g, pl.ds(r * HEAD_ROWS, HEAD_ROWS), :] = back_ref[d, pl.ds(start, HEAD_ROWS), :]
        tile = back_ref[d, pl.ds(KV_HEADS * head_span, STAT_ROWS), :]
        shift = lax.rem(HEAD_DIM - rank * HEAD_ROWS, HEAD_DIM)
        stat_ref[pl.ds(r * STAT_ROWS, STAT_ROWS), :] = pltpu.roll(tile, shift, 1)
    columns = stat_ref[...].T[:HEAD_ROWS, :]

    def column(k):
        return jnp.concatenate(
            [columns[:, r * STAT_ROWS + k : r * STAT_ROWS + k + 1] for r in range(count)], axis=0
        )

    def step_rows(c):
        return jnp.concatenate([step_ref[r, 2 * c : 2 * c + 2, :] for r in range(count)] + [pad], axis=0)

    pick = own_pick(count)
    for g in range(KV_HEADS):
        query = query_ref[:, pl.ds(g * HEAD_ROWS, HEAD_ROWS), :].reshape(rows, HEAD_DIM)
        query = jnp.concatenate([query, pick], axis=1)
        keys = jnp.concatenate([store_ref[:, pl.ds(g * HEAD_DIM, HEAD_DIM)], bias_ref[...]], axis=1)
        step_keys = jnp.concatenate([step_rows(g), step_bias], axis=1)
        values = store_ref[:, pl.ds(KEY_WIDTH + g * HEAD_DIM, HEAD_DIM)]
        step_values = step_rows(KV_HEADS + g)
        scores = lax.dot_general(query, keys, NT, preferred_element_type=jnp.float32) * SCALE
        step_scores = lax.dot_general(query, step_keys, NT, preferred_element_type=jnp.float32) * SCALE
        part_top, part_total = column(g), column(KV_HEADS + g)
        top = jnp.maximum(
            jnp.maximum(jnp.max(scores, axis=1, keepdims=True), jnp.max(step_scores, axis=1, keepdims=True)),
            part_top,
        )
        terms = jnp.exp(scores - top)
        step_terms = jnp.exp(step_scores - top)
        part_weight = jnp.exp(part_top - top)
        total = (
            jnp.sum(terms, axis=1, keepdims=True)
            + jnp.sum(step_terms, axis=1, keepdims=True)
            + part_weight * part_total
        )
        blended = jnp.dot(terms.astype(jnp.bfloat16), values, preferred_element_type=jnp.float32)
        blended = blended + jnp.dot(
            step_terms.astype(jnp.bfloat16), step_values, preferred_element_type=jnp.float32
        )
        blended = blended + part_weight * part_ref[g]
        out_ref[:, pl.ds(g * HEAD_ROWS, HEAD_ROWS), :] = (
            (blended / total).astype(jnp.bfloat16).reshape(count, HEAD_ROWS, HEAD_DIM)
        )


def call(kernel, out_shape, scalars, arrays, scratch):
    smem = pl.BlockSpec(memory_space=pltpu.SMEM)
    vmem = pl.BlockSpec(memory_space=pltpu.VMEM)
    return pl.pallas_call(
        kernel,
        out_shape=out_shape,
        in_specs=[smem] * len(scalars) + [vmem] * len(arrays),
        out_specs=vmem,
        scratch_shapes=scratch,
        compiler_params=pltpu.CompilerParams(vmem_limit_bytes=VMEM_BYTES),
    )(*scalars, *arrays)


def head_rows(tokens):
    count, pair, width = tokens.shape
    blocks = tokens.reshape(count, pair, width // HEAD_DIM, HEAD_DIM)
    return blocks.transpose(0, 2, 1, 3).reshape(count, -1, HEAD_DIM)


def local(
    kv_store, queries, step_kv, suffix_pages, suffix_len, owner, parent_id, parent_pages, parent_len
):
    decoding = lax.axis_index("role") == 1
    seq_count = lax.axis_size("seq")
    store = kv_store[0]
    count, pair, width = queries.shape[1:]
    cap = max(2, 2 * count // seq_count)
    head_span = cap * HEAD_ROWS
    chunk = max(1, 256 // head_span)
    query_rows = head_rows(queries[0])
    owner_of = owner.reshape(-1)
    suffix_table = suffix_pages.T
    token_rows = store.shape[0]

    suffix_store = lax.ppermute(store, "role", [(0, 1)])

    sent = jax.ShapeDtypeStruct((seq_count, KV_HEADS * head_span + 16, HEAD_DIM), jnp.bfloat16)
    answer = jax.ShapeDtypeStruct((seq_count, KV_HEADS * head_span + STAT_ROWS, HEAD_DIM), jnp.float32)
    result = jax.ShapeDtypeStruct(query_rows.shape, jnp.bfloat16)
    bias = pltpu.VMEM((token_rows, HEAD_DIM), jnp.bfloat16)

    def exchange(block):
        return lax.all_to_all(block, "seq", split_axis=0, concat_axis=0, tiled=True)

    def send_queries(query_rows):
        packed = call(
            functools.partial(pack_kernel, cap),
            sent,
            (owner_of, parent_id),
            (query_rows,),
            [pltpu.VMEM((seq_count, 16, HEAD_DIM), jnp.float32)],
        )
        return exchange(packed)

    received = lax.cond(
        decoding, send_queries, lambda query_rows: jnp.zeros(sent.shape, sent.dtype), query_rows
    )

    def decode(received, suffix_store, query_rows):
        parts = call(
            functools.partial(parent_kernel, cap, chunk),
            answer,
            (parent_pages, parent_len),
            (received, store),
            [bias],
        )
        back = exchange(parts)
        return call(
            functools.partial(merge_kernel, cap),
            result,
            (owner_of, suffix_table, suffix_len),
            (back, query_rows, suffix_store, head_rows(step_kv)),
            [
                bias,
                pltpu.VMEM((KV_HEADS, count * HEAD_ROWS, HEAD_DIM), jnp.float32),
                pltpu.VMEM((count * STAT_ROWS, HEAD_DIM), jnp.float32),
            ],
        )

    def prefill(received, suffix_store, query_rows):
        return call(
            prefill_kernel, result, (suffix_table, suffix_len), (query_rows, store), [bias]
        )

    served = lax.cond(decoding, decode, prefill, received, suffix_store, query_rows)
    served = served.reshape(count, width // HEAD_DIM, pair, HEAD_DIM).transpose(0, 2, 1, 3)
    return served.reshape(1, count, pair, width)


def solution(mesh):
    in_specs = (
        P("role", ("groups", "seq"), None),
        P("role", ("groups", "seq"), None, None),
        P(("groups", "seq"), None, None),
        P(("groups", "seq"), None),
        P(("groups", "seq")),
        P(("groups", "seq"), None),
        P(("groups", "seq")),
        P(("groups", "seq"), None),
        P(("groups", "seq")),
    )
    out_specs = P("role", ("groups", "seq"), None, None)
    return jax.shard_map(local, mesh=mesh, in_specs=in_specs, out_specs=out_specs, check_vma=False)
```

time: 140 us -> 45.3 us (0.32)
  local copies, waits for them, and re-layouts: 41.4 us -> 0.85 us
  blocking collectives: 53.5 us -> 34.9 us
  matrix products: 16.8 us -> 0 us
  starting transfers between devices: 10.4 us -> 1.28 us
  other arithmetic: 8.64 us -> 0 us
  Pallas kernels: 0 us -> 7.97 us
  waiting for transfers between devices: 7.87 us -> 0.01 us
    all_to_all x1 -> x2, blocking collectives: 53.5 us -> 34.9 us  [exchange(): return lax.all_to_all(block, 'seq', split_axis=0, concat_axis=0, tiled=True)]
    dot_general x29 -> x0, matrix products: 16.8 us -> none  [the longest x4 6.47 us: decode_rows(): jnp.einsum('rtqh,rnh->rtqn', query_one, step_keys[:, :, kv_head], preferr...]
    slice x12 -> x0, local copies, waits for them, and re-layouts: 12.6 us -> none  [the longest x4 2.83 us: split_heads(): kv_rows[..., key_width:].reshape(shape_head)]
    reshape x19 -> x2, local copies, waits for them, and re-layouts: 13.3 us -> 0.82 us  [the longest x1 0.77 us: local(): return served.reshape(1, count, pair, width)]
    all_to_all x2 -> x0, starting transfers between devices: 9.02 us -> none  [the longest x1 4.86 us: local(): lax.all_to_all(as_sent(finished), 'seq', split_axis=0, concat_axis=0, til...]
    pallas_call x0 -> x3, Pallas kernels: none -> 7.97 us  [call(): pl.pallas_call(kernel, out_shape=out_shape, in_specs=[smem] * len(scalars...]
    all_to_all x2 -> x0, waiting for transfers between devices: 7.87 us -> none  [the longest x1 7.3 us: local(): lax.all_to_all(as_sent(finished), 'seq', split_axis=0, concat_axis=0, til...]
    another operation x8 -> x0, local copies, waits for them, and re-layouts: 5.98 us -> none  [the longest x1 3.27 us: decode_rows(): page_slots.reshape(slot_count, -1, kv_width)]
  transfers between devices with their start and end apart: 3 -> 1, of which waited for: 2 -> 0; matrix products, arithmetic and copies ran while one was open for 5% -> 0% of each run, Pallas kernels for 0% -> 3%
where the time goes in v1:
time: 45.3 us; the launch traced here: 45.1 us
  blocking collectives  34.9 us (77%)
  Pallas kernels  7.97 us (18%)
  starting transfers between devices  1.28 us (3%)
  local copies, waits for them, and re-layouts  0.85 us (2%)
    all_to_all x2, blocking collectives, exchange(): return lax.all_to_all(block, 'seq', split_axis=0, concat_axis=0, tiled=True)  34.9 us
    pallas_call x3, Pallas kernels, call(): pl.pallas_call(kernel, out_shape=out_shape, in_specs=[smem] * len(scalars...  7.97 us
    ppermute x1, starting transfers between devices, local(): suffix_store = lax.ppermute(store, 'role', [(0, 1)])  1.28 us
  transfers between devices with their start and end apart: 1, of which 0 were waited for; matrix products, arithmetic and copies ran while one was open for 0% of the time, Pallas kernels for 3%

profile of v1, /device:TPU:1, one launch (start us, length us, event | category | flops | bytes accessed | tf_op | source)
XLA Modules:
  0.0 45.1 jit_solution(6447568988557295667)
XLA Ops:
  0.0 1.3 %collective-permute-start = (bf16[512,1024]{1,0:T(8,128)(2,1)}, bf16[512,1024]{1,0:T(8,128)(2,1)S(1)}, u32[]{:S(2)}, u32[]{:S(2)}) collective-permute-start(bf16[512,1024]{1,0:T(8,128)(2,1)} %bitcast.19), channel_id=1, source_target_pairs={{0,8},{1,9},{2,10},{3,11},{4,12},{5,13},{6,14},{7,15},{16,24},{17,... | collective-permute-start | bytes 3145736 | tf_op jit(solution)/shard_map/ppermute | solution.py:251
  1.3 0.0 copy-start
  1.3 0.0 copy-start.2
  1.3 0.0 copy-start.3
  1.3 0.0 copy-start.4
  1.3 0.0 copy-start.6
  1.3 0.0 copy-start.7
  1.4 17.7 %conditional.2 = (bf16[8,272,128]{2,1,0:T(8,128)(2,1)S(1)}) conditional(s32[]{:T(128)} %convert_element_type.4, () %tuple.18, (s32[16]{0:T(128)}, s32[16]{0:T(128)}, bf16[16,64,128]{2,1,0:T(8,128)(2,1)}) %tuple.35), branch_computations={%region_0.0_spmd, %region_1.0_spmd} | conditional | bytes 1114120 | solution.py:271
  1.4 1.3 %branch_1_fun.3 = bf16[8,272,128]{2,1,0:T(8,128)(2,1)S(1)} custom-call(s32[16]{0:T(128)} %get-tuple-element.44.owner_ref, s32[16]{0:T(128)} %get-tuple-element.63.parent_ref, bf16[16,64,128]{2,1,0:T(8,128)(2,1)} %get-tuple-element.47.query_ref), custom_call_target="tpu_custom_call" | custom-call | tf_op jit(solution)/shard_map/cond/branch_1_fun/pallas_call | solution.py:220
  2.7 16.4 %all_to_all.8 = bf16[8,272,128]{2,1,0:T(8,128)(2,1)S(1)} all-to-all(bf16[8,272,128]{2,1,0:T(8,128)(2,1)S(1)} %branch_1_fun.3), channel_id=1, replica_groups=mesh['groups'=2,'role'=2,'seq'=8] {'seq'}, dimensions={0} | all-to-all | bytes 1114112 | tf_op jit(solution)/shard_map/cond/branch_1_fun/all_to_all | solution.py:259
  19.1 0.0 collective-permute-done
  19.1 0.0 copy-done
  19.1 0.0 copy-done.2
  19.1 0.0 copy-done.3
  19.1 0.0 copy-done.4
  19.1 0.0 copy-done.6
  19.1 0.0 copy-done.7
  19.1 25.1 %conditional.3 = (bf16[16,64,128]{2,1,0:T(8,128)(2,1)S(1)}) conditional(s32[]{:T(128)} %convert_element_type.4, (s32[2,16]{1,0:T(2,128)S(1)}, s32[16]{0:T(128)S(1)}, bf16[16,64,128]{2,1,0:T(8,128)(2,1)}, bf16[512,1024]{1,0:T(8,128)(2,1)S(1)}) %tuple.33, (s32[2,16]{1,0:T(2,128)S(1)}, s32[2]{0:T(128)S(1)}, bf16[8,272,128]{2,1,0:T(8,128)(2,1)S(1)}, ...), branch_computations={%region_2.0_spmd, %region_3.0_spmd} | conditional | bytes 3211584 | solution.py:301
  19.2 3.5 %branch_1_fun.4 = f32[8,264,128]{2,1,0:T(8,128)S(1)} custom-call(s32[2,16]{1,0:T(2,128)S(1)} %get-tuple-element.67.pages_ref, s32[2]{0:T(128)S(1)} %get-tuple-element.68.len_ref, bf16[8,272,128]{2,1,0:T(8,128)(2,1)S(1)} %get-tuple-element.57.recv_ref, bf16[512,1024]{1,0:T(8,128)(2,1)S(1)} %get-tuple-element.58.store_ref), custom_call_target="tpu_custom_call" | custom-call | tf_op jit(solution)/shard_map/cond/branch_1_fun/pallas_call | solution.py:220
  22.7 18.4 %all_to_all.9.back_ref = f32[8,264,128]{2,1,0:T(8,128)S(1)} all-to-all(f32[8,264,128]{2,1,0:T(8,128)S(1)} %branch_1_fun.4), channel_id=1, replica_groups=mesh['groups'=2,'role'=2,'seq'=8] {'seq'}, dimensions={0} | all-to-all | bytes 2162688 | tf_op jit(solution)/shard_map/cond/branch_1_fun/all_to_all | solution.py:259
  41.1 0.0 copy-done.1
  41.1 0.0 copy-done.5
  41.1 3.2 %branch_1_fun.5 = bf16[16,64,128]{2,1,0:T(8,128)(2,1)S(1)} custom-call(s32[16]{0:T(128)S(1)} %copy-done.5, s32[2,16]{1,0:T(2,128)S(1)} %get-tuple-element.53.pages_ref, s32[16]{0:T(128)S(1)} %get-tuple-element.54.len_ref, f32[8,264,128]{2,1,0:T(8,128)S(1)} %all_to_all.9.back_ref, bf16[16,64,128]{2,1,0:T(8,128)(2,1)S(1)} %copy-done.1, ...), custom_call_target="tpu_custom_call" | custom-call | tf_op jit(solution)/shard_map/cond/branch_1_fun/pallas_call | solution.py:220
  44.3 0.8 %reshape.21 = bf16[1,16,2,4096]{3,2,1,0:T(2,128)(2,1)} reshape(bf16[16,2,32,128]{3,2,1,0:T(8,128)(2,1)S(1)} %bitcast.26) | data formatting | bytes 524288 | tf_op jit(solution)/shard_map/reshape | solution.py:303
  (3 shorter events, 0.0 us)
Async XLA Ops:
  0.0 19.1 %collective-permute-start = (bf16[512,1024]{1,0:T(8,128)(2,1)}, bf16[512,1024]{1,0:T(8,128)(2,1)S(1)}, u32[]{:S(2)}, u32[]{:S(2)}) collective-permute-start(bf16[512,1024]{1,0:T(8,128)(2,1)} %bitcast.19), channel_id=1, source_target_pairs={{0,8},{1,9},{2,10},{3,11},{4,12},{5,13},{6,14},{7,15},{16,24},{17,... | collective-permute-start | bytes 3145736 | tf_op jit(solution)/shard_map/ppermute | solution.py:251
  1.3 17.8 %copy-start = (bf16[1,512,1024]{2,1,0:T(8,128)(2,1)S(1)}, bf16[1,512,1024]{2,1,0:T(8,128)(2,1)}, u32[]{:S(2)}) copy-start(bf16[1,512,1024]{2,1,0:T(8,128)(2,1)} %param.13) | copy-start | bytes 3145732
  1.3 17.8 %copy-start.2 = (bf16[16,2,1024]{2,1,0:T(2,128)(2,1)S(1)}, bf16[16,2,1024]{2,1,0:T(2,128)(2,1)}, u32[]{:S(2)}) copy-start(bf16[16,2,1024]{2,1,0:T(2,128)(2,1)} %param.15) | copy-start | bytes 196612
  1.3 17.8 %copy-start.3 = (s32[16,2]{0,1:T(2,128)S(1)}, s32[16,2]{0,1:T(2,128)}, u32[]{:S(2)}) copy-start(s32[16,2]{0,1:T(2,128)} %param.16) | copy-start | bytes 388
  1.3 17.8 %copy-start.4 = (s32[16]{0:T(128)S(1)}, s32[16]{0:T(128)}, u32[]{:S(2)}) copy-start(s32[16]{0:T(128)} %param.17) | copy-start | bytes 196
  1.3 17.8 %copy-start.6 = (s32[2,16]{1,0:T(2,128)S(1)}, s32[2,16]{1,0:T(2,128)}, u32[]{:S(2)}) copy-start(s32[2,16]{1,0:T(2,128)} %param.20) | copy-start | bytes 388
  1.3 17.8 %copy-start.7 = (s32[2]{0:T(128)S(1)}, s32[2]{0:T(128)}, u32[]{:S(2)}) copy-start(s32[2]{0:T(128)} %param.21) | copy-start | bytes 28
  22.7 18.4 %copy-start.1 = (bf16[16,64,128]{2,1,0:T(8,128)(2,1)S(1)}, bf16[16,64,128]{2,1,0:T(8,128)(2,1)}, u32[]{:S(2)}) copy-start(bf16[16,64,128]{2,1,0:T(8,128)(2,1)} %get-tuple-element.59.query_ref) | copy-start | bytes 786436 | tf_op jit(solution)/shard_map/cond
  22.7 18.4 %copy-start.5 = (s32[16]{0:T(128)S(1)}, s32[16]{0:T(128)}, u32[]{:S(2)}) copy-start(s32[16]{0:T(128)} %get-tuple-element.52.owner_ref) | copy-start | bytes 196 | tf_op jit(solution)/shard_map/cond

commit v2 on v1

--- a/solution.py
+++ b/solution.py
@@ -15,7 +15,9 @@
 KEY_WIDTH = KV_HEADS * HEAD_DIM
 SCALE = HEAD_DIM ** (-0.5)
 MASKED = -1e30
-STAT_ROWS = 8
+STAT_ROWS = 4 * KV_HEADS
+LOG_STEPS = 4.0
+SCALE_STEPS = 128.0
 VMEM_BYTES = 48 * 1024 * 1024
 
 NT = (((1,), (1,)), ((), ()))
@@ -42,65 +44,89 @@
     out_ref[...] = jnp.zeros_like(out_ref)
     meta_ref[...] = jnp.zeros_like(meta_ref)
     names, ranks = slot_ranks(owner_ref, count)
-    row, lane = iota((16, HEAD_DIM), 0), iota((16, HEAD_DIM), 1)
+    row = iota((16, HEAD_DIM), 0)
     for r in range(count):
         d, rank = names[r], ranks[r]
         for g in range(KV_HEADS):
             start = pl.multiple_of(g * head_span + rank * HEAD_ROWS, HEAD_ROWS)
             out_ref[d, pl.ds(start, HEAD_ROWS), :] = query_ref[r, pl.ds(g * HEAD_ROWS, HEAD_ROWS), :]
-        hit = (row == rank) & (lane == parent_ref[r])
-        meta_ref[d] = jnp.where(hit, 1.0, meta_ref[d])
+        meta_ref[d] = jnp.where(row == rank, parent_ref[r].astype(jnp.float32), meta_ref[d])
     out_ref[:, pl.ds(KV_HEADS * head_span, 16), :] = meta_ref[...].astype(jnp.bfloat16)
 
 
-def parent_kernel(
-    cap, chunk, pages_ref, len_ref, recv_ref, store_ref, out_ref, bias_ref
-):
+def two_codes(values, steps):
+    scaled = values * steps
+    whole = jnp.floor(scaled)
+    rest = jnp.minimum(jnp.floor((scaled - whole) * 65536.0 + 0.5), 65535.0) - 32768.0
+    return whole, rest
+
+
+def from_codes(whole, rest, steps):
+    return (whole + (rest + 32768.0) * (1.0 / 65536.0)) * (1.0 / steps)
+
+
+def parent_kernel(cap, chunk, pages_ref, len_ref, recv_ref, store_ref, out_ref, key_ref, value_ref):
     parents, page_count = pages_ref.shape
     sources = recv_ref.shape[0]
     head_span = cap * HEAD_ROWS
-    row, lane = iota((PAGE, HEAD_DIM), 0), iota((PAGE, HEAD_DIM), 1)
+    tokens = page_count * PAGE
     for p in range(parents):
         for i in range(page_count):
-            keep = (lane == p) & (row + i * PAGE < len_ref[p])
             start = pl.multiple_of(pages_ref[p, i] * PAGE, PAGE)
-            bias_ref[pl.ds(start, PAGE), :] = jnp.where(keep, 0.0, MASKED).astype(jnp.bfloat16)
+            page = store_ref[pl.ds(start, PAGE), :]
+            for g in range(KV_HEADS):
+                span = (g, pl.ds(i * PAGE, PAGE), pl.ds(p * HEAD_DIM, HEAD_DIM))
+                key_ref[span] = page[:, g * HEAD_DIM : (g + 1) * HEAD_DIM]
+                value_ref[span] = page[:, KEY_WIDTH + g * HEAD_DIM : KEY_WIDTH + (g + 1) * HEAD_DIM]
+
+    rows = chunk * head_span
+    lanes = iota((rows, HEAD_DIM), 1)
+    positions = iota((rows, tokens), 1)
 
     def body(c, carry):
         base = c * chunk
-        rows = chunk * head_span
         meta = recv_ref[pl.ds(base, chunk), pl.ds(KV_HEADS * head_span, 16), :].astype(jnp.float32)
         picks = [
             jnp.broadcast_to(meta[:, s : s + 1, :], (chunk, HEAD_ROWS, HEAD_DIM)) for s in range(cap)
         ]
-        pick = jnp.concatenate(picks, axis=1).reshape(rows, HEAD_DIM).astype(jnp.bfloat16)
+        parent = jnp.concatenate(picks, axis=1).reshape(rows, HEAD_DIM)
+        limit = jnp.full((rows, HEAD_DIM), len_ref[0], jnp.int32)
+        for p in range(1, parents):
+            limit = jnp.where(parent == p, len_ref[p], limit)
+        limit = limit[:, :1]
+        parent_low = parent.astype(jnp.bfloat16)
         stats = jnp.zeros((rows, HEAD_DIM), jnp.float32)
-        lanes = iota((rows, HEAD_DIM), 1)
         for g in range(KV_HEADS):
             query = recv_ref[pl.ds(base, chunk), pl.ds(g * head_span, head_span), :].reshape(rows, HEAD_DIM)
-            keys = store_ref[:, pl.ds(g * HEAD_DIM, HEAD_DIM)]
-            values = store_ref[:, pl.ds(KEY_WIDTH + g * HEAD_DIM, HEAD_DIM)]
-            scores = lax.dot_general(
-                jnp.concatenate([query, pick], axis=1),
-                jnp.concatenate([keys, bias_ref[...]], axis=1),
-                NT,
-                preferred_element_type=jnp.float32,
-            ) * SCALE
+            query = jnp.concatenate(
+                [jnp.where(parent_low == p, query, jnp.zeros_like(query)) for p in range(parents)], axis=1
+            )
+            scores = lax.dot_general(query, key_ref[g], NT, preferred_element_type=jnp.float32) * SCALE
+            scores = jnp.where(positions < limit, scores, MASKED)
             top = jnp.max(scores, axis=1, keepdims=True)
             terms = jnp.exp(scores - top)
             total = jnp.sum(terms, axis=1, keepdims=True)
-            blended = jnp.dot(terms.astype(jnp.bfloat16), values, preferred_element_type=jnp.float32)
-            out_ref[pl.ds(base, chunk), pl.ds(g * head_span, head_span), :] = blended.reshape(
+            both = jnp.dot(terms.astype(jnp.bfloat16), value_ref[g], preferred_element_type=jnp.float32)
+            blended = both[:, :HEAD_DIM]
+            for p in range(1, parents):
+                blended = jnp.where(parent == p, both[:, p * HEAD_DIM : (p + 1) * HEAD_DIM], blended)
+            reach = jnp.maximum(jnp.max(jnp.abs(blended), axis=1, keepdims=True), 1e-30)
+            coded = jnp.round(blended * (32767.0 / reach)).astype(jnp.int32).astype(jnp.int16)
+            out_ref[pl.ds(base, chunk), pl.ds(g * head_span, head_span), :] = coded.reshape(
                 chunk, head_span, HEAD_DIM
             )
             stats = jnp.where(lanes == g, top, stats)
             stats = jnp.where(lanes == KV_HEADS + g, total, stats)
-        flat = stats.T[:STAT_ROWS, :]
+            stats = jnp.where(lanes == 2 * KV_HEADS + g, reach, stats)
+        flat = stats.T
+        top, total, reach = (flat[k * KV_HEADS : (k + 1) * KV_HEADS, :] for k in range(3))
+        codes = two_codes(top + jnp.log(total), LOG_STEPS) + two_codes(jnp.log2(reach / total), SCALE_STEPS)
+        flat = jnp.concatenate(codes, axis=0).astype(jnp.int32).astype(jnp.int16)
         for j in range(chunk):
             piece = flat[:, j * head_span : (j + 1) * head_span]
             if head_span < HEAD_DIM:
                 piece = jnp.concatenate(
-                    [piece, jnp.zeros((STAT_ROWS, HEAD_DIM - head_span), jnp.float32)], axis=1
+                    [piece, jnp.zeros((STAT_ROWS, HEAD_DIM - head_span), jnp.int16)], axis=1
                 )
             out_ref[base + j, pl.ds(KV_HEADS * head_span, STAT_ROWS), :] = piece
         return carry
@@ -147,13 +173,9 @@
         )
 
 
-def merge_kernel(
-    cap, owner_ref, pages_ref, len_ref, back_ref, query_ref, store_ref, step_ref, out_ref,
-    bias_ref, part_ref, stat_ref,
-):
+def local_kernel(pages_ref, len_ref, query_ref, store_ref, step_ref, out_ref, stat_ref, bias_ref):
     count = query_ref.shape[0]
     rows = count * HEAD_ROWS
-    head_span = cap * HEAD_ROWS
     fill_suffix_bias(pages_ref, len_ref, bias_ref, lambda length, t: length - 1)
     steps = 2 * count
     step_pad = -steps % HEAD_DIM
@@ -162,26 +184,12 @@
     step_bias = jnp.where(seen, 0.0, MASKED).astype(jnp.bfloat16)
     pad = jnp.zeros((step_pad, HEAD_DIM), jnp.bfloat16)
 
-    names, ranks = slot_ranks(owner_ref, count)
-    for r in range(count):
-        d, rank = names[r], ranks[r]
-        for g in range(KV_HEADS):
-            start = pl.multiple_of(g * head_span + rank * HEAD_ROWS, HEAD_ROWS)
-            part_ref[g, pl.ds(r * HEAD_ROWS, HEAD_ROWS), :] = back_ref[d, pl.ds(start, HEAD_ROWS), :]
-        tile = back_ref[d, pl.ds(KV_HEADS * head_span, STAT_ROWS), :]
-        shift = lax.rem(HEAD_DIM - rank * HEAD_ROWS, HEAD_DIM)
-        stat_ref[pl.ds(r * STAT_ROWS, STAT_ROWS), :] = pltpu.roll(tile, shift, 1)
-    columns = stat_ref[...].T[:HEAD_ROWS, :]
-
-    def column(k):
-        return jnp.concatenate(
-            [columns[:, r * STAT_ROWS + k : r * STAT_ROWS + k + 1] for r in range(count)], axis=0
-        )
-
     def step_rows(c):
         return jnp.concatenate([step_ref[r, 2 * c : 2 * c + 2, :] for r in range(count)] + [pad], axis=0)
 
     pick = own_pick(count)
+    lanes = iota((rows, HEAD_DIM), 1)
+    stats = jnp.zeros((rows, HEAD_DIM), jnp.float32)
     for g in range(KV_HEADS):
         query = query_ref[:, pl.ds(g * HEAD_ROWS, HEAD_ROWS), :].reshape(rows, HEAD_DIM)
         query = jnp.concatenate([query, pick], axis=1)
@@ -191,37 +199,69 @@
         step_values = step_rows(KV_HEADS + g)
         scores = lax.dot_general(query, keys, NT, preferred_element_type=jnp.float32) * SCALE
         step_scores = lax.dot_general(query, step_keys, NT, preferred_element_type=jnp.float32) * SCALE
-        part_top, part_total = column(g), column(KV_HEADS + g)
         top = jnp.maximum(
-            jnp.maximum(jnp.max(scores, axis=1, keepdims=True), jnp.max(step_scores, axis=1, keepdims=True)),
-            part_top,
+            jnp.max(scores, axis=1, keepdims=True), jnp.max(step_scores, axis=1, keepdims=True)
         )
         terms = jnp.exp(scores - top)
         step_terms = jnp.exp(step_scores - top)
-        part_weight = jnp.exp(part_top - top)
-        total = (
-            jnp.sum(terms, axis=1, keepdims=True)
-            + jnp.sum(step_terms, axis=1, keepdims=True)
-            + part_weight * part_total
-        )
+        total = jnp.sum(terms, axis=1, keepdims=True) + jnp.sum(step_terms, axis=1, keepdims=True)
         blended = jnp.dot(terms.astype(jnp.bfloat16), values, preferred_element_type=jnp.float32)
         blended = blended + jnp.dot(
             step_terms.astype(jnp.bfloat16), step_values, preferred_element_type=jnp.float32
         )
-        blended = blended + part_weight * part_ref[g]
-        out_ref[:, pl.ds(g * HEAD_ROWS, HEAD_ROWS), :] = (
-            (blended / total).astype(jnp.bfloat16).reshape(count, HEAD_ROWS, HEAD_DIM)
-        )
-
-
-def call(kernel, out_shape, scalars, arrays, scratch):
+        out_ref[g] = blended
+        stats = jnp.where(lanes == g, top, stats)
+        stats = jnp.where(lanes == KV_HEADS + g, total, stats)
+    stat_ref[...] = stats
+
+
+def merge_kernel(cap, owner_ref, back_ref, own_ref, own_stat_ref, out_ref, part_ref, decoded_ref, stat_ref):
+    count = out_ref.shape[0]
+    head_span = cap * HEAD_ROWS
+    codes = back_ref[:, pl.ds(KV_HEADS * head_span, STAT_ROWS), :].astype(jnp.int32).astype(jnp.float32)
+    codes = [codes[:, k * KV_HEADS : (k + 1) * KV_HEADS, :] for k in range(4)]
+    log_total = from_codes(codes[0], codes[1], LOG_STEPS)
+    unit = jnp.exp2(from_codes(codes[2], codes[3], SCALE_STEPS)) * (1.0 / 32767.0)
+    decoded_ref[...] = jnp.concatenate([log_total, unit], axis=1)
+
+    names, ranks = slot_ranks(owner_ref, count)
+    for r in range(count):
+        d, rank = names[r], ranks[r]
+        for g in range(KV_HEADS):
+            start = pl.multiple_of(g * head_span + rank * HEAD_ROWS, HEAD_ROWS)
+            coded = back_ref[d, pl.ds(start, HEAD_ROWS), :].astype(jnp.int32).astype(jnp.float32)
+            part_ref[g, pl.ds(r * HEAD_ROWS, HEAD_ROWS), :] = coded
+        shift = lax.rem(HEAD_DIM - rank * HEAD_ROWS, HEAD_DIM)
+        stat_ref[pl.ds(r * 2 * KV_HEADS, 2 * KV_HEADS), :] = pltpu.roll(decoded_ref[d], shift, 1)
+    columns = stat_ref[...].T[:HEAD_ROWS, :]
+
+    def column(k):
+        return jnp.concatenate(
+            [columns[:, r * 2 * KV_HEADS + k : r * 2 * KV_HEADS + k + 1] for r in range(count)], axis=0
+        )
+
+    for g in range(KV_HEADS):
+        part_top, unit = column(g), column(KV_HEADS + g)
+        own_top = own_stat_ref[:, g : g + 1]
+        own_total = own_stat_ref[:, KV_HEADS + g : KV_HEADS + g + 1]
+        top = jnp.maximum(own_top, part_top)
+        own_weight, part_weight = jnp.exp(own_top - top), jnp.exp(part_top - top)
+        inverse = 1.0 / (own_weight * own_total + part_weight)
+        merged = own_ref[g] * (own_weight * inverse) + part_ref[g] * (unit * part_weight * inverse)
+        out_ref[:, pl.ds(g * HEAD_ROWS, HEAD_ROWS), :] = merged.astype(jnp.bfloat16).reshape(
+            count, HEAD_ROWS, HEAD_DIM
+        )
+
+
+def call(kernel, out_shape, scalars, arrays, scratch, cost=None):
     smem = pl.BlockSpec(memory_space=pltpu.SMEM)
     vmem = pl.BlockSpec(memory_space=pltpu.VMEM)
     return pl.pallas_call(
         kernel,
         out_shape=out_shape,
         in_specs=[smem] * len(scalars) + [vmem] * len(arrays),
-        out_specs=vmem,
+        out_specs=jax.tree.map(lambda _: vmem, out_shape),
+        cost_estimate=cost,
         scratch_shapes=scratch,
         compiler_params=pltpu.CompilerParams(vmem_limit_bytes=VMEM_BYTES),
     )(*scalars, *arrays)
@@ -248,15 +288,22 @@
     suffix_table = suffix_pages.T
     token_rows = store.shape[0]
 
-    suffix_store = lax.ppermute(store, "role", [(0, 1)])
+    suffix_store = lax.ppermute(store, "role", [(0, 1), (1, 0)])
 
     sent = jax.ShapeDtypeStruct((seq_count, KV_HEADS * head_span + 16, HEAD_DIM), jnp.bfloat16)
-    answer = jax.ShapeDtypeStruct((seq_count, KV_HEADS * head_span + STAT_ROWS, HEAD_DIM), jnp.float32)
+    answer = jax.ShapeDtypeStruct((seq_count, KV_HEADS * head_span + STAT_ROWS, HEAD_DIM), jnp.int16)
     result = jax.ShapeDtypeStruct(query_rows.shape, jnp.bfloat16)
     bias = pltpu.VMEM((token_rows, HEAD_DIM), jnp.bfloat16)
+    rows = count * HEAD_ROWS
+    part = (KV_HEADS, rows, HEAD_DIM)
 
     def exchange(block):
         return lax.all_to_all(block, "seq", split_axis=0, concat_axis=0, tiled=True)
+
+    def tokens_of(rows):
+        return rows.reshape(count, width // HEAD_DIM, pair, HEAD_DIM).transpose(0, 2, 1, 3).reshape(
+            1, count, pair, width
+        )
 
     def send_queries(query_rows):
         packed = call(
@@ -273,34 +320,44 @@
     )
 
     def decode(received, suffix_store, query_rows):
+        parents, page_count = parent_pages.shape
+        beside = (KV_HEADS, page_count * PAGE, parents * HEAD_DIM)
         parts = call(
             functools.partial(parent_kernel, cap, chunk),
             answer,
             (parent_pages, parent_len),
             (received, store),
+            [pltpu.VMEM(beside, jnp.bfloat16), pltpu.VMEM(beside, jnp.bfloat16)],
+        )
+        back = exchange(parts)
+        own, own_stats = call(
+            local_kernel,
+            (jax.ShapeDtypeStruct(part, jnp.float32), jax.ShapeDtypeStruct((rows, HEAD_DIM), jnp.float32)),
+            (suffix_table, suffix_len),
+            (query_rows, suffix_store, head_rows(step_kv)),
             [bias],
-        )
-        back = exchange(parts)
-        return call(
-            functools.partial(merge_kernel, cap),
-            result,
-            (owner_of, suffix_table, suffix_len),
-            (back, query_rows, suffix_store, head_rows(step_kv)),
-            [
-                bias,
-                pltpu.VMEM((KV_HEADS, count * HEAD_ROWS, HEAD_DIM), jnp.float32),
-                pltpu.VMEM((count * STAT_ROWS, HEAD_DIM), jnp.float32),
-            ],
+            pl.CostEstimate(flops=1 << 31, bytes_accessed=1 << 22, transcendentals=1 << 20),
+        )
+        return tokens_of(
+            call(
+                functools.partial(merge_kernel, cap),
+                result,
+                (owner_of,),
+                (back, own, own_stats),
+                [
+                    pltpu.VMEM(part, jnp.float32),
+                    pltpu.VMEM((seq_count, 2 * KV_HEADS, HEAD_DIM), jnp.float32),
+                    pltpu.VMEM((count * 2 * KV_HEADS, HEAD_DIM), jnp.float32),
+                ],
+            )
         )
 
     def prefill(received, suffix_store, query_rows):
-        return call(
-            prefill_kernel, result, (suffix_table, suffix_len), (query_rows, store), [bias]
-        )
-
-    served = lax.cond(decoding, decode, prefill, received, suffix_store, query_rows)
-    served = served.reshape(count, width // HEAD_DIM, pair, HEAD_DIM).transpose(0, 2, 1, 3)
-    return served.reshape(1, count, pair, width)
+        return tokens_of(
+            call(prefill_kernel, result, (suffix_table, suffix_len), (query_rows, store), [bias])
+        )
+
+    return lax.cond(decoding, decode, prefill, received, suffix_store, query_rows)
 
 
 def solution(mesh):

time: 45.3 us -> 38.8 us (0.86)
  blocking collectives: 34.9 us -> 17.1 us
  waiting for transfers between devices: 0.01 us -> 6.82 us
  starting transfers between devices: 1.28 us -> 3.72 us
  local copies, waits for them, and re-layouts: 0.85 us -> 2.02 us
  Pallas kernels: 7.97 us -> 8.85 us
    all_to_all x2 -> x1, blocking collectives: 34.9 us -> 17.1 us  [exchange(): return lax.all_to_all(block, 'seq', split_axis=0, concat_axis=0, tiled=True)]
    all_to_all x0 -> x1, waiting for transfers between devices: none -> 6.81 us  [exchange(): return lax.all_to_all(block, 'seq', split_axis=0, concat_axis=0, tiled=True)]
    all_to_all x0 -> x1, starting transfers between devices: none -> 3.67 us  [exchange(): return lax.all_to_all(block, 'seq', split_axis=0, concat_axis=0, tiled=True)]
    unnamed x12 -> x18, local copies, waits for them, and re-layouts: 0.03 us -> 2.02 us
    ppermute x1, starting transfers between devices: 1.28 us -> 0.06 us  [local(): suffix_store = lax.ppermute(store, 'role', [(0, 1), (1, 0)])]
    pallas_call x3 -> x4, Pallas kernels: 7.97 us -> 8.85 us  [call(): pl.pallas_call(kernel, out_shape=out_shape, in_specs=[smem] * len(scalars...]
    reshape x2 -> x0, local copies, waits for them, and re-layouts: 0.82 us -> none  [the longest x1 0.77 us: local(): return served.reshape(1, count, pair, width)]
  transfers between devices with their start and end apart: 1 -> 2, of which waited for: 0 -> 1; matrix products, arithmetic and copies ran while one was open for 0% -> 0% of each run, Pallas kernels for 3% -> 10%
where the time goes in v2:
time: 38.8 us; the launch traced here: 38.6 us
  blocking collectives  17.1 us (44%)
  Pallas kernels  8.85 us (23%)
  waiting for transfers between devices  6.82 us (18%)
  starting transfers between devices  3.72 us (10%)
  local copies, waits for them, and re-layouts  2.02 us (5%)
    all_to_all x1, blocking collectives, exchange(): return lax.all_to_all(block, 'seq', split_axis=0, concat_axis=0, tiled=True)  17.1 us
    pallas_call x4, Pallas kernels, call(): pl.pallas_call(kernel, out_shape=out_shape, in_specs=[smem] * len(scalars...  8.85 us
    all_to_all x1, waiting for transfers between devices, exchange(): return lax.all_to_all(block, 'seq', split_axis=0, concat_axis=0, tiled=True)  6.81 us
    all_to_all x1, starting transfers between devices, exchange(): return lax.all_to_all(block, 'seq', split_axis=0, concat_axis=0, tiled=True)  3.67 us
    unnamed x18, local copies, waits for them, and re-layouts  2.02 us
  transfers between devices with their start and end apart: 2, of which 1 were waited for; matrix products, arithmetic and copies ran while one was open for 0% of the time, Pallas kernels for 10%

profile of v2, /device:TPU:1, one launch (start us, length us, event | category | flops | bytes accessed | tf_op | source)
XLA Modules:
  0.0 38.6 jit_solution(5031382027628704736)
XLA Ops:
  0.0 0.1 collective-permute-start
  0.1 0.0 copy-start.3
  0.1 0.0 copy-start.7
  0.1 0.7 %copy-done.3 = s32[16,1]{0,1:T(1,128)S(1)} copy-done((s32[16,1]{0,1:T(1,128)S(1)}, s32[16,1]{0,1:T(1,128)}, u32[]{:S(2)}) %copy-start.3) | copy-done | bytes 88
  0.7 0.0 copy-done.7
  0.7 18.4 %conditional.2 = (bf16[8,272,128]{2,1,0:T(8,128)(2,1)S(1)}) conditional(s32[]{:T(128)} %convert_element_type.4, () %tuple.18, (s32[16]{0:T(128)S(1)}, s32[16]{0:T(128)S(1)}, bf16[16,64,128]{2,1,0:T(8,128)(2,1)}) %tuple.40), branch_computations={%region_0.0_spmd, %region_1.0_spmd} | conditional | bytes 1114120 | solution.py:318
  0.8 1.3 %branch_1_fun.4 = bf16[8,272,128]{2,1,0:T(8,128)(2,1)S(1)} custom-call(s32[16]{0:T(128)S(1)} %get-tuple-element.44.owner_ref, s32[16]{0:T(128)S(1)} %get-tuple-element.65.parent_ref, bf16[16,64,128]{2,1,0:T(8,128)(2,1)} %get-tuple-element.47.query_ref), custom_call_target="tpu_custom_call" | custom-call | tf_op jit(solution)/shard_map/cond/branch_1_fun/pallas_call | solution.py:259
  2.1 17.1 %all_to_all.8 = bf16[8,272,128]{2,1,0:T(8,128)(2,1)S(1)} all-to-all(bf16[8,272,128]{2,1,0:T(8,128)(2,1)S(1)} %branch_1_fun.4), channel_id=1, replica_groups=mesh['groups'=2,'role'=2,'seq'=8] {'seq'}, dimensions={0} | all-to-all | bytes 1114112 | tf_op jit(solution)/shard_map/cond/branch_1_fun/all_to_all | solution.py:301
  19.1 0.0 collective-permute-done
  19.1 0.0 copy-done
  19.1 0.0 copy-done.5
  19.1 0.0 copy-done.8
  19.2 0.0 copy-done.9
  19.2 0.6 %copy-done.4 = s32[16,2]{0,1:T(2,128)S(1)} copy-done((s32[16,2]{0,1:T(2,128)S(1)}, s32[16,2]{0,1:T(2,128)}, u32[]{:S(2)}) %copy-start.4) | copy-done | bytes 152
  19.8 0.0 copy-done.6
  19.8 18.1 %conditional.3 = (bf16[1,16,2,4096]{3,2,1,0:T(2,128)(2,1)S(1)}) conditional(s32[]{:T(128)} %convert_element_type.4, (s32[2,16]{1,0:T(2,128)S(1)}, s32[16]{0:T(128)S(1)}, bf16[16,64,128]{2,1,0:T(8,128)(2,1)}, bf16[512,1024]{1,0:T(8,128)(2,1)S(1)}) %tuple.38, (s32[2,16]{1,0:T(2,128)S(1)}, s32[2]{0:T(128)S(1)}, bf16[8,272,128]{2,1,0:T(8,128)(2,1)S(1)}, ...), branch_computations={%region_2.0_spmd, %region_3.0_spmd} | conditional | flops 2147483648 | bytes 6914116 | solution.py:360
  19.8 3.2 %branch_1_fun.5 = s16[8,272,128]{2,1,0:T(8,128)(2,1)} custom-call(s32[2,16]{1,0:T(2,128)S(1)} %get-tuple-element.70.pages_ref, s32[2]{0:T(128)S(1)} %get-tuple-element.71.len_ref, bf16[8,272,128]{2,1,0:T(8,128)(2,1)S(1)} %get-tuple-element.55.recv_ref, bf16[512,1024]{1,0:T(8,128)(2,1)S(1)} %get-tuple-element.56.store_ref), custom_call_target="tpu_custom_call" | custom-call | tf_op jit(solution)/shard_map/cond/branch_1_fun/pallas_call | solution.py:259
  23.0 3.7 %all-to-all-start.1 = ((s16[8,272,128]{2,1,0:T(8,128)(2,1)}), s16[8,272,128]{2,1,0:T(8,128)(2,1)S(1)}, u32[]{:S(2)}, u32[]{:S(2)}) async-start(s16[8,272,128]{2,1,0:T(8,128)(2,1)} %branch_1_fun.5), calls=%async_computation.1 | async-start | bytes 1114112 | tf_op jit(solution)/shard_map/cond/branch_1_fun/all_to_all | solution.py:301
  26.6 0.0 copy-done.1
  26.6 2.6 %branch_1_fun.6 = (f32[4,256,128]{2,1,0:T(8,128)S(1)}, f32[256,128]{1,0:T(8,128)S(1)}) custom-call(s32[2,16]{1,0:T(2,128)S(1)} %get-tuple-element.57.pages_ref, s32[16]{0:T(128)S(1)} %get-tuple-element.58.len_ref, bf16[16,64,128]{2,1,0:T(8,128)(2,1)S(1)} %copy-done.1, bf16[512,1024]{1,0:T(8,128)(2,1)S(1)} %get-tuple-element.60.store_ref, ...), custom_call_target="tpu_custom_call" | custom-call | flops 2147483648 | bytes 4194304 | tf_op jit(solution)/shard_map/cond/branch_1_fun/pallas_call | solution.py:259
  29.2 6.8 %all-to-all-done.1.back_ref = s16[8,272,128]{2,1,0:T(8,128)(2,1)S(1)} async-done(((s16[8,272,128]{2,1,0:T(8,128)(2,1)}), s16[8,272,128]{2,1,0:T(8,128)(2,1)S(1)}, u32[]{:S(2)}, u32[]{:S(2)}) %all-to-all-start.1) | async-done | bytes 557088 | tf_op jit(solution)/shard_map/cond/branch_1_fun/all_to_all | solution.py:301
  36.0 1.8 %branch_1_fun.7 = bf16[16,64,128]{2,1,0:T(8,128)(2,1)S(1)} custom-call(s32[16]{0:T(128)S(1)} %get-tuple-element.52.owner_ref, s16[8,272,128]{2,1,0:T(8,128)(2,1)S(1)} %all-to-all-done.1.back_ref, f32[4,256,128]{2,1,0:T(8,128)S(1)} %get-tuple-element.62.own_ref, f32[256,128]{1,0:T(8,128)S(1)} %get-tuple-element.63.own_stat_ref), custom_call_target="tpu_custom_call" | custom-call | tf_op jit(solution)/shard_map/cond/branch_1_fun/pallas_call | solution.py:259
  37.9 0.0 copy-start.2
  37.9 0.7 %copy-done.2 = bf16[1,16,2,4096]{3,2,1,0:T(2,128)(2,1)} copy-done((bf16[1,16,2,4096]{3,2,1,0:T(2,128)(2,1)}, bf16[1,16,2,4096]{3,2,1,0:T(2,128)(2,1)S(1)}, u32[]{:S(2)}) %copy-start.2) | copy-done | bytes 262168
  (7 shorter events, 0.0 us)
Async XLA Ops:
  0.0 19.1 %collective-permute-start = (bf16[512,1024]{1,0:T(8,128)(2,1)}, bf16[512,1024]{1,0:T(8,128)(2,1)S(1)}, u32[]{:S(2)}, u32[]{:S(2)}) collective-permute-start(bf16[512,1024]{1,0:T(8,128)(2,1)} %bitcast.23), channel_id=1, source_target_pairs={{0,8},{8,0},{1,9},{9,1},{2,10},{10,2},{3,11},{11,3},{4,12},{12,4},... | collective-permute-start | bytes 3145736 | tf_op jit(solution)/shard_map/ppermute | solution.py:291
  0.1 0.7 %copy-start.3 = (s32[16,1]{0,1:T(1,128)S(1)}, s32[16,1]{0,1:T(1,128)}, u32[]{:S(2)}) copy-start(s32[16,1]{0,1:T(1,128)} %param.18) | copy-start | bytes 196
  0.1 0.7 %copy-start.7 = (s32[16]{0:T(128)S(1)}, s32[16]{0:T(128)}, u32[]{:S(2)}) copy-start(s32[16]{0:T(128)} %param.19) | copy-start | bytes 196
  0.7 18.4 %copy-start = (bf16[1,512,1024]{2,1,0:T(8,128)(2,1)S(1)}, bf16[1,512,1024]{2,1,0:T(8,128)(2,1)}, u32[]{:S(2)}) copy-start(bf16[1,512,1024]{2,1,0:T(8,128)(2,1)} %param.13) | copy-start | bytes 3145732
  0.7 18.4 %copy-start.5 = (s32[2,16]{1,0:T(2,128)S(1)}, s32[2,16]{1,0:T(2,128)}, u32[]{:S(2)}) copy-start(s32[2,16]{1,0:T(2,128)} %param.20) | copy-start | bytes 388
  0.7 18.4 %copy-start.8 = (s32[2]{0:T(128)S(1)}, s32[2]{0:T(128)}, u32[]{:S(2)}) copy-start(s32[2]{0:T(128)} %param.21) | copy-start | bytes 28
  0.7 18.4 %copy-start.9 = (bf16[16,2,1024]{2,1,0:T(2,128)(2,1)S(1)}, bf16[16,2,1024]{2,1,0:T(2,128)(2,1)}, u32[]{:S(2)}) copy-start(bf16[16,2,1024]{2,1,0:T(2,128)(2,1)} %param.15) | copy-start | bytes 196612
  19.1 0.7 %copy-start.4 = (s32[16,2]{0,1:T(2,128)S(1)}, s32[16,2]{0,1:T(2,128)}, u32[]{:S(2)}) copy-start(s32[16,2]{0,1:T(2,128)} %param.16) | copy-start | bytes 388
  19.1 0.7 %copy-start.6 = (s32[16]{0:T(128)S(1)}, s32[16]{0:T(128)}, u32[]{:S(2)}) copy-start(s32[16]{0:T(128)} %param.17) | copy-start | bytes 196
  23.0 3.7 %copy-start.1 = (bf16[16,64,128]{2,1,0:T(8,128)(2,1)S(1)}, bf16[16,64,128]{2,1,0:T(8,128)(2,1)}, u32[]{:S(2)}) copy-start(bf16[16,64,128]{2,1,0:T(8,128)(2,1)} %get-tuple-element.59.query_ref) | copy-start | bytes 786436 | tf_op jit(solution)/shard_map/cond
  23.0 13.1 %all-to-all-start.1 = ((s16[8,272,128]{2,1,0:T(8,128)(2,1)}), s16[8,272,128]{2,1,0:T(8,128)(2,1)S(1)}, u32[]{:S(2)}, u32[]{:S(2)}) async-start(s16[8,272,128]{2,1,0:T(8,128)(2,1)} %branch_1_fun.5), calls=%async_computation.1 | async-start | bytes 1114112 | tf_op jit(solution)/shard_map/cond/branch_1_fun/all_to_all | solution.py:301
  37.9 0.7 %copy-start.2 = (bf16[1,16,2,4096]{3,2,1,0:T(2,128)(2,1)}, bf16[1,16,2,4096]{3,2,1,0:T(2,128)(2,1)S(1)}, u32[]{:S(2)}) copy-start(bf16[1,16,2,4096]{3,2,1,0:T(2,128)(2,1)S(1)} %get-tuple-element.78) | copy-start | bytes 786436

commit v3 on v2

--- a/solution.py
+++ b/solution.py
@@ -28,7 +28,8 @@
 
 
 def slot_ranks(owner_ref, count):
-    names = [owner_ref[r] for r in range(count)]
+    owner = owner_ref[...]
+    names = [owner[0, r] for r in range(count)]
     ranks = []
     for r in range(count):
         rank = jnp.int32(0)
@@ -38,7 +39,11 @@
     return names, ranks
 
 
-def pack_kernel(cap, owner_ref, parent_ref, query_ref, out_ref, meta_ref):
+def pack_kernel(cap, query_ref, owner_ref, parent_ref, *refs):
+    tables, (out_ref, *copies), meta_ref = refs[: len(refs) // 2 - 1], refs[len(refs) // 2 - 1 : -1], refs[-1]
+    for table, copy in zip((owner_ref, *tables), copies):
+        copy[...] = table[...]
+    parent = parent_ref[...]
     count = query_ref.shape[0]
     head_span = cap * HEAD_ROWS
     out_ref[...] = jnp.zeros_like(out_ref)
@@ -50,8 +55,15 @@
         for g in range(KV_HEADS):
             start = pl.multiple_of(g * head_span + rank * HEAD_ROWS, HEAD_ROWS)
             out_ref[d, pl.ds(start, HEAD_ROWS), :] = query_ref[r, pl.ds(g * HEAD_ROWS, HEAD_ROWS), :]
-        meta_ref[d] = jnp.where(row == rank, parent_ref[r].astype(jnp.float32), meta_ref[d])
+        meta_ref[d] = jnp.where(row == rank, parent[0, r].astype(jnp.float32), meta_ref[d])
     out_ref[:, pl.ds(KV_HEADS * head_span, 16), :] = meta_ref[...].astype(jnp.bfloat16)
+
+
+def idle_kernel(*refs):
+    tables, (out_ref, *copies) = refs[: len(refs) // 2], refs[len(refs) // 2 :]
+    out_ref[...] = jnp.zeros_like(out_ref)
+    for table, copy in zip(tables, copies):
+        copy[...] = table[...]
 
 
 def two_codes(values, steps):
@@ -67,12 +79,13 @@
 
 def parent_kernel(cap, chunk, pages_ref, len_ref, recv_ref, store_ref, out_ref, key_ref, value_ref):
     parents, page_count = pages_ref.shape
+    pages, lengths = pages_ref[...], len_ref[...]
     sources = recv_ref.shape[0]
     head_span = cap * HEAD_ROWS
     tokens = page_count * PAGE
     for p in range(parents):
         for i in range(page_count):
-            start = pl.multiple_of(pages_ref[p, i] * PAGE, PAGE)
+            start = pl.multiple_of(pages[p, i] * PAGE, PAGE)
             page = store_ref[pl.ds(start, PAGE), :]
             for g in range(KV_HEADS):
                 span = (g, pl.ds(i * PAGE, PAGE), pl.ds(p * HEAD_DIM, HEAD_DIM))
@@ -90,9 +103,9 @@
             jnp.broadcast_to(meta[:, s : s + 1, :], (chunk, HEAD_ROWS, HEAD_DIM)) for s in range(cap)
         ]
         parent = jnp.concatenate(picks, axis=1).reshape(rows, HEAD_DIM)
-        limit = jnp.full((rows, HEAD_DIM), len_ref[0], jnp.int32)
+        limit = jnp.full((rows, HEAD_DIM), lengths[0, 0], jnp.int32)
         for p in range(1, parents):
-            limit = jnp.where(parent == p, len_ref[p], limit)
+            limit = jnp.where(parent == p, lengths[0, p], limit)
         limit = limit[:, :1]
         parent_low = parent.astype(jnp.bfloat16)
         stats = jnp.zeros((rows, HEAD_DIM), jnp.float32)
@@ -136,11 +149,12 @@
 
 def fill_suffix_bias(pages_ref, len_ref, bias_ref, last_of):
     page_count, count = pages_ref.shape
+    pages, lengths = pages_ref[...], len_ref[...]
     row, lane = iota((PAGE, HEAD_DIM), 0), iota((PAGE, HEAD_DIM), 1)
     for r in range(count):
         for i in range(page_count):
-            keep = (lane // 2 == r) & (row + i * PAGE <= last_of(len_ref[r], lane % 2))
-            start = pl.multiple_of(pages_ref[i, r] * PAGE, PAGE)
+            keep = (lane // 2 == r) & (row + i * PAGE <= last_of(lengths[0, r], lane % 2))
+            start = pl.multiple_of(pages[i, r] * PAGE, PAGE)
             bias_ref[pl.ds(start, PAGE), :] = jnp.where(keep, 0.0, MASKED).astype(jnp.bfloat16)
 
 
@@ -253,18 +267,17 @@
         )
 
 
-def call(kernel, out_shape, scalars, arrays, scratch, cost=None):
-    smem = pl.BlockSpec(memory_space=pltpu.SMEM)
+def call(kernel, out_shape, arrays, scratch, cost=None):
     vmem = pl.BlockSpec(memory_space=pltpu.VMEM)
     return pl.pallas_call(
         kernel,
         out_shape=out_shape,
-        in_specs=[smem] * len(scalars) + [vmem] * len(arrays),
+        in_specs=[vmem] * len(arrays),
         out_specs=jax.tree.map(lambda _: vmem, out_shape),
         cost_estimate=cost,
         scratch_shapes=scratch,
         compiler_params=pltpu.CompilerParams(vmem_limit_bytes=VMEM_BYTES),
-    )(*scalars, *arrays)
+    )(*arrays)
 
 
 def head_rows(tokens):
@@ -284,8 +297,8 @@
     head_span = cap * HEAD_ROWS
     chunk = max(1, 256 // head_span)
     query_rows = head_rows(queries[0])
-    owner_of = owner.reshape(-1)
-    suffix_table = suffix_pages.T
+    owner_row, parent_row = owner.reshape(1, -1), parent_id.reshape(1, -1)
+    tables = (suffix_pages.T, suffix_len.reshape(1, -1), parent_pages, parent_len.reshape(1, -1))
     token_rows = store.shape[0]
 
     suffix_store = lax.ppermute(store, "role", [(0, 1), (1, 0)])
@@ -305,36 +318,37 @@
             1, count, pair, width
         )
 
+    handed = (sent, *(jax.ShapeDtypeStruct(t.shape, t.dtype) for t in (owner_row, *tables)))
+
     def send_queries(query_rows):
-        packed = call(
+        packed, *copies = call(
             functools.partial(pack_kernel, cap),
-            sent,
-            (owner_of, parent_id),
-            (query_rows,),
+            handed,
+            (query_rows, owner_row, parent_row, *tables),
             [pltpu.VMEM((seq_count, 16, HEAD_DIM), jnp.float32)],
         )
-        return exchange(packed)
-
-    received = lax.cond(
-        decoding, send_queries, lambda query_rows: jnp.zeros(sent.shape, sent.dtype), query_rows
-    )
+        return exchange(packed), *copies
+
+    def idle(query_rows):
+        return call(idle_kernel, handed, (owner_row, *tables), [])
+
+    received = lax.cond(decoding, send_queries, idle, query_rows)
 
     def decode(received, suffix_store, query_rows):
+        received, owner_row, suffix_table, suffix_lengths, parent_pages, parent_lengths = received
         parents, page_count = parent_pages.shape
         beside = (KV_HEADS, page_count * PAGE, parents * HEAD_DIM)
         parts = call(
             functools.partial(parent_kernel, cap, chunk),
             answer,
-            (parent_pages, parent_len),
-            (received, store),
+            (parent_pages, parent_lengths, received, store),
             [pltpu.VMEM(beside, jnp.bfloat16), pltpu.VMEM(beside, jnp.bfloat16)],
         )
         back = exchange(parts)
         own, own_stats = call(
             local_kernel,
             (jax.ShapeDtypeStruct(part, jnp.float32), jax.ShapeDtypeStruct((rows, HEAD_DIM), jnp.float32)),
-            (suffix_table, suffix_len),
-            (query_rows, suffix_store, head_rows(step_kv)),
+            (suffix_table, suffix_lengths, query_rows, suffix_store, head_rows(step_kv)),
             [bias],
             pl.CostEstimate(flops=1 << 31, bytes_accessed=1 << 22, transcendentals=1 << 20),
         )
@@ -342,8 +356,7 @@
             call(
                 functools.partial(merge_kernel, cap),
                 result,
-                (owner_of,),
-                (back, own, own_stats),
+                (owner_row, back, own, own_stats),
                 [
                     pltpu.VMEM(part, jnp.float32),
                     pltpu.VMEM((seq_count, 2 * KV_HEADS, HEAD_DIM), jnp.float32),
@@ -354,7 +367,7 @@
 
     def prefill(received, suffix_store, query_rows):
         return tokens_of(
-            call(prefill_kernel, result, (suffix_table, suffix_len), (query_rows, store), [bias])
+            call(prefill_kernel, result, (*received[2:4], query_rows, store), [bias])
         )
 
     return lax.cond(decoding, decode, prefill, received, suffix_store, query_rows)

time: 38.8 us -> 36.7 us (0.946)
  local copies, waits for them, and re-layouts: 2.02 us -> 0.71 us
  Pallas kernels: 8.85 us -> 7.74 us
  waiting for transfers between devices: 6.82 us -> 7.29 us
    unnamed x18 -> x6, local copies, waits for them, and re-layouts: 2.02 us -> 0.7 us
    pallas_call x4, Pallas kernels: 8.85 us -> 7.74 us  [call(): pl.pallas_call(kernel, out_shape=out_shape, in_specs=[vmem] * len(arrays)...]
    all_to_all x1, waiting for transfers between devices: 6.81 us -> 7.29 us  [exchange(): return lax.all_to_all(block, 'seq', split_axis=0, concat_axis=0, tiled=True)]
where the time goes in v3:
time: 36.7 us; the launch traced here: 36.5 us
  blocking collectives  17 us (46%)
  Pallas kernels  7.74 us (21%)
  waiting for transfers between devices  7.29 us (20%)
  starting transfers between devices  3.72 us (10%)
  local copies, waits for them, and re-layouts  0.71 us (2%)
    all_to_all x1, blocking collectives, exchange(): return lax.all_to_all(block, 'seq', split_axis=0, concat_axis=0, tiled=True)  17 us
    pallas_call x4, Pallas kernels, call(): pl.pallas_call(kernel, out_shape=out_shape, in_specs=[vmem] * len(arrays)...  7.74 us
    all_to_all x1, waiting for transfers between devices, exchange(): return lax.all_to_all(block, 'seq', split_axis=0, concat_axis=0, tiled=True)  7.29 us
    all_to_all x1, starting transfers between devices, exchange(): return lax.all_to_all(block, 'seq', split_axis=0, concat_axis=0, tiled=True)  3.67 us
  transfers between devices with their start and end apart: 2, of which 1 were waited for; matrix products, arithmetic and copies ran while one was open for 0% of the time, Pallas kernels for 10%

profile of v3, /device:TPU:1, one launch (start us, length us, event | category | flops | bytes accessed | tf_op | source)
XLA Modules:
  0.0 36.5 jit_solution(3727959711599422451)
XLA Ops:
  0.0 0.0 copy-start
  0.0 0.1 collective-permute-start
  0.1 0.0 copy-start.3
  0.1 18.5 %conditional.2 = ((bf16[8,272,128]{2,1,0:T(8,128)(2,1)S(1)}, s32[1,16]{1,0:T(1,128)S(1)}, s32[2,16]{1,0:T(2,128)S(1)}, s32[1,16]{1,0:T(1,128)S(1)}, s32[2,16]{1,0:T(2,128)S(1)}, /*index=5*/s32[1,2]{1,0:T(1,128)S(1)})) conditional(s32[]{:T(128)} %convert_element_type.4, (s32[1,16]{1,0:T(1,128)}, s32[2,16]{1,0:T(2,128)}, s32[1,16]{1,0:T(1,128)}, ...), branch_computations={%region_0.0_spmd, %region_1.0_spmd} | conditional | bytes 1114168 | solution.py:335
  0.1 1.5 %branch_1_fun.4 = (bf16[8,272,128]{2,1,0:T(8,128)(2,1)S(1)}, s32[1,16]{1,0:T(1,128)S(1)}, s32[2,16]{1,0:T(2,128)S(1)}, s32[1,16]{1,0:T(1,128)S(1)}, s32[2,16]{1,0:T(2,128)S(1)}, /*index=5*/s32[1,2]{1,0:T(1,128)S(1)}) custom-call(bf16[16,64,128]{2,1,0:T(8,128)(2,1)} %get-tuple-element.66.query_ref, s32[1,16]{1,0:T(1,128)} %get-tuple-element.67.owner_ref, ...), custom_call_target="tpu_custom_call" | custom-call | tf_op jit(solution)/shard_map/cond/branch_1_fun/pallas_call | solution.py:272
  1.6 17.0 %all_to_all.8 = bf16[8,272,128]{2,1,0:T(8,128)(2,1)S(1)} all-to-all(bf16[8,272,128]{2,1,0:T(8,128)(2,1)S(1)} %get-tuple-element.73), channel_id=1, replica_groups=mesh['groups'=2,'role'=2,'seq'=8] {'seq'}, dimensions={0} | all-to-all | bytes 1114112 | tf_op jit(solution)/shard_map/cond/branch_1_fun/all_to_all | solution.py:314
  18.6 0.0 collective-permute-done
  18.6 0.0 copy-done
  18.6 0.0 copy-done.3
  18.6 17.3 %conditional.3 = (bf16[1,16,2,4096]{3,2,1,0:T(2,128)(2,1)S(1)}) conditional(s32[]{:T(128)} %convert_element_type.4, (s32[2,16]{1,0:T(2,128)S(1)}, s32[1,16]{1,0:T(1,128)S(1)}, bf16[16,64,128]{2,1,0:T(8,128)(2,1)}, bf16[512,1024]{1,0:T(8,128)(2,1)S(1)}) %tuple.33, (s32[2,16]{1,0:T(2,128)S(1)}, s32[1,2]{1,0:T(1,128)S(1)}, ...), branch_computations={%region_2.0_spmd, %region_3.0_spmd} | conditional | flops 2147483648 | bytes 6914116 | solution.py:373
  18.6 2.8 %branch_1_fun.5 = s16[8,272,128]{2,1,0:T(8,128)(2,1)} custom-call(s32[2,16]{1,0:T(2,128)S(1)} %get-tuple-element.84.pages_ref, s32[1,2]{1,0:T(1,128)S(1)} %get-tuple-element.85.len_ref, bf16[8,272,128]{2,1,0:T(8,128)(2,1)S(1)} %get-tuple-element.86.recv_ref, bf16[512,1024]{1,0:T(8,128)(2,1)S(1)} %get-tuple-element.87.store_ref), custom_call_target="tpu_custom_call" | custom-call | tf_op jit(solution)/shard_map/cond/branch_1_fun/pallas_call | solution.py:272
  21.4 0.0 copy-start.1
  21.4 3.7 %all-to-all-start.1 = ((s16[8,272,128]{2,1,0:T(8,128)(2,1)}), s16[8,272,128]{2,1,0:T(8,128)(2,1)S(1)}, u32[]{:S(2)}, u32[]{:S(2)}) async-start(s16[8,272,128]{2,1,0:T(8,128)(2,1)} %branch_1_fun.5), calls=%async_computation.1 | async-start | bytes 1114112 | tf_op jit(solution)/shard_map/cond/branch_1_fun/all_to_all | solution.py:314
  25.1 0.0 copy-done.1
  25.1 2.1 %branch_1_fun.6 = (f32[4,256,128]{2,1,0:T(8,128)S(1)}, f32[256,128]{1,0:T(8,128)S(1)}) custom-call(s32[2,16]{1,0:T(2,128)S(1)} %get-tuple-element.88.pages_ref, s32[1,16]{1,0:T(1,128)S(1)} %get-tuple-element.89.len_ref, bf16[16,64,128]{2,1,0:T(8,128)(2,1)S(1)} %copy-done.1, bf16[512,1024]{1,0:T(8,128)(2,1)S(1)} %get-tuple-element.91.store_ref, ...), custom_call_target="tpu_custom_call" | custom-call | flops 2147483648 | bytes 4194304 | tf_op jit(solution)/shard_map/cond/branch_1_fun/pallas_call | solution.py:272
  27.2 7.3 %all-to-all-done.1.back_ref = s16[8,272,128]{2,1,0:T(8,128)(2,1)S(1)} async-done(((s16[8,272,128]{2,1,0:T(8,128)(2,1)}), s16[8,272,128]{2,1,0:T(8,128)(2,1)S(1)}, u32[]{:S(2)}, u32[]{:S(2)}) %all-to-all-start.1) | async-done | bytes 557088 | tf_op jit(solution)/shard_map/cond/branch_1_fun/all_to_all | solution.py:314
  34.5 1.4 %branch_1_fun.7 = bf16[16,64,128]{2,1,0:T(8,128)(2,1)S(1)} custom-call(s32[1,16]{1,0:T(1,128)S(1)} %get-tuple-element.83.owner_ref, s16[8,272,128]{2,1,0:T(8,128)(2,1)S(1)} %all-to-all-done.1.back_ref, f32[4,256,128]{2,1,0:T(8,128)S(1)} %get-tuple-element.93.own_ref, f32[256,128]{1,0:T(8,128)S(1)} %get-tuple-element.94.own_stat_ref), custom_call_target="tpu_custom_call" | custom-call | tf_op jit(solution)/shard_map/cond/branch_1_fun/pallas_call | solution.py:272
  35.8 0.0 copy-start.2
  35.8 0.7 %copy-done.2 = bf16[1,16,2,4096]{3,2,1,0:T(2,128)(2,1)} copy-done((bf16[1,16,2,4096]{3,2,1,0:T(2,128)(2,1)}, bf16[1,16,2,4096]{3,2,1,0:T(2,128)(2,1)S(1)}, u32[]{:S(2)}) %copy-start.2) | copy-done | bytes 262168
Async XLA Ops:
  0.0 18.6 %copy-start = (bf16[1,512,1024]{2,1,0:T(8,128)(2,1)S(1)}, bf16[1,512,1024]{2,1,0:T(8,128)(2,1)}, u32[]{:S(2)}) copy-start(bf16[1,512,1024]{2,1,0:T(8,128)(2,1)} %param.13) | copy-start | bytes 3145732
  0.0 18.6 %collective-permute-start = (bf16[512,1024]{1,0:T(8,128)(2,1)}, bf16[512,1024]{1,0:T(8,128)(2,1)S(1)}, u32[]{:S(2)}, u32[]{:S(2)}) collective-permute-start(bf16[512,1024]{1,0:T(8,128)(2,1)} %bitcast.26), channel_id=1, source_target_pairs={{0,8},{8,0},{1,9},{9,1},{2,10},{10,2},{3,11},{11,3},{4,12},{12,4},... | collective-permute-start | bytes 3145736 | tf_op jit(solution)/shard_map/ppermute | solution.py:304
  0.1 18.5 %copy-start.3 = (bf16[16,2,1024]{2,1,0:T(2,128)(2,1)S(1)}, bf16[16,2,1024]{2,1,0:T(2,128)(2,1)}, u32[]{:S(2)}) copy-start(bf16[16,2,1024]{2,1,0:T(2,128)(2,1)} %param.15) | copy-start | bytes 196612
  21.4 3.7 %copy-start.1 = (bf16[16,64,128]{2,1,0:T(8,128)(2,1)S(1)}, bf16[16,64,128]{2,1,0:T(8,128)(2,1)}, u32[]{:S(2)}) copy-start(bf16[16,64,128]{2,1,0:T(8,128)(2,1)} %get-tuple-element.90.query_ref) | copy-start | bytes 786436 | tf_op jit(solution)/shard_map/cond
  21.4 13.1 %all-to-all-start.1 = ((s16[8,272,128]{2,1,0:T(8,128)(2,1)}), s16[8,272,128]{2,1,0:T(8,128)(2,1)S(1)}, u32[]{:S(2)}, u32[]{:S(2)}) async-start(s16[8,272,128]{2,1,0:T(8,128)(2,1)} %branch_1_fun.5), calls=%async_computation.1 | async-start | bytes 1114112 | tf_op jit(solution)/shard_map/cond/branch_1_fun/all_to_all | solution.py:314
  35.8 0.7 %copy-start.2 = (bf16[1,16,2,4096]{3,2,1,0:T(2,128)(2,1)}, bf16[1,16,2,4096]{3,2,1,0:T(2,128)(2,1)S(1)}, u32[]{:S(2)}) copy-start(bf16[1,16,2,4096]{3,2,1,0:T(2,128)(2,1)S(1)} %get-tuple-element.130) | copy-start | bytes 786436

commit v4 on v3

--- a/solution.py
+++ b/solution.py
@@ -18,6 +18,8 @@
 STAT_ROWS = 4 * KV_HEADS
 LOG_STEPS = 4.0
 SCALE_STEPS = 128.0
+CODE_TOP = 32600.0
+LOG2_E = 1.4426950408889634
 VMEM_BYTES = 48 * 1024 * 1024
 
 NT = (((1,), (1,)), ((), ()))
@@ -77,17 +79,20 @@
     return (whole + (rest + 32768.0) * (1.0 / 65536.0)) * (1.0 / steps)
 
 
-def parent_kernel(cap, chunk, pages_ref, len_ref, recv_ref, store_ref, out_ref, key_ref, value_ref):
+def parent_kernel(
+    cap, chunk, pages_ref, len_ref, recv_ref, store_ref, out_hbm, out_ref, key_ref, value_ref, sems
+):
     parents, page_count = pages_ref.shape
     pages, lengths = pages_ref[...], len_ref[...]
     sources = recv_ref.shape[0]
     head_span = cap * HEAD_ROWS
     tokens = page_count * PAGE
+    heads = range(KV_HEADS)
     for p in range(parents):
         for i in range(page_count):
             start = pl.multiple_of(pages[p, i] * PAGE, PAGE)
             page = store_ref[pl.ds(start, PAGE), :]
-            for g in range(KV_HEADS):
+            for g in heads:
                 span = (g, pl.ds(i * PAGE, PAGE), pl.ds(p * HEAD_DIM, HEAD_DIM))
                 key_ref[span] = page[:, g * HEAD_DIM : (g + 1) * HEAD_DIM]
                 value_ref[span] = page[:, KEY_WIDTH + g * HEAD_DIM : KEY_WIDTH + (g + 1) * HEAD_DIM]
@@ -96,9 +101,13 @@
     lanes = iota((rows, HEAD_DIM), 1)
     positions = iota((rows, tokens), 1)
 
+    def put(c, k):
+        part = (pl.ds(c * chunk, chunk), pl.ds(k * head_span, head_span if k < KV_HEADS else STAT_ROWS))
+        return pltpu.make_async_copy(out_ref.at[part], out_hbm.at[part], sems.at[c, k])
+
     def body(c, carry):
-        base = c * chunk
-        meta = recv_ref[pl.ds(base, chunk), pl.ds(KV_HEADS * head_span, 16), :].astype(jnp.float32)
+        part = pl.ds(c * chunk, chunk)
+        meta = recv_ref[part, pl.ds(KV_HEADS * head_span, 16), :].astype(jnp.float32)
         picks = [
             jnp.broadcast_to(meta[:, s : s + 1, :], (chunk, HEAD_ROWS, HEAD_DIM)) for s in range(cap)
         ]
@@ -106,34 +115,45 @@
         limit = jnp.full((rows, HEAD_DIM), lengths[0, 0], jnp.int32)
         for p in range(1, parents):
             limit = jnp.where(parent == p, lengths[0, p], limit)
-        limit = limit[:, :1]
+        bias = jnp.where(positions < limit[:, :1], 0.0, MASKED)
         parent_low = parent.astype(jnp.bfloat16)
-        stats = jnp.zeros((rows, HEAD_DIM), jnp.float32)
-        for g in range(KV_HEADS):
-            query = recv_ref[pl.ds(base, chunk), pl.ds(g * head_span, head_span), :].reshape(rows, HEAD_DIM)
+
+        def scores_of(g):
+            query = recv_ref[part, pl.ds(g * head_span, head_span), :].reshape(rows, HEAD_DIM)
             query = jnp.concatenate(
                 [jnp.where(parent_low == p, query, jnp.zeros_like(query)) for p in range(parents)], axis=1
             )
-            scores = lax.dot_general(query, key_ref[g], NT, preferred_element_type=jnp.float32) * SCALE
-            scores = jnp.where(positions < limit, scores, MASKED)
+            return lax.dot_general(query, key_ref[g], NT, preferred_element_type=jnp.float32)
+
+        def softmax_of(scores):
+            scores = scores + bias
             top = jnp.max(scores, axis=1, keepdims=True)
-            terms = jnp.exp(scores - top)
-            total = jnp.sum(terms, axis=1, keepdims=True)
-            both = jnp.dot(terms.astype(jnp.bfloat16), value_ref[g], preferred_element_type=jnp.float32)
+            terms = jnp.exp2((scores - top) * (SCALE * LOG2_E))
+            return terms.astype(jnp.bfloat16), top, jnp.sum(terms, axis=1, keepdims=True)
+
+        def blended_of(g, weights):
+            both = jnp.dot(weights, value_ref[g], preferred_element_type=jnp.float32)
             blended = both[:, :HEAD_DIM]
             for p in range(1, parents):
                 blended = jnp.where(parent == p, both[:, p * HEAD_DIM : (p + 1) * HEAD_DIM], blended)
-            reach = jnp.maximum(jnp.max(jnp.abs(blended), axis=1, keepdims=True), 1e-30)
-            coded = jnp.round(blended * (32767.0 / reach)).astype(jnp.int32).astype(jnp.int16)
-            out_ref[pl.ds(base, chunk), pl.ds(g * head_span, head_span), :] = coded.reshape(
-                chunk, head_span, HEAD_DIM
-            )
-            stats = jnp.where(lanes == g, top, stats)
-            stats = jnp.where(lanes == KV_HEADS + g, total, stats)
-            stats = jnp.where(lanes == 2 * KV_HEADS + g, reach, stats)
+            return blended
+
+        scores = [scores_of(g) for g in heads]
+        softmaxes = [softmax_of(scores[g]) for g in heads]
+        blends = [blended_of(g, softmaxes[g][0]) for g in heads]
+        stats = jnp.zeros((rows, HEAD_DIM), jnp.float32)
+        for g in heads:
+            reach = jnp.maximum(jnp.max(jnp.abs(blends[g]), axis=1, keepdims=True), 1e-30)
+            inverse = pltpu.reciprocal(reach, approx=True) * CODE_TOP
+            coded = jnp.round(blends[g] * inverse).astype(jnp.int32).astype(jnp.int16)
+            out_ref[part, pl.ds(g * head_span, head_span), :] = coded.reshape(chunk, head_span, HEAD_DIM)
+            put(c, g).start()
+            for k, value in enumerate((softmaxes[g][1], softmaxes[g][2], inverse)):
+                stats = jnp.where(lanes == k * KV_HEADS + g, value, stats)
         flat = stats.T
-        top, total, reach = (flat[k * KV_HEADS : (k + 1) * KV_HEADS, :] for k in range(3))
-        codes = two_codes(top + jnp.log(total), LOG_STEPS) + two_codes(jnp.log2(reach / total), SCALE_STEPS)
+        top, total, inverse = (flat[k * KV_HEADS : (k + 1) * KV_HEADS, :] for k in range(3))
+        codes = two_codes(top * SCALE + jnp.log(total), LOG_STEPS)
+        codes += two_codes(-jnp.log2(inverse * total), SCALE_STEPS)
         flat = jnp.concatenate(codes, axis=0).astype(jnp.int32).astype(jnp.int16)
         for j in range(chunk):
             piece = flat[:, j * head_span : (j + 1) * head_span]
@@ -141,10 +161,14 @@
                 piece = jnp.concatenate(
                     [piece, jnp.zeros((STAT_ROWS, HEAD_DIM - head_span), jnp.int16)], axis=1
                 )
-            out_ref[base + j, pl.ds(KV_HEADS * head_span, STAT_ROWS), :] = piece
+            out_ref[c * chunk + j, pl.ds(KV_HEADS * head_span, STAT_ROWS), :] = piece
+        put(c, KV_HEADS).start()
         return carry
 
-    lax.fori_loop(0, sources // chunk, body, 0, unroll=min(2, sources // chunk))
+    lax.fori_loop(0, sources // chunk, body, 0, unroll=sources == chunk)
+    for c in range(sources // chunk):
+        for k in range(KV_HEADS + 1):
+            put(c, k).wait()
 
 
 def fill_suffix_bias(pages_ref, len_ref, bias_ref, last_of):
@@ -226,54 +250,56 @@
         out_ref[g] = blended
         stats = jnp.where(lanes == g, top, stats)
         stats = jnp.where(lanes == KV_HEADS + g, total, stats)
-    stat_ref[...] = stats
-
-
-def merge_kernel(cap, owner_ref, back_ref, own_ref, own_stat_ref, out_ref, part_ref, decoded_ref, stat_ref):
+    stat_ref[...] = stats.T[: 2 * KV_HEADS, :]
+
+
+def merge_kernel(cap, owner_ref, back_ref, own_ref, own_stat_ref, out_ref, decoded_ref):
     count = out_ref.shape[0]
+    rows = count * HEAD_ROWS
     head_span = cap * HEAD_ROWS
     codes = back_ref[:, pl.ds(KV_HEADS * head_span, STAT_ROWS), :].astype(jnp.int32).astype(jnp.float32)
     codes = [codes[:, k * KV_HEADS : (k + 1) * KV_HEADS, :] for k in range(4)]
     log_total = from_codes(codes[0], codes[1], LOG_STEPS)
-    unit = jnp.exp2(from_codes(codes[2], codes[3], SCALE_STEPS)) * (1.0 / 32767.0)
+    unit = jnp.exp2(from_codes(codes[2], codes[3], SCALE_STEPS))
     decoded_ref[...] = jnp.concatenate([log_total, unit], axis=1)
 
     names, ranks = slot_ranks(owner_ref, count)
+    per_tile = HEAD_DIM // HEAD_ROWS
+    place = iota((2 * KV_HEADS, HEAD_DIM), 1) // HEAD_ROWS
+    tiles = []
+    for first in range(0, count, per_tile):
+        tile = jnp.zeros((2 * KV_HEADS, HEAD_DIM), jnp.float32)
+        for r in range(first, min(first + per_tile, count)):
+            shift = lax.rem((r - first) * HEAD_ROWS - ranks[r] * HEAD_ROWS + HEAD_DIM, HEAD_DIM)
+            tile = jnp.where(place == r - first, pltpu.roll(decoded_ref[names[r]], shift, 1), tile)
+        tiles.append(tile)
+    flat = jnp.concatenate(tiles, axis=1)[:, :rows]
+    part_top, unit = flat[:KV_HEADS], flat[KV_HEADS:]
+    own_top, own_total = own_stat_ref[:KV_HEADS, :], own_stat_ref[KV_HEADS:, :]
+    top = jnp.maximum(own_top, part_top)
+    own_weight, part_weight = jnp.exp(own_top - top), jnp.exp(part_top - top)
+    inverse = 1.0 / (own_weight * own_total + part_weight)
+    weights = [own_weight * inverse, unit * part_weight * inverse]
+    weights.append(jnp.zeros((HEAD_DIM - 2 * KV_HEADS, rows), jnp.float32))
+    weights = jnp.concatenate(weights, axis=0).T
     for r in range(count):
-        d, rank = names[r], ranks[r]
+        span = slice(r * HEAD_ROWS, (r + 1) * HEAD_ROWS)
         for g in range(KV_HEADS):
-            start = pl.multiple_of(g * head_span + rank * HEAD_ROWS, HEAD_ROWS)
-            coded = back_ref[d, pl.ds(start, HEAD_ROWS), :].astype(jnp.int32).astype(jnp.float32)
-            part_ref[g, pl.ds(r * HEAD_ROWS, HEAD_ROWS), :] = coded
-        shift = lax.rem(HEAD_DIM - rank * HEAD_ROWS, HEAD_DIM)
-        stat_ref[pl.ds(r * 2 * KV_HEADS, 2 * KV_HEADS), :] = pltpu.roll(decoded_ref[d], shift, 1)
-    columns = stat_ref[...].T[:HEAD_ROWS, :]
-
-    def column(k):
-        return jnp.concatenate(
-            [columns[:, r * 2 * KV_HEADS + k : r * 2 * KV_HEADS + k + 1] for r in range(count)], axis=0
-        )
-
-    for g in range(KV_HEADS):
-        part_top, unit = column(g), column(KV_HEADS + g)
-        own_top = own_stat_ref[:, g : g + 1]
-        own_total = own_stat_ref[:, KV_HEADS + g : KV_HEADS + g + 1]
-        top = jnp.maximum(own_top, part_top)
-        own_weight, part_weight = jnp.exp(own_top - top), jnp.exp(part_top - top)
-        inverse = 1.0 / (own_weight * own_total + part_weight)
-        merged = own_ref[g] * (own_weight * inverse) + part_ref[g] * (unit * part_weight * inverse)
-        out_ref[:, pl.ds(g * HEAD_ROWS, HEAD_ROWS), :] = merged.astype(jnp.bfloat16).reshape(
-            count, HEAD_ROWS, HEAD_DIM
-        )
-
-
-def call(kernel, out_shape, arrays, scratch, cost=None):
+            start = pl.multiple_of(g * head_span + ranks[r] * HEAD_ROWS, HEAD_ROWS)
+            part = back_ref[names[r], pl.ds(start, HEAD_ROWS), :].astype(jnp.int32).astype(jnp.float32)
+            merged = own_ref[g, span, :] * weights[span, g : g + 1]
+            merged = merged + part * weights[span, KV_HEADS + g : KV_HEADS + g + 1]
+            out_ref[r, pl.ds(g * HEAD_ROWS, HEAD_ROWS), :] = merged.astype(jnp.bfloat16)
+
+
+def call(kernel, out_shape, arrays, scratch, cost=None, out_space=pltpu.VMEM):
     vmem = pl.BlockSpec(memory_space=pltpu.VMEM)
+    put = pl.BlockSpec(memory_space=out_space)
     return pl.pallas_call(
         kernel,
         out_shape=out_shape,
         in_specs=[vmem] * len(arrays),
-        out_specs=jax.tree.map(lambda _: vmem, out_shape),
+        out_specs=jax.tree.map(lambda _: put, out_shape),
         cost_estimate=cost,
         scratch_shapes=scratch,
         compiler_params=pltpu.CompilerParams(vmem_limit_bytes=VMEM_BYTES),
@@ -295,7 +321,7 @@
     count, pair, width = queries.shape[1:]
     cap = max(2, 2 * count // seq_count)
     head_span = cap * HEAD_ROWS
-    chunk = max(1, 256 // head_span)
+    chunk = max(1, min(seq_count, 512 // head_span))
     query_rows = head_rows(queries[0])
     owner_row, parent_row = owner.reshape(1, -1), parent_id.reshape(1, -1)
     tables = (suffix_pages.T, suffix_len.reshape(1, -1), parent_pages, parent_len.reshape(1, -1))
@@ -342,12 +368,18 @@
             functools.partial(parent_kernel, cap, chunk),
             answer,
             (parent_pages, parent_lengths, received, store),
-            [pltpu.VMEM(beside, jnp.bfloat16), pltpu.VMEM(beside, jnp.bfloat16)],
+            [
+                pltpu.VMEM(answer.shape, jnp.int16),
+                pltpu.VMEM(beside, jnp.bfloat16),
+                pltpu.VMEM(beside, jnp.bfloat16),
+                pltpu.SemaphoreType.DMA((seq_count // chunk, KV_HEADS + 1)),
+            ],
+            out_space=pl.ANY,
         )
         back = exchange(parts)
         own, own_stats = call(
             local_kernel,
-            (jax.ShapeDtypeStruct(part, jnp.float32), jax.ShapeDtypeStruct((rows, HEAD_DIM), jnp.float32)),
+            (jax.ShapeDtypeStruct(part, jnp.float32), jax.ShapeDtypeStruct((2 * KV_HEADS, rows), jnp.float32)),
             (suffix_table, suffix_lengths, query_rows, suffix_store, head_rows(step_kv)),
             [bias],
             pl.CostEstimate(flops=1 << 31, bytes_accessed=1 << 22, transcendentals=1 << 20),
@@ -357,11 +389,7 @@
                 functools.partial(merge_kernel, cap),
                 result,
                 (owner_row, back, own, own_stats),
-                [
-                    pltpu.VMEM(part, jnp.float32),
-                    pltpu.VMEM((seq_count, 2 * KV_HEADS, HEAD_DIM), jnp.float32),
-                    pltpu.VMEM((count * 2 * KV_HEADS, HEAD_DIM), jnp.float32),
-                ],
+                [pltpu.VMEM((seq_count, 2 * KV_HEADS, HEAD_DIM), jnp.float32)],
             )
         )
 

time: 36.7 us -> 35.8 us (0.975)
  Pallas kernels: 7.74 us -> 6.85 us
    pallas_call x4, Pallas kernels: 7.74 us -> 6.85 us  [call(): pl.pallas_call(kernel, out_shape=out_shape, in_specs=[vmem] * len(arrays)...]
where the time goes in v4:
time: 35.8 us; the launch traced here: 35.6 us
  blocking collectives  17 us (47%)
  waiting for transfers between devices  7.26 us (20%)
  Pallas kernels  6.85 us (19%)
  starting transfers between devices  3.74 us (10%)
  local copies, waits for them, and re-layouts  0.71 us (2%)
    all_to_all x1, blocking collectives, exchange(): return lax.all_to_all(block, 'seq', split_axis=0, concat_axis=0, tiled=True)  17 us
    all_to_all x1, waiting for transfers between devices, exchange(): return lax.all_to_all(block, 'seq', split_axis=0, concat_axis=0, tiled=True)  7.26 us
    pallas_call x4, Pallas kernels, call(): pl.pallas_call(kernel, out_shape=out_shape, in_specs=[vmem] * len(arrays)...  6.85 us
    all_to_all x1, starting transfers between devices, exchange(): return lax.all_to_all(block, 'seq', split_axis=0, concat_axis=0, tiled=True)  3.68 us
  transfers between devices with their start and end apart: 2, of which 1 were waited for; matrix products, arithmetic and copies ran while one was open for 0% of the time, Pallas kernels for 10%

profile of v4, /device:TPU:1, one launch (start us, length us, event | category | flops | bytes accessed | tf_op | source)
XLA Modules:
  0.0 35.6 jit_solution(5240795677739672957)
XLA Ops:
  0.0 0.0 copy-start
  0.0 0.1 collective-permute-start
  0.1 0.0 copy-start.3
  0.1 18.5 %conditional.2 = ((bf16[8,272,128]{2,1,0:T(8,128)(2,1)S(1)}, s32[1,16]{1,0:T(1,128)S(1)}, s32[2,16]{1,0:T(2,128)S(1)}, s32[1,16]{1,0:T(1,128)S(1)}, s32[2,16]{1,0:T(2,128)S(1)}, /*index=5*/s32[1,2]{1,0:T(1,128)S(1)})) conditional(s32[]{:T(128)} %convert_element_type.4, (s32[1,16]{1,0:T(1,128)}, s32[2,16]{1,0:T(2,128)}, s32[1,16]{1,0:T(1,128)}, ...), branch_computations={%region_0.0_spmd, %region_1.0_spmd} | conditional | bytes 1114168 | solution.py:361
  0.1 1.5 %branch_1_fun.4 = (bf16[8,272,128]{2,1,0:T(8,128)(2,1)S(1)}, s32[1,16]{1,0:T(1,128)S(1)}, s32[2,16]{1,0:T(2,128)S(1)}, s32[1,16]{1,0:T(1,128)S(1)}, s32[2,16]{1,0:T(2,128)S(1)}, /*index=5*/s32[1,2]{1,0:T(1,128)S(1)}) custom-call(bf16[16,64,128]{2,1,0:T(8,128)(2,1)} %get-tuple-element.66.query_ref, s32[1,16]{1,0:T(1,128)} %get-tuple-element.67.owner_ref, ...), custom_call_target="tpu_custom_call" | custom-call | tf_op jit(solution)/shard_map/cond/branch_1_fun/pallas_call | solution.py:298
  1.6 17.0 %all_to_all.8 = bf16[8,272,128]{2,1,0:T(8,128)(2,1)S(1)} all-to-all(bf16[8,272,128]{2,1,0:T(8,128)(2,1)S(1)} %get-tuple-element.73), channel_id=1, replica_groups=mesh['groups'=2,'role'=2,'seq'=8] {'seq'}, dimensions={0} | all-to-all | bytes 1114112 | tf_op jit(solution)/shard_map/cond/branch_1_fun/all_to_all | solution.py:340
  18.6 0.0 collective-permute-done
  18.6 0.0 copy-done
  18.6 0.0 copy-done.3
  18.6 16.4 %conditional.3 = (bf16[1,16,2,4096]{3,2,1,0:T(2,128)(2,1)S(1)}) conditional(s32[]{:T(128)} %convert_element_type.4, (s32[2,16]{1,0:T(2,128)S(1)}, s32[1,16]{1,0:T(1,128)S(1)}, bf16[16,64,128]{2,1,0:T(8,128)(2,1)}, bf16[512,1024]{1,0:T(8,128)(2,1)S(1)}) %tuple.33, (s32[2,16]{1,0:T(2,128)S(1)}, s32[1,2]{1,0:T(1,128)S(1)}, ...), branch_computations={%region_2.0_spmd, %region_3.0_spmd} | conditional | flops 2147483648 | bytes 6914116 | solution.py:401
  18.6 2.3 %branch_1_fun.5 = s16[8,272,128]{2,1,0:T(8,128)(2,1)} custom-call(s32[2,16]{1,0:T(2,128)S(1)} %get-tuple-element.84.pages_ref, s32[1,2]{1,0:T(1,128)S(1)} %get-tuple-element.85.len_ref, bf16[8,272,128]{2,1,0:T(8,128)(2,1)S(1)} %get-tuple-element.86.recv_ref, bf16[512,1024]{1,0:T(8,128)(2,1)S(1)} %get-tuple-element.87.store_ref), custom_call_target="tpu_custom_call" | custom-call | tf_op jit(solution)/shard_map/cond/branch_1_fun/pallas_call | solution.py:298
  20.9 0.0 copy-start.1
  20.9 3.7 %all-to-all-start.1 = ((s16[8,272,128]{2,1,0:T(8,128)(2,1)}), s16[8,272,128]{2,1,0:T(8,128)(2,1)S(1)}, u32[]{:S(2)}, u32[]{:S(2)}) async-start(s16[8,272,128]{2,1,0:T(8,128)(2,1)} %branch_1_fun.5), calls=%async_computation.1 | async-start | bytes 1114112 | tf_op jit(solution)/shard_map/cond/branch_1_fun/all_to_all | solution.py:340
  24.6 0.0 copy-done.1
  24.6 2.1 %branch_1_fun.6 = (f32[4,256,128]{2,1,0:T(8,128)S(1)}, f32[8,256]{1,0:T(8,128)S(1)}) custom-call(s32[2,16]{1,0:T(2,128)S(1)} %get-tuple-element.88.pages_ref, s32[1,16]{1,0:T(1,128)S(1)} %get-tuple-element.89.len_ref, bf16[16,64,128]{2,1,0:T(8,128)(2,1)S(1)} %copy-done.1, bf16[512,1024]{1,0:T(8,128)(2,1)S(1)} %get-tuple-element.91.store_ref, ...), custom_call_target="tpu_custom_call" | custom-call | flops 2147483648 | bytes 4194304 | tf_op jit(solution)/shard_map/cond/branch_1_fun/pallas_call | solution.py:298
  26.8 7.3 %all-to-all-done.1.back_ref = s16[8,272,128]{2,1,0:T(8,128)(2,1)S(1)} async-done(((s16[8,272,128]{2,1,0:T(8,128)(2,1)}), s16[8,272,128]{2,1,0:T(8,128)(2,1)S(1)}, u32[]{:S(2)}, u32[]{:S(2)}) %all-to-all-start.1) | async-done | bytes 557088 | tf_op jit(solution)/shard_map/cond/branch_1_fun/all_to_all | solution.py:340
  34.0 0.9 %branch_1_fun.7 = bf16[16,64,128]{2,1,0:T(8,128)(2,1)S(1)} custom-call(s32[1,16]{1,0:T(1,128)S(1)} %get-tuple-element.83.owner_ref, s16[8,272,128]{2,1,0:T(8,128)(2,1)S(1)} %all-to-all-done.1.back_ref, f32[4,256,128]{2,1,0:T(8,128)S(1)} %get-tuple-element.93.own_ref, f32[8,256]{1,0:T(8,128)S(1)} %get-tuple-element.94.own_stat_ref), custom_call_target="tpu_custom_call" | custom-call | tf_op jit(solution)/shard_map/cond/branch_1_fun/pallas_call | solution.py:298
  34.9 0.0 copy-start.2
  34.9 0.7 %copy-done.2 = bf16[1,16,2,4096]{3,2,1,0:T(2,128)(2,1)} copy-done((bf16[1,16,2,4096]{3,2,1,0:T(2,128)(2,1)}, bf16[1,16,2,4096]{3,2,1,0:T(2,128)(2,1)S(1)}, u32[]{:S(2)}) %copy-start.2) | copy-done | bytes 262168
Async XLA Ops:
  0.0 18.6 %copy-start = (bf16[1,512,1024]{2,1,0:T(8,128)(2,1)S(1)}, bf16[1,512,1024]{2,1,0:T(8,128)(2,1)}, u32[]{:S(2)}) copy-start(bf16[1,512,1024]{2,1,0:T(8,128)(2,1)} %param.13) | copy-start | bytes 3145732
  0.0 18.6 %collective-permute-start = (bf16[512,1024]{1,0:T(8,128)(2,1)}, bf16[512,1024]{1,0:T(8,128)(2,1)S(1)}, u32[]{:S(2)}, u32[]{:S(2)}) collective-permute-start(bf16[512,1024]{1,0:T(8,128)(2,1)} %bitcast.26), channel_id=1, source_target_pairs={{0,8},{8,0},{1,9},{9,1},{2,10},{10,2},{3,11},{11,3},{4,12},{12,4},... | collective-permute-start | bytes 3145736 | tf_op jit(solution)/shard_map/ppermute | solution.py:330
  0.1 18.5 %copy-start.3 = (bf16[16,2,1024]{2,1,0:T(2,128)(2,1)S(1)}, bf16[16,2,1024]{2,1,0:T(2,128)(2,1)}, u32[]{:S(2)}) copy-start(bf16[16,2,1024]{2,1,0:T(2,128)(2,1)} %param.15) | copy-start | bytes 196612
  20.9 3.7 %copy-start.1 = (bf16[16,64,128]{2,1,0:T(8,128)(2,1)S(1)}, bf16[16,64,128]{2,1,0:T(8,128)(2,1)}, u32[]{:S(2)}) copy-start(bf16[16,64,128]{2,1,0:T(8,128)(2,1)} %get-tuple-element.90.query_ref) | copy-start | bytes 786436 | tf_op jit(solution)/shard_map/cond
  20.9 13.1 %all-to-all-start.1 = ((s16[8,272,128]{2,1,0:T(8,128)(2,1)}), s16[8,272,128]{2,1,0:T(8,128)(2,1)S(1)}, u32[]{:S(2)}, u32[]{:S(2)}) async-start(s16[8,272,128]{2,1,0:T(8,128)(2,1)} %branch_1_fun.5), calls=%async_computation.1 | async-start | bytes 1114112 | tf_op jit(solution)/shard_map/cond/branch_1_fun/all_to_all | solution.py:340
  34.9 0.7 %copy-start.2 = (bf16[1,16,2,4096]{3,2,1,0:T(2,128)(2,1)}, bf16[1,16,2,4096]{3,2,1,0:T(2,128)(2,1)S(1)}, u32[]{:S(2)}) copy-start(bf16[1,16,2,4096]{3,2,1,0:T(2,128)(2,1)S(1)} %get-tuple-element.130) | copy-start | bytes 786436

commit v5 on v4

--- a/solution.py
+++ b/solution.py
@@ -29,14 +29,25 @@
     return lax.broadcasted_iota(jnp.int32, shape, dim)
 
 
-def slot_ranks(owner_ref, count):
+def slot_ranks(owner_ref, cap, owners):
     owner = owner_ref[...]
-    names = [owner[0, r] for r in range(count)]
-    ranks = []
-    for r in range(count):
-        rank = jnp.int32(0)
-        for earlier in range(r):
-            rank = rank + jnp.where(names[earlier] == names[r], 1, 0)
+    bits = cap.bit_length()
+    per_word = 30 // bits
+    words = [jnp.int32(0)] * -(-owners // per_word)
+    names, ranks = [], []
+    for r in range(owner.shape[1]):
+        name = owner[0, r]
+        word, rank = name // per_word if len(words) > 1 else 0, jnp.int32(0)
+        shift = (name - word * per_word) * bits
+        for k, counts in enumerate(words):
+            here = (word == k) if len(words) > 1 else True
+            count = (counts >> shift) & ((1 << bits) - 1)
+            step = jnp.int32(1) << shift
+            if len(words) > 1:
+                count, step = jnp.where(here, count, 0), jnp.where(here, step, 0)
+            rank = rank + count
+            words[k] = counts + step
+        names.append(name)
         ranks.append(rank)
     return names, ranks
 
@@ -50,14 +61,13 @@
     head_span = cap * HEAD_ROWS
     out_ref[...] = jnp.zeros_like(out_ref)
     meta_ref[...] = jnp.zeros_like(meta_ref)
-    names, ranks = slot_ranks(owner_ref, count)
-    row = iota((16, HEAD_DIM), 0)
+    names, ranks = slot_ranks(owner_ref, cap, out_ref.shape[0])
     for r in range(count):
         d, rank = names[r], ranks[r]
         for g in range(KV_HEADS):
             start = pl.multiple_of(g * head_span + rank * HEAD_ROWS, HEAD_ROWS)
             out_ref[d, pl.ds(start, HEAD_ROWS), :] = query_ref[r, pl.ds(g * HEAD_ROWS, HEAD_ROWS), :]
-        meta_ref[d] = jnp.where(row == rank, parent[0, r].astype(jnp.float32), meta_ref[d])
+        meta_ref[d, pl.ds(rank, 1), :] = jnp.full((1, HEAD_DIM), parent[0, r].astype(jnp.float32))
     out_ref[:, pl.ds(KV_HEADS * head_span, 16), :] = meta_ref[...].astype(jnp.bfloat16)
 
 
@@ -263,7 +273,7 @@
     unit = jnp.exp2(from_codes(codes[2], codes[3], SCALE_STEPS))
     decoded_ref[...] = jnp.concatenate([log_total, unit], axis=1)
 
-    names, ranks = slot_ranks(owner_ref, count)
+    names, ranks = slot_ranks(owner_ref, cap, back_ref.shape[0])
     per_tile = HEAD_DIM // HEAD_ROWS
     place = iota((2 * KV_HEADS, HEAD_DIM), 1) // HEAD_ROWS
     tiles = []
@@ -327,8 +337,6 @@
     tables = (suffix_pages.T, suffix_len.reshape(1, -1), parent_pages, parent_len.reshape(1, -1))
     token_rows = store.shape[0]
 
-    suffix_store = lax.ppermute(store, "role", [(0, 1), (1, 0)])
-
     sent = jax.ShapeDtypeStruct((seq_count, KV_HEADS * head_span + 16, HEAD_DIM), jnp.bfloat16)
     answer = jax.ShapeDtypeStruct((seq_count, KV_HEADS * head_span + STAT_ROWS, HEAD_DIM), jnp.int16)
     result = jax.ShapeDtypeStruct(query_rows.shape, jnp.bfloat16)
@@ -358,16 +366,17 @@
     def idle(query_rows):
         return call(idle_kernel, handed, (owner_row, *tables), [])
 
-    received = lax.cond(decoding, send_queries, idle, query_rows)
-
-    def decode(received, suffix_store, query_rows):
-        received, owner_row, suffix_table, suffix_lengths, parent_pages, parent_lengths = received
+    received, owner_row, *tables = lax.cond(decoding, send_queries, idle, query_rows)
+    store_after, received = lax.optimization_barrier((store, received))
+    suffix_store = lax.ppermute(store_after, "role", [(0, 1), (1, 0)])
+
+    def answer_queries(received):
         parents, page_count = parent_pages.shape
         beside = (KV_HEADS, page_count * PAGE, parents * HEAD_DIM)
-        parts = call(
+        return call(
             functools.partial(parent_kernel, cap, chunk),
             answer,
-            (parent_pages, parent_lengths, received, store),
+            (*tables[2:], received, store),
             [
                 pltpu.VMEM(answer.shape, jnp.int16),
                 pltpu.VMEM(beside, jnp.bfloat16),
@@ -376,11 +385,15 @@
             ],
             out_space=pl.ANY,
         )
+
+    parts = lax.cond(decoding, answer_queries, lambda _: jnp.zeros(answer.shape, answer.dtype), received)
+
+    def decode(parts, suffix_store, query_rows):
         back = exchange(parts)
         own, own_stats = call(
             local_kernel,
             (jax.ShapeDtypeStruct(part, jnp.float32), jax.ShapeDtypeStruct((2 * KV_HEADS, rows), jnp.float32)),
-            (suffix_table, suffix_lengths, query_rows, suffix_store, head_rows(step_kv)),
+            (*tables[:2], query_rows, suffix_store, head_rows(step_kv)),
             [bias],
             pl.CostEstimate(flops=1 << 31, bytes_accessed=1 << 22, transcendentals=1 << 20),
         )
@@ -393,12 +406,12 @@
             )
         )
 
-    def prefill(received, suffix_store, query_rows):
+    def prefill(parts, suffix_store, query_rows):
         return tokens_of(
-            call(prefill_kernel, result, (*received[2:4], query_rows, store), [bias])
-        )
-
-    return lax.cond(decoding, decode, prefill, received, suffix_store, query_rows)
+            call(prefill_kernel, result, (*tables[:2], query_rows, store), [bias])
+        )
+
+    return lax.cond(decoding, decode, prefill, parts, suffix_store, query_rows)
 
 
 def solution(mesh):

time: 35.8 us -> 35.3 us (0.986)
  Pallas kernels: 6.85 us -> 7.86 us
  waiting for transfers between devices: 7.26 us -> 6.49 us
  blocking collectives: 17 us -> 16.4 us
    all_to_all x1, waiting for transfers between devices: 7.26 us -> 6.06 us  [exchange(): return lax.all_to_all(block, 'seq', split_axis=0, concat_axis=0, tiled=True)]
    pallas_call x4, Pallas kernels: 6.85 us -> 7.86 us  [call(): pl.pallas_call(kernel, out_shape=out_shape, in_specs=[vmem] * len(arrays)...]
    all_to_all x1, blocking collectives: 17 us -> 16.4 us  [exchange(): return lax.all_to_all(block, 'seq', split_axis=0, concat_axis=0, tiled=True)]
    ppermute x1, waiting for transfers between devices: 0.01 us -> 0.44 us  [local(): suffix_store = lax.ppermute(store_after, 'role', [(0, 1), (1, 0)])]
  transfers between devices with their start and end apart: 2 -> 2, of which waited for: 1 -> 2; matrix products, arithmetic and copies ran while one was open for 0% -> 0% of each run, Pallas kernels for 10% -> 16%
where the time goes in v5:
time: 35.3 us; the launch traced here: 35.1 us
  blocking collectives  16.4 us (46%)
  Pallas kernels  7.86 us (22%)
  waiting for transfers between devices  6.49 us (18%)
  starting transfers between devices  3.54 us (10%)
  local copies, waits for them, and re-layouts  0.71 us (2%)
    all_to_all x1, blocking collectives, exchange(): return lax.all_to_all(block, 'seq', split_axis=0, concat_axis=0, tiled=True)  16.4 us
    pallas_call x4, Pallas kernels, call(): pl.pallas_call(kernel, out_shape=out_shape, in_specs=[vmem] * len(arrays)...  7.86 us
    all_to_all x1, waiting for transfers between devices, exchange(): return lax.all_to_all(block, 'seq', split_axis=0, concat_axis=0, tiled=True)  6.06 us
    all_to_all x1, starting transfers between devices, exchange(): return lax.all_to_all(block, 'seq', split_axis=0, concat_axis=0, tiled=True)  3.54 us
    unnamed x8, local copies, waits for them, and re-layouts  0.71 us
  transfers between devices with their start and end apart: 2, of which 2 were waited for; matrix products, arithmetic and copies ran while one was open for 0% of the time, Pallas kernels for 16%

profile of v5, /device:TPU:1, one launch (start us, length us, event | category | flops | bytes accessed | tf_op | source)
XLA Modules:
  0.0 35.1 jit_solution(433499198093362927)
XLA Ops:
  0.0 0.0 copy-start
  0.0 17.8 %conditional.3 = ((bf16[8,272,128]{2,1,0:T(8,128)(2,1)S(1)}, s32[1,16]{1,0:T(1,128)S(1)}, s32[2,16]{1,0:T(2,128)S(1)}, s32[1,16]{1,0:T(1,128)S(1)}, s32[2,16]{1,0:T(2,128)S(1)}, /*index=5*/s32[1,2]{1,0:T(1,128)S(1)})) conditional(s32[]{:T(128)} %convert_element_type.2, (s32[1,16]{1,0:T(1,128)}, s32[2,16]{1,0:T(2,128)}, s32[1,16]{1,0:T(1,128)}, ...), branch_computations={%region_0.0_spmd, %region_1.0_spmd} | conditional | bytes 1114168 | solution.py:369
  0.0 1.4 %branch_1_fun.4 = (bf16[8,272,128]{2,1,0:T(8,128)(2,1)S(1)}, s32[1,16]{1,0:T(1,128)S(1)}, s32[2,16]{1,0:T(2,128)S(1)}, s32[1,16]{1,0:T(1,128)S(1)}, s32[2,16]{1,0:T(2,128)S(1)}, /*index=5*/s32[1,2]{1,0:T(1,128)S(1)}) custom-call(bf16[16,64,128]{2,1,0:T(8,128)(2,1)} %get-tuple-element.71.query_ref, s32[1,16]{1,0:T(1,128)} %get-tuple-element.72.owner_ref, ...), custom_call_target="tpu_custom_call" | custom-call | tf_op jit(solution)/shard_map/cond/branch_1_fun/pallas_call | solution.py:308
  1.4 16.4 %all_to_all.8 = bf16[8,272,128]{2,1,0:T(8,128)(2,1)S(1)} all-to-all(bf16[8,272,128]{2,1,0:T(8,128)(2,1)S(1)} %get-tuple-element.78), channel_id=1, replica_groups=mesh['groups'=2,'role'=2,'seq'=8] {'seq'}, dimensions={0} | all-to-all | bytes 1114112 | tf_op jit(solution)/shard_map/cond/branch_1_fun/all_to_all | solution.py:348
  17.8 0.0 copy-done
  17.8 0.0 collective-permute-start
  17.8 0.0 copy-start.1
  17.9 0.0 copy-start.3
  17.9 2.3 %conditional.4 = (s16[8,272,128]{2,1,0:T(8,128)(2,1)}) conditional(s32[]{:T(128)} %convert_element_type.2, () %tuple.28, (s32[2,16]{1,0:T(2,128)S(1)}, s32[1,2]{1,0:T(1,128)S(1)}, bf16[8,272,128]{2,1,0:T(8,128)(2,1)S(1)}, bf16[512,1024]{1,0:T(8,128)(2,1)S(1)}) %tuple.42), branch_computations={%region_2.0_spmd, %region_3.0_spmd} | conditional | bytes 557066 | solution.py:389
  17.9 2.3 %branch_1_fun.5 = s16[8,272,128]{2,1,0:T(8,128)(2,1)} custom-call(s32[2,16]{1,0:T(2,128)S(1)} %get-tuple-element.84.pages_ref, s32[1,2]{1,0:T(1,128)S(1)} %get-tuple-element.85.len_ref, bf16[8,272,128]{2,1,0:T(8,128)(2,1)S(1)} %get-tuple-element.86.recv_ref, bf16[512,1024]{1,0:T(8,128)(2,1)S(1)} %get-tuple-element.87.store_ref), custom_call_target="tpu_custom_call" | custom-call | tf_op jit(solution)/shard_map/cond/branch_1_fun/pallas_call | solution.py:308
  20.2 0.4 %collective-permute-done = bf16[512,1024]{1,0:T(8,128)(2,1)} collective-permute-done((bf16[512,1024]{1,0:T(8,128)(2,1)S(1)}, bf16[512,1024]{1,0:T(8,128)(2,1)}, u32[]{:S(2)}, u32[]{:S(2)}) %collective-permute-start) | collective-permute-done | bytes 1048608 | tf_op jit(solution)/shard_map/ppermute | solution.py:371
  20.6 0.0 copy-done.1
  20.6 0.0 copy-done.3
  20.6 13.8 %conditional.5 = (bf16[1,16,2,4096]{3,2,1,0:T(2,128)(2,1)S(1)}) conditional(s32[]{:T(128)} %convert_element_type.2, (s32[2,16]{1,0:T(2,128)S(1)}, s32[1,16]{1,0:T(1,128)S(1)}, bf16[16,64,128]{2,1,0:T(8,128)(2,1)S(1)}, bf16[512,1024]{1,0:T(8,128)(2,1)S(1)}) %tuple.45, (s16[8,272,128]{2,1,0:T(8,128)(2,1)}, bf16[16,2,1024]{2,1,0:T(2,128)(2,1)S(1)}, ...), branch_computations={%region_4.0_spmd, %region_5.0_spmd} | conditional | flops 2147483648 | bytes 5865512 | solution.py:414
  20.6 3.5 %all-to-all-start.1 = ((s16[8,272,128]{2,1,0:T(8,128)(2,1)}), s16[8,272,128]{2,1,0:T(8,128)(2,1)S(1)}, u32[]{:S(2)}, u32[]{:S(2)}) async-start(s16[8,272,128]{2,1,0:T(8,128)(2,1)} %get-tuple-element.93), calls=%async_computation.1 | async-start | bytes 1114112 | tf_op jit(solution)/shard_map/cond/branch_1_fun/all_to_all | solution.py:348
  24.2 3.3 %branch_1_fun.6 = (f32[4,256,128]{2,1,0:T(8,128)S(1)}, f32[8,256]{1,0:T(8,128)S(1)}) custom-call(s32[2,16]{1,0:T(2,128)S(1)} %get-tuple-element.94.pages_ref, s32[1,16]{1,0:T(1,128)S(1)} %get-tuple-element.95.len_ref, bf16[16,64,128]{2,1,0:T(8,128)(2,1)S(1)} %get-tuple-element.96.query_ref, bf16[512,1024]{1,0:T(8,128)(2,1)} %get-tuple-element.97.store_ref, ...), custom_call_target="tpu_custom_call" | custom-call | flops 2147483648 | bytes 4194304 | tf_op jit(solution)/shard_map/cond/branch_1_fun/pallas_call | solution.py:308
  27.5 6.1 %all-to-all-done.1.back_ref = s16[8,272,128]{2,1,0:T(8,128)(2,1)S(1)} async-done(((s16[8,272,128]{2,1,0:T(8,128)(2,1)}), s16[8,272,128]{2,1,0:T(8,128)(2,1)S(1)}, u32[]{:S(2)}, u32[]{:S(2)}) %all-to-all-start.1) | async-done | bytes 557088 | tf_op jit(solution)/shard_map/cond/branch_1_fun/all_to_all | solution.py:348
  33.6 0.8 %branch_1_fun.7 = bf16[16,64,128]{2,1,0:T(8,128)(2,1)S(1)} custom-call(s32[1,16]{1,0:T(1,128)S(1)} %get-tuple-element.92.owner_ref, s16[8,272,128]{2,1,0:T(8,128)(2,1)S(1)} %all-to-all-done.1.back_ref, f32[4,256,128]{2,1,0:T(8,128)S(1)} %get-tuple-element.99.own_ref, f32[8,256]{1,0:T(8,128)S(1)} %get-tuple-element.100.own_stat_ref), custom_call_target="tpu_custom_call" | custom-call | tf_op jit(solution)/shard_map/cond/branch_1_fun/pallas_call | solution.py:308
  34.4 0.0 copy-start.2
  34.4 0.7 %copy-done.2 = bf16[1,16,2,4096]{3,2,1,0:T(2,128)(2,1)} copy-done((bf16[1,16,2,4096]{3,2,1,0:T(2,128)(2,1)}, bf16[1,16,2,4096]{3,2,1,0:T(2,128)(2,1)S(1)}, u32[]{:S(2)}) %copy-start.2) | copy-done | bytes 262168
Async XLA Ops:
  0.0 17.8 %copy-start = (bf16[1,512,1024]{2,1,0:T(8,128)(2,1)S(1)}, bf16[1,512,1024]{2,1,0:T(8,128)(2,1)}, u32[]{:S(2)}) copy-start(bf16[1,512,1024]{2,1,0:T(8,128)(2,1)} %param.15) | copy-start | bytes 3145732
  17.8 2.8 %collective-permute-start = (bf16[512,1024]{1,0:T(8,128)(2,1)S(1)}, bf16[512,1024]{1,0:T(8,128)(2,1)}, u32[]{:S(2)}, u32[]{:S(2)}) collective-permute-start(bf16[512,1024]{1,0:T(8,128)(2,1)S(1)} %bitcast.26), channel_id=1, source_target_pairs={{0,8},{8,0},{1,9},{9,1},{2,10},{10,2},{3,11},{11,3},{4,12},{12,4},... | collective-permute-start | bytes 3145736 | tf_op jit(solution)/shard_map/ppermute | solution.py:371
  17.8 2.8 %copy-start.1 = (bf16[1,16,2,4096]{3,2,1,0:T(2,128)(2,1)S(1)}, bf16[1,16,2,4096]{3,2,1,0:T(2,128)(2,1)}, u32[]{:S(2)}) copy-start(bf16[1,16,2,4096]{3,2,1,0:T(2,128)(2,1)} %param.16) | copy-start | bytes 786436
  17.9 2.8 %copy-start.3 = (bf16[16,2,1024]{2,1,0:T(2,128)(2,1)S(1)}, bf16[16,2,1024]{2,1,0:T(2,128)(2,1)}, u32[]{:S(2)}) copy-start(bf16[16,2,1024]{2,1,0:T(2,128)(2,1)} %param.17) | copy-start | bytes 196612
  20.6 12.9 %all-to-all-start.1 = ((s16[8,272,128]{2,1,0:T(8,128)(2,1)}), s16[8,272,128]{2,1,0:T(8,128)(2,1)S(1)}, u32[]{:S(2)}, u32[]{:S(2)}) async-start(s16[8,272,128]{2,1,0:T(8,128)(2,1)} %get-tuple-element.93), calls=%async_computation.1 | async-start | bytes 1114112 | tf_op jit(solution)/shard_map/cond/branch_1_fun/all_to_all | solution.py:348
  34.4 0.7 %copy-start.2 = (bf16[1,16,2,4096]{3,2,1,0:T(2,128)(2,1)}, bf16[1,16,2,4096]{3,2,1,0:T(2,128)(2,1)S(1)}, u32[]{:S(2)}) copy-start(bf16[1,16,2,4096]{3,2,1,0:T(2,128)(2,1)S(1)} %get-tuple-element.141) | copy-start | bytes 786436

commit v6 on v5

--- a/solution.py
+++ b/solution.py
@@ -52,23 +52,32 @@
     return names, ranks
 
 
-def pack_kernel(cap, query_ref, owner_ref, parent_ref, *refs):
-    tables, (out_ref, *copies), meta_ref = refs[: len(refs) // 2 - 1], refs[len(refs) // 2 - 1 : -1], refs[-1]
-    for table, copy in zip((owner_ref, *tables), copies):
-        copy[...] = table[...]
-    parent = parent_ref[...]
+def pack_kernel(cap, query_hbm, owner_hbm, parent_hbm, *refs):
+    *refs, query_ref, parent_ref, meta_ref, sems = refs
+    tables, (out_ref, owner_ref, *copies) = refs[: len(refs) // 2 - 1], refs[len(refs) // 2 - 1 :]
+    moves = [(owner_hbm, owner_ref), (parent_hbm, parent_ref), (query_hbm, query_ref), *zip(tables, copies)]
+    moves = [pltpu.make_async_copy(src, dst, sems.at[k]) for k, (src, dst) in enumerate(moves)]
+    for move in moves:
+        move.start()
     count = query_ref.shape[0]
     head_span = cap * HEAD_ROWS
     out_ref[...] = jnp.zeros_like(out_ref)
     meta_ref[...] = jnp.zeros_like(meta_ref)
+    moves[0].wait()
+    moves[1].wait()
+    parent = parent_ref[...]
     names, ranks = slot_ranks(owner_ref, cap, out_ref.shape[0])
+    for r in range(count):
+        meta_ref[names[r], pl.ds(ranks[r], 1), :] = jnp.full((1, HEAD_DIM), parent[0, r].astype(jnp.float32))
+    out_ref[:, pl.ds(KV_HEADS * head_span, 16), :] = meta_ref[...].astype(jnp.bfloat16)
+    moves[2].wait()
     for r in range(count):
         d, rank = names[r], ranks[r]
         for g in range(KV_HEADS):
             start = pl.multiple_of(g * head_span + rank * HEAD_ROWS, HEAD_ROWS)
             out_ref[d, pl.ds(start, HEAD_ROWS), :] = query_ref[r, pl.ds(g * HEAD_ROWS, HEAD_ROWS), :]
-        meta_ref[d, pl.ds(rank, 1), :] = jnp.full((1, HEAD_DIM), parent[0, r].astype(jnp.float32))
-    out_ref[:, pl.ds(KV_HEADS * head_span, 16), :] = meta_ref[...].astype(jnp.bfloat16)
+    for move in moves[3:]:
+        move.wait()
 
 
 def idle_kernel(*refs):
@@ -302,13 +311,13 @@
             out_ref[r, pl.ds(g * HEAD_ROWS, HEAD_ROWS), :] = merged.astype(jnp.bfloat16)
 
 
-def call(kernel, out_shape, arrays, scratch, cost=None, out_space=pltpu.VMEM):
-    vmem = pl.BlockSpec(memory_space=pltpu.VMEM)
+def call(kernel, out_shape, arrays, scratch, cost=None, in_space=pltpu.VMEM, out_space=pltpu.VMEM):
+    take = pl.BlockSpec(memory_space=in_space)
     put = pl.BlockSpec(memory_space=out_space)
     return pl.pallas_call(
         kernel,
         out_shape=out_shape,
-        in_specs=[vmem] * len(arrays),
+        in_specs=[take] * len(arrays),
         out_specs=jax.tree.map(lambda _: put, out_shape),
         cost_estimate=cost,
         scratch_shapes=scratch,
@@ -359,16 +368,23 @@
             functools.partial(pack_kernel, cap),
             handed,
             (query_rows, owner_row, parent_row, *tables),
-            [pltpu.VMEM((seq_count, 16, HEAD_DIM), jnp.float32)],
-        )
-        return exchange(packed), *copies
+            [
+                pltpu.VMEM(query_rows.shape, jnp.bfloat16),
+                pltpu.VMEM(parent_row.shape, jnp.int32),
+                pltpu.VMEM((seq_count, 16, HEAD_DIM), jnp.float32),
+                pltpu.SemaphoreType.DMA((3 + len(tables),)),
+            ],
+            in_space=pl.ANY,
+        )
+        return packed, *copies
 
     def idle(query_rows):
         return call(idle_kernel, handed, (owner_row, *tables), [])
 
-    received, owner_row, *tables = lax.cond(decoding, send_queries, idle, query_rows)
-    store_after, received = lax.optimization_barrier((store, received))
+    packed, owner_row, *tables = lax.cond(decoding, send_queries, idle, query_rows)
+    store_after, packed = lax.optimization_barrier((store, packed))
     suffix_store = lax.ppermute(store_after, "role", [(0, 1), (1, 0)])
+    received = lax.cond(decoding, exchange, lambda block: jnp.zeros_like(block), packed)
 
     def answer_queries(received):
         parents, page_count = parent_pages.shape

time: 35.3 us -> 35.2 us (level)
  waiting for transfers between devices: 6.49 us -> 6.06 us
    ppermute x1, waiting for transfers between devices: 0.44 us -> 0.01 us  [local(): suffix_store = lax.ppermute(store_after, 'role', [(0, 1), (1, 0)])]
  transfers between devices with their start and end apart: 2 -> 2, of which waited for: 2 -> 1; matrix products, arithmetic and copies ran while one was open for 0% -> 0% of each run, Pallas kernels for 16% -> 16%
where the time goes in v6:
time: 35.2 us; the launch traced here: 34.9 us
  blocking collectives  16.7 us (47%)
  Pallas kernels  7.69 us (22%)
  waiting for transfers between devices  6.06 us (17%)
  starting transfers between devices  3.62 us (10%)
  local copies, waits for them, and re-layouts  0.71 us (2%)
    all_to_all x1, blocking collectives, exchange(): return lax.all_to_all(block, 'seq', split_axis=0, concat_axis=0, tiled=True)  16.7 us
    pallas_call x4, Pallas kernels, call(): pl.pallas_call(kernel, out_shape=out_shape, in_specs=[take] * len(arrays)...  7.69 us
    all_to_all x1, waiting for transfers between devices, exchange(): return lax.all_to_all(block, 'seq', split_axis=0, concat_axis=0, tiled=True)  6.06 us
    all_to_all x1, starting transfers between devices, exchange(): return lax.all_to_all(block, 'seq', split_axis=0, concat_axis=0, tiled=True)  3.55 us
    unnamed x8, local copies, waits for them, and re-layouts  0.71 us
  transfers between devices with their start and end apart: 2, of which 1 were waited for; matrix products, arithmetic and copies ran while one was open for 0% of the time, Pallas kernels for 16%

profile of v6, /device:TPU:1, one launch (start us, length us, event | category | flops | bytes accessed | tf_op | source)
XLA Modules:
  0.0 34.9 jit_solution(4016861917851289987)
XLA Ops:
  0.0 0.0 copy-start
  0.0 1.2 %conditional.4 = ((bf16[8,272,128]{2,1,0:T(8,128)(2,1)S(1)}, s32[1,16]{1,0:T(1,128)S(1)}, s32[2,16]{1,0:T(2,128)S(1)}, s32[1,16]{1,0:T(1,128)S(1)}, s32[2,16]{1,0:T(2,128)S(1)}, /*index=5*/s32[1,2]{1,0:T(1,128)S(1)})) conditional(s32[]{:T(128)} %convert_element_type.2, (s32[1,16]{1,0:T(1,128)}, s32[2,16]{1,0:T(2,128)}, s32[1,16]{1,0:T(1,128)}, ...), branch_computations={%region_0.0_spmd, %region_1.0_spmd} | conditional | bytes 8 | solution.py:384
  0.0 1.2 %branch_1_fun.4 = (bf16[8,272,128]{2,1,0:T(8,128)(2,1)S(1)}, s32[1,16]{1,0:T(1,128)S(1)}, s32[2,16]{1,0:T(2,128)S(1)}, s32[1,16]{1,0:T(1,128)S(1)}, s32[2,16]{1,0:T(2,128)S(1)}, /*index=5*/s32[1,2]{1,0:T(1,128)S(1)}) custom-call(bf16[16,64,128]{2,1,0:T(8,128)(2,1)} %get-tuple-element.75.query_hbm, s32[1,16]{1,0:T(1,128)} %get-tuple-element.76.owner_hbm, ...), custom_call_target="tpu_custom_call" | custom-call | tf_op jit(solution)/shard_map/cond/branch_1_fun/pallas_call | solution.py:317
  1.2 0.1 collective-permute-start
  1.3 16.7 %conditional.5 = (bf16[8,272,128]{2,1,0:T(8,128)(2,1)S(1)}) conditional(s32[]{:T(128)} %convert_element_type.2, () %tuple.34, bf16[8,272,128]{2,1,0:T(8,128)(2,1)S(1)} %get-tuple-element.112), branch_computations={%region_2.0_spmd, %region_3.0_spmd} | conditional | bytes 1114120 | solution.py:387
  1.3 16.7 %all_to_all.8 = bf16[8,272,128]{2,1,0:T(8,128)(2,1)S(1)} all-to-all(bf16[8,272,128]{2,1,0:T(8,128)(2,1)S(1)} %param.3), channel_id=1, replica_groups=mesh['groups'=2,'role'=2,'seq'=8] {'seq'}, dimensions={0} | all-to-all | bytes 1114112 | tf_op jit(solution)/shard_map/cond/branch_1_fun/all_to_all | solution.py:357
  18.1 0.0 copy-done
  18.1 0.0 copy-start.1
  18.1 0.0 copy-start.3
  18.1 2.3 %conditional.6 = (s16[8,272,128]{2,1,0:T(8,128)(2,1)}) conditional(s32[]{:T(128)} %convert_element_type.2, () %tuple.33, (s32[2,16]{1,0:T(2,128)S(1)}, s32[1,2]{1,0:T(1,128)S(1)}, bf16[8,272,128]{2,1,0:T(8,128)(2,1)S(1)}, bf16[512,1024]{1,0:T(8,128)(2,1)S(1)}) %tuple.50), branch_computations={%region_4.0_spmd, %region_5.0_spmd} | conditional | bytes 557066 | solution.py:405
  18.1 2.3 %branch_1_fun.5 = s16[8,272,128]{2,1,0:T(8,128)(2,1)} custom-call(s32[2,16]{1,0:T(2,128)S(1)} %get-tuple-element.82.pages_ref, s32[1,2]{1,0:T(1,128)S(1)} %get-tuple-element.83.len_ref, bf16[8,272,128]{2,1,0:T(8,128)(2,1)S(1)} %get-tuple-element.84.recv_ref, bf16[512,1024]{1,0:T(8,128)(2,1)S(1)} %get-tuple-element.85.store_ref), custom_call_target="tpu_custom_call" | custom-call | tf_op jit(solution)/shard_map/cond/branch_1_fun/pallas_call | solution.py:317
  20.4 0.0 collective-permute-done
  20.4 0.0 copy-done.1
  20.4 0.0 copy-done.3
  20.4 13.8 %conditional.7 = (bf16[1,16,2,4096]{3,2,1,0:T(2,128)(2,1)S(1)}) conditional(s32[]{:T(128)} %convert_element_type.2, (s32[2,16]{1,0:T(2,128)S(1)}, s32[1,16]{1,0:T(1,128)S(1)}, bf16[16,64,128]{2,1,0:T(8,128)(2,1)S(1)}, bf16[512,1024]{1,0:T(8,128)(2,1)S(1)}) %tuple.53, (s16[8,272,128]{2,1,0:T(8,128)(2,1)}, bf16[16,2,1024]{2,1,0:T(2,128)(2,1)S(1)}, ...), branch_computations={%region_6.0_spmd, %region_7.0_spmd} | conditional | flops 2147483648 | bytes 5865512 | solution.py:430
  20.4 3.5 %all-to-all-start.1 = ((s16[8,272,128]{2,1,0:T(8,128)(2,1)}), s16[8,272,128]{2,1,0:T(8,128)(2,1)S(1)}, u32[]{:S(2)}, u32[]{:S(2)}) async-start(s16[8,272,128]{2,1,0:T(8,128)(2,1)} %get-tuple-element.91), calls=%async_computation.1 | async-start | bytes 1114112 | tf_op jit(solution)/shard_map/cond/branch_1_fun/all_to_all | solution.py:357
  24.0 3.3 %branch_1_fun.6 = (f32[4,256,128]{2,1,0:T(8,128)S(1)}, f32[8,256]{1,0:T(8,128)S(1)}) custom-call(s32[2,16]{1,0:T(2,128)S(1)} %get-tuple-element.92.pages_ref, s32[1,16]{1,0:T(1,128)S(1)} %get-tuple-element.93.len_ref, bf16[16,64,128]{2,1,0:T(8,128)(2,1)S(1)} %get-tuple-element.94.query_ref, bf16[512,1024]{1,0:T(8,128)(2,1)} %get-tuple-element.95.store_ref, ...), custom_call_target="tpu_custom_call" | custom-call | flops 2147483648 | bytes 4194304 | tf_op jit(solution)/shard_map/cond/branch_1_fun/pallas_call | solution.py:317
  27.3 6.1 %all-to-all-done.1.back_ref = s16[8,272,128]{2,1,0:T(8,128)(2,1)S(1)} async-done(((s16[8,272,128]{2,1,0:T(8,128)(2,1)}), s16[8,272,128]{2,1,0:T(8,128)(2,1)S(1)}, u32[]{:S(2)}, u32[]{:S(2)}) %all-to-all-start.1) | async-done | bytes 557088 | tf_op jit(solution)/shard_map/cond/branch_1_fun/all_to_all | solution.py:357
  33.4 0.8 %branch_1_fun.7 = bf16[16,64,128]{2,1,0:T(8,128)(2,1)S(1)} custom-call(s32[1,16]{1,0:T(1,128)S(1)} %get-tuple-element.90.owner_ref, s16[8,272,128]{2,1,0:T(8,128)(2,1)S(1)} %all-to-all-done.1.back_ref, f32[4,256,128]{2,1,0:T(8,128)S(1)} %get-tuple-element.97.own_ref, f32[8,256]{1,0:T(8,128)S(1)} %get-tuple-element.98.own_stat_ref), custom_call_target="tpu_custom_call" | custom-call | tf_op jit(solution)/shard_map/cond/branch_1_fun/pallas_call | solution.py:317
  34.2 0.0 copy-start.2
  34.2 0.7 %copy-done.2 = bf16[1,16,2,4096]{3,2,1,0:T(2,128)(2,1)} copy-done((bf16[1,16,2,4096]{3,2,1,0:T(2,128)(2,1)}, bf16[1,16,2,4096]{3,2,1,0:T(2,128)(2,1)S(1)}, u32[]{:S(2)}) %copy-start.2) | copy-done | bytes 262168
Async XLA Ops:
  0.0 18.1 %copy-start = (bf16[1,512,1024]{2,1,0:T(8,128)(2,1)S(1)}, bf16[1,512,1024]{2,1,0:T(8,128)(2,1)}, u32[]{:S(2)}) copy-start(bf16[1,512,1024]{2,1,0:T(8,128)(2,1)} %param.17) | copy-start | bytes 3145732
  1.2 19.2 %collective-permute-start = (bf16[512,1024]{1,0:T(8,128)(2,1)}, bf16[512,1024]{1,0:T(8,128)(2,1)}, u32[]{:S(2)}, u32[]{:S(2)}) collective-permute-start(bf16[512,1024]{1,0:T(8,128)(2,1)} %bitcast.26), channel_id=1, source_target_pairs={{0,8},{8,0},{1,9},{9,1},{2,10},{10,2},{3,11},{11,3},{4,12},{12,4},... | collective-permute-start | bytes 3145736 | tf_op jit(solution)/shard_map/ppermute | solution.py:386
  18.1 2.3 %copy-start.1 = (bf16[1,16,2,4096]{3,2,1,0:T(2,128)(2,1)S(1)}, bf16[1,16,2,4096]{3,2,1,0:T(2,128)(2,1)}, u32[]{:S(2)}) copy-start(bf16[1,16,2,4096]{3,2,1,0:T(2,128)(2,1)} %param.18) | copy-start | bytes 786436
  18.1 2.4 %copy-start.3 = (bf16[16,2,1024]{2,1,0:T(2,128)(2,1)S(1)}, bf16[16,2,1024]{2,1,0:T(2,128)(2,1)}, u32[]{:S(2)}) copy-start(bf16[16,2,1024]{2,1,0:T(2,128)(2,1)} %param.19) | copy-start | bytes 196612
  20.4 13.0 %all-to-all-start.1 = ((s16[8,272,128]{2,1,0:T(8,128)(2,1)}), s16[8,272,128]{2,1,0:T(8,128)(2,1)S(1)}, u32[]{:S(2)}, u32[]{:S(2)}) async-start(s16[8,272,128]{2,1,0:T(8,128)(2,1)} %get-tuple-element.91), calls=%async_computation.1 | async-start | bytes 1114112 | tf_op jit(solution)/shard_map/cond/branch_1_fun/all_to_all | solution.py:357
  34.2 0.7 %copy-start.2 = (bf16[1,16,2,4096]{3,2,1,0:T(2,128)(2,1)}, bf16[1,16,2,4096]{3,2,1,0:T(2,128)(2,1)S(1)}, u32[]{:S(2)}) copy-start(bf16[1,16,2,4096]{3,2,1,0:T(2,128)(2,1)S(1)} %get-tuple-element.141) | copy-start | bytes 786436

commit v7 on v6

--- a/solution.py
+++ b/solution.py
@@ -98,9 +98,33 @@
     return (whole + (rest + 32768.0) * (1.0 / 65536.0)) * (1.0 / steps)
 
 
+def coded_rows(blended):
+    reach = jnp.maximum(jnp.max(jnp.abs(blended), axis=1, keepdims=True), 1e-30)
+    factor = pltpu.reciprocal(reach, approx=True) * CODE_TOP
+    return jnp.round(blended * factor).astype(jnp.int32).astype(jnp.int16), factor
+
+
+def coded_stats(stats):
+    flat = stats.T
+    top, total, factor = (flat[k * KV_HEADS : (k + 1) * KV_HEADS, :] for k in range(3))
+    codes = two_codes(top * SCALE + jnp.log(total), LOG_STEPS)
+    codes += two_codes(-jnp.log2(factor * total), SCALE_STEPS)
+    return jnp.concatenate(codes, axis=0).astype(jnp.int32).astype(jnp.int16)
+
+
+def decoded_stats(codes):
+    codes = codes.astype(jnp.int32).astype(jnp.float32)
+    codes = [codes[..., k * KV_HEADS : (k + 1) * KV_HEADS, :] for k in range(4)]
+    log_total = from_codes(codes[0], codes[1], LOG_STEPS)
+    return jnp.concatenate([log_total, jnp.exp2(from_codes(codes[2], codes[3], SCALE_STEPS))], axis=-2)
+
+
 def parent_kernel(
-    cap, chunk, pages_ref, len_ref, recv_ref, store_ref, out_hbm, out_ref, key_ref, value_ref, sems
+    cap, chunk, pages_ref, len_ref, recv_ref, store_ref, out_ref, spare_hbm, spare_ref, key_ref, value_ref, sem
 ):
+    spare_ref[...] = jnp.zeros_like(spare_ref)
+    spare_copy = pltpu.make_async_copy(spare_ref, spare_hbm, sem)
+    spare_copy.start()
     parents, page_count = pages_ref.shape
     pages, lengths = pages_ref[...], len_ref[...]
     sources = recv_ref.shape[0]
@@ -120,10 +144,6 @@
     lanes = iota((rows, HEAD_DIM), 1)
     positions = iota((rows, tokens), 1)
 
-    def put(c, k):
-        part = (pl.ds(c * chunk, chunk), pl.ds(k * head_span, head_span if k < KV_HEADS else STAT_ROWS))
-        return pltpu.make_async_copy(out_ref.at[part], out_hbm.at[part], sems.at[c, k])
-
     def body(c, carry):
         part = pl.ds(c * chunk, chunk)
         meta = recv_ref[part, pl.ds(KV_HEADS * head_span, 16), :].astype(jnp.float32)
@@ -162,18 +182,11 @@
         blends = [blended_of(g, softmaxes[g][0]) for g in heads]
         stats = jnp.zeros((rows, HEAD_DIM), jnp.float32)
         for g in heads:
-            reach = jnp.maximum(jnp.max(jnp.abs(blends[g]), axis=1, keepdims=True), 1e-30)
-            inverse = pltpu.reciprocal(reach, approx=True) * CODE_TOP
-            coded = jnp.round(blends[g] * inverse).astype(jnp.int32).astype(jnp.int16)
+            coded, factor = coded_rows(blends[g])
             out_ref[part, pl.ds(g * head_span, head_span), :] = coded.reshape(chunk, head_span, HEAD_DIM)
-            put(c, g).start()
-            for k, value in enumerate((softmaxes[g][1], softmaxes[g][2], inverse)):
+            for k, value in enumerate((softmaxes[g][1], softmaxes[g][2], factor)):
                 stats = jnp.where(lanes == k * KV_HEADS + g, value, stats)
-        flat = stats.T
-        top, total, inverse = (flat[k * KV_HEADS : (k + 1) * KV_HEADS, :] for k in range(3))
-        codes = two_codes(top * SCALE + jnp.log(total), LOG_STEPS)
-        codes += two_codes(-jnp.log2(inverse * total), SCALE_STEPS)
-        flat = jnp.concatenate(codes, axis=0).astype(jnp.int32).astype(jnp.int16)
+        flat = coded_stats(stats)
         for j in range(chunk):
             piece = flat[:, j * head_span : (j + 1) * head_span]
             if head_span < HEAD_DIM:
@@ -181,13 +194,10 @@
                     [piece, jnp.zeros((STAT_ROWS, HEAD_DIM - head_span), jnp.int16)], axis=1
                 )
             out_ref[c * chunk + j, pl.ds(KV_HEADS * head_span, STAT_ROWS), :] = piece
-        put(c, KV_HEADS).start()
         return carry
 
     lax.fori_loop(0, sources // chunk, body, 0, unroll=sources == chunk)
-    for c in range(sources // chunk):
-        for k in range(KV_HEADS + 1):
-            put(c, k).wait()
+    spare_copy.wait()
 
 
 def fill_suffix_bias(pages_ref, len_ref, bias_ref, last_of):
@@ -230,9 +240,11 @@
         )
 
 
-def local_kernel(pages_ref, len_ref, query_ref, store_ref, step_ref, out_ref, stat_ref, bias_ref):
+def local_kernel(cap, pages_ref, len_ref, query_ref, store_ref, step_ref, spare_ref, out_ref, bias_ref):
     count = query_ref.shape[0]
     rows = count * HEAD_ROWS
+    head_span = cap * HEAD_ROWS
+    blocks = count // cap
     fill_suffix_bias(pages_ref, len_ref, bias_ref, lambda length, t: length - 1)
     steps = 2 * count
     step_pad = -steps % HEAD_DIM
@@ -254,33 +266,34 @@
         step_keys = jnp.concatenate([step_rows(g), step_bias], axis=1)
         values = store_ref[:, pl.ds(KEY_WIDTH + g * HEAD_DIM, HEAD_DIM)]
         step_values = step_rows(KV_HEADS + g)
-        scores = lax.dot_general(query, keys, NT, preferred_element_type=jnp.float32) * SCALE
-        step_scores = lax.dot_general(query, step_keys, NT, preferred_element_type=jnp.float32) * SCALE
+        scores = lax.dot_general(query, keys, NT, preferred_element_type=jnp.float32)
+        step_scores = lax.dot_general(query, step_keys, NT, preferred_element_type=jnp.float32)
         top = jnp.maximum(
             jnp.max(scores, axis=1, keepdims=True), jnp.max(step_scores, axis=1, keepdims=True)
         )
-        terms = jnp.exp(scores - top)
-        step_terms = jnp.exp(step_scores - top)
+        terms = jnp.exp2((scores - top) * (SCALE * LOG2_E))
+        step_terms = jnp.exp2((step_scores - top) * (SCALE * LOG2_E))
         total = jnp.sum(terms, axis=1, keepdims=True) + jnp.sum(step_terms, axis=1, keepdims=True)
         blended = jnp.dot(terms.astype(jnp.bfloat16), values, preferred_element_type=jnp.float32)
         blended = blended + jnp.dot(
             step_terms.astype(jnp.bfloat16), step_values, preferred_element_type=jnp.float32
         )
-        out_ref[g] = blended
-        stats = jnp.where(lanes == g, top, stats)
-        stats = jnp.where(lanes == KV_HEADS + g, total, stats)
-    stat_ref[...] = stats.T[: 2 * KV_HEADS, :]
-
-
-def merge_kernel(cap, owner_ref, back_ref, own_ref, own_stat_ref, out_ref, decoded_ref):
+        coded, factor = coded_rows(blended)
+        out_ref[:, pl.ds(g * head_span, head_span), :] = coded.reshape(blocks, head_span, HEAD_DIM)
+        for k, value in enumerate((top, total, factor)):
+            stats = jnp.where(lanes == k * KV_HEADS + g, value, stats)
+    flat = coded_stats(stats)
+    for j in range(rows // HEAD_DIM):
+        out_ref[j, pl.ds(KV_HEADS * head_span, STAT_ROWS), :] = flat[:, j * HEAD_DIM : (j + 1) * HEAD_DIM]
+
+
+def merge_kernel(cap, owner_ref, back_ref, own_ref, out_ref, decoded_ref):
     count = out_ref.shape[0]
     rows = count * HEAD_ROWS
     head_span = cap * HEAD_ROWS
-    codes = back_ref[:, pl.ds(KV_HEADS * head_span, STAT_ROWS), :].astype(jnp.int32).astype(jnp.float32)
-    codes = [codes[:, k * KV_HEADS : (k + 1) * KV_HEADS, :] for k in range(4)]
-    log_total = from_codes(codes[0], codes[1], LOG_STEPS)
-    unit = jnp.exp2(from_codes(codes[2], codes[3], SCALE_STEPS))
-    decoded_ref[...] = jnp.concatenate([log_total, unit], axis=1)
+    stat_span = pl.ds(KV_HEADS * head_span, STAT_ROWS)
+    decoded_ref[...] = decoded_stats(back_ref[:, stat_span, :])
+    own = jnp.concatenate([decoded_stats(own_ref[j, stat_span, :]) for j in range(rows // HEAD_DIM)], axis=1)
 
     names, ranks = slot_ranks(owner_ref, cap, back_ref.shape[0])
     per_tile = HEAD_DIM // HEAD_ROWS
@@ -293,12 +306,11 @@
             tile = jnp.where(place == r - first, pltpu.roll(decoded_ref[names[r]], shift, 1), tile)
         tiles.append(tile)
     flat = jnp.concatenate(tiles, axis=1)[:, :rows]
-    part_top, unit = flat[:KV_HEADS], flat[KV_HEADS:]
-    own_top, own_total = own_stat_ref[:KV_HEADS, :], own_stat_ref[KV_HEADS:, :]
+    part_top, own_top = flat[:KV_HEADS], own[:KV_HEADS]
     top = jnp.maximum(own_top, part_top)
     own_weight, part_weight = jnp.exp(own_top - top), jnp.exp(part_top - top)
-    inverse = 1.0 / (own_weight * own_total + part_weight)
-    weights = [own_weight * inverse, unit * part_weight * inverse]
+    inverse = 1.0 / (own_weight + part_weight)
+    weights = [own[KV_HEADS:] * own_weight * inverse, flat[KV_HEADS:] * part_weight * inverse]
     weights.append(jnp.zeros((HEAD_DIM - 2 * KV_HEADS, rows), jnp.float32))
     weights = jnp.concatenate(weights, axis=0).T
     for r in range(count):
@@ -306,19 +318,22 @@
         for g in range(KV_HEADS):
             start = pl.multiple_of(g * head_span + ranks[r] * HEAD_ROWS, HEAD_ROWS)
             part = back_ref[names[r], pl.ds(start, HEAD_ROWS), :].astype(jnp.int32).astype(jnp.float32)
-            merged = own_ref[g, span, :] * weights[span, g : g + 1]
+            own_start = g * head_span + r % cap * HEAD_ROWS
+            own_part = own_ref[r // cap, pl.ds(own_start, HEAD_ROWS), :].astype(jnp.int32).astype(jnp.float32)
+            merged = own_part * weights[span, g : g + 1]
             merged = merged + part * weights[span, KV_HEADS + g : KV_HEADS + g + 1]
             out_ref[r, pl.ds(g * HEAD_ROWS, HEAD_ROWS), :] = merged.astype(jnp.bfloat16)
 
 
 def call(kernel, out_shape, arrays, scratch, cost=None, in_space=pltpu.VMEM, out_space=pltpu.VMEM):
     take = pl.BlockSpec(memory_space=in_space)
-    put = pl.BlockSpec(memory_space=out_space)
+    if not isinstance(out_space, tuple):
+        out_space = jax.tree.map(lambda _: out_space, out_shape)
     return pl.pallas_call(
         kernel,
         out_shape=out_shape,
         in_specs=[take] * len(arrays),
-        out_specs=jax.tree.map(lambda _: put, out_shape),
+        out_specs=jax.tree.map(lambda space: pl.BlockSpec(memory_space=space), out_space),
         cost_estimate=cost,
         scratch_shapes=scratch,
         compiler_params=pltpu.CompilerParams(vmem_limit_bytes=VMEM_BYTES),
@@ -348,6 +363,7 @@
 
     sent = jax.ShapeDtypeStruct((seq_count, KV_HEADS * head_span + 16, HEAD_DIM), jnp.bfloat16)
     answer = jax.ShapeDtypeStruct((seq_count, KV_HEADS * head_span + STAT_ROWS, HEAD_DIM), jnp.int16)
+    own_part = jax.ShapeDtypeStruct((count // cap, *answer.shape[1:]), answer.dtype)
     result = jax.ShapeDtypeStruct(query_rows.shape, jnp.bfloat16)
     bias = pltpu.VMEM((token_rows, HEAD_DIM), jnp.bfloat16)
     rows = count * HEAD_ROWS
@@ -382,52 +398,52 @@
         return call(idle_kernel, handed, (owner_row, *tables), [])
 
     packed, owner_row, *tables = lax.cond(decoding, send_queries, idle, query_rows)
-    store_after, packed = lax.optimization_barrier((store, packed))
-    suffix_store = lax.ppermute(store_after, "role", [(0, 1), (1, 0)])
+    query_after, packed = lax.optimization_barrier((query_rows, packed))
+    decode_query = lax.ppermute(query_after, "role", [(0, 1), (1, 0)])
     received = lax.cond(decoding, exchange, lambda block: jnp.zeros_like(block), packed)
 
-    def answer_queries(received):
+    def answer_queries(received, decode_query):
         parents, page_count = parent_pages.shape
         beside = (KV_HEADS, page_count * PAGE, parents * HEAD_DIM)
         return call(
             functools.partial(parent_kernel, cap, chunk),
-            answer,
+            (answer, own_part),
             (*tables[2:], received, store),
             [
-                pltpu.VMEM(answer.shape, jnp.int16),
+                pltpu.VMEM(own_part.shape, jnp.int16),
                 pltpu.VMEM(beside, jnp.bfloat16),
                 pltpu.VMEM(beside, jnp.bfloat16),
-                pltpu.SemaphoreType.DMA((seq_count // chunk, KV_HEADS + 1)),
+                pltpu.SemaphoreType.DMA,
             ],
-            out_space=pl.ANY,
-        )
-
-    parts = lax.cond(decoding, answer_queries, lambda _: jnp.zeros(answer.shape, answer.dtype), received)
-
-    def decode(parts, suffix_store, query_rows):
-        back = exchange(parts)
-        own, own_stats = call(
-            local_kernel,
-            (jax.ShapeDtypeStruct(part, jnp.float32), jax.ShapeDtypeStruct((2 * KV_HEADS, rows), jnp.float32)),
-            (*tables[:2], query_rows, suffix_store, head_rows(step_kv)),
+            out_space=(pltpu.VMEM, pl.ANY),
+        )
+
+    def attend_own(received, decode_query):
+        return call(
+            functools.partial(local_kernel, cap),
+            (answer, own_part),
+            (*tables[:2], decode_query, store, head_rows(step_kv)),
             [bias],
-            pl.CostEstimate(flops=1 << 31, bytes_accessed=1 << 22, transcendentals=1 << 20),
-        )
+        )
+
+    parts, own = lax.cond(decoding, answer_queries, attend_own, received, decode_query)
+    own = lax.ppermute(own, "role", [(0, 1), (1, 0)])
+    back = lax.cond(decoding, exchange, lambda block: jnp.zeros_like(block), parts)
+
+    def merge(back, own, query_rows):
         return tokens_of(
             call(
                 functools.partial(merge_kernel, cap),
                 result,
-                (owner_row, back, own, own_stats),
+                (owner_row, back, own),
                 [pltpu.VMEM((seq_count, 2 * KV_HEADS, HEAD_DIM), jnp.float32)],
             )
         )
 
-    def prefill(parts, suffix_store, query_rows):
-        return tokens_of(
-            call(prefill_kernel, result, (*tables[:2], query_rows, store), [bias])
-        )
-
-    return lax.cond(decoding, decode, prefill, parts, suffix_store, query_rows)
+    def prefill(back, own, query_rows):
+        return tokens_of(call(prefill_kernel, result, (*tables[:2], query_rows, store), [bias]))
+
+    return lax.cond(decoding, merge, prefill, back, own, query_rows)
 
 
 def solution(mesh):

time: 35.2 us -> 34.6 us (0.983)
  blocking collectives: 16.7 us -> 29.6 us
  waiting for transfers between devices: 6.06 us -> 0.01 us
  Pallas kernels: 7.69 us -> 3.76 us
  starting transfers between devices: 3.62 us -> 0.14 us
    all_to_all x1 -> x2, blocking collectives: 16.7 us -> 29.6 us  [exchange(): return lax.all_to_all(block, 'seq', split_axis=0, concat_axis=0, tiled=True)]
    all_to_all x1 -> x0, waiting for transfers between devices: 6.06 us -> none  [exchange(): return lax.all_to_all(block, 'seq', split_axis=0, concat_axis=0, tiled=True)]
    pallas_call x4 -> x3, Pallas kernels: 7.69 us -> 3.76 us  [call(): pl.pallas_call(kernel, out_shape=out_shape, in_specs=[take] * len(arrays)...]
    all_to_all x1 -> x0, starting transfers between devices: 3.55 us -> none  [exchange(): return lax.all_to_all(block, 'seq', split_axis=0, concat_axis=0, tiled=True)]
  transfers between devices with their start and end apart: 2 -> 2, of which waited for: 1 -> 0; matrix products, arithmetic and copies ran while one was open for 0% -> 0% of each run, Pallas kernels for 16% -> 0%
where the time goes in v7:
time: 34.6 us; the launch traced here: 34.4 us
  blocking collectives  29.6 us (86%)
  Pallas kernels  3.76 us (11%)
  local copies, waits for them, and re-layouts  0.71 us (2%)
    all_to_all x2, blocking collectives, exchange(): return lax.all_to_all(block, 'seq', split_axis=0, concat_axis=0, tiled=True)  29.6 us
    pallas_call x3, Pallas kernels, call(): pl.pallas_call(kernel, out_shape=out_shape, in_specs=[take] * len(arrays)...  3.76 us
    unnamed x8, local copies, waits for them, and re-layouts  0.71 us
  transfers between devices with their start and end apart: 2, of which 0 were waited for; matrix products, arithmetic and copies ran while one was open for 0% of the time, Pallas kernels for 0%

profile of v7, /device:TPU:1, one launch (start us, length us, event | category | flops | bytes accessed | tf_op | source)
XLA Modules:
  0.0 34.4 jit_solution(17382117125646343609)
XLA Ops:
  0.0 0.0 copy-start
  0.0 1.2 %conditional.5 = ((bf16[8,272,128]{2,1,0:T(8,128)(2,1)S(1)}, s32[1,16]{1,0:T(1,128)S(1)}, s32[2,16]{1,0:T(2,128)S(1)}, s32[1,16]{1,0:T(1,128)S(1)}, s32[2,16]{1,0:T(2,128)S(1)}, /*index=5*/s32[1,2]{1,0:T(1,128)S(1)})) conditional(s32[]{:T(128)} %convert_element_type.2, (s32[1,16]{1,0:T(1,128)}, s32[2,16]{1,0:T(2,128)}, s32[1,16]{1,0:T(1,128)}, ...), branch_computations={%region_0.0_spmd, %region_1.0_spmd} | conditional | bytes 8 | solution.py:400
  0.0 1.2 %branch_1_fun.3 = (bf16[8,272,128]{2,1,0:T(8,128)(2,1)S(1)}, s32[1,16]{1,0:T(1,128)S(1)}, s32[2,16]{1,0:T(2,128)S(1)}, s32[1,16]{1,0:T(1,128)S(1)}, s32[2,16]{1,0:T(2,128)S(1)}, /*index=5*/s32[1,2]{1,0:T(1,128)S(1)}) custom-call(bf16[16,64,128]{2,1,0:T(8,128)(2,1)} %get-tuple-element.83.query_hbm, s32[1,16]{1,0:T(1,128)} %get-tuple-element.84.owner_hbm, ...), custom_call_target="tpu_custom_call" | custom-call | tf_op jit(solution)/shard_map/cond/branch_1_fun/pallas_call | solution.py:332
  1.2 0.1 collective-permute-start
  1.3 0.0 copy-start.3
  1.3 16.9 %conditional.6 = (bf16[8,272,128]{2,1,0:T(8,128)(2,1)S(1)}) conditional(s32[]{:T(128)} %convert_element_type.2, () %tuple.48, bf16[8,272,128]{2,1,0:T(8,128)(2,1)S(1)} %get-tuple-element.127), branch_computations={%region_2.0_spmd, %region_3.0_spmd} | conditional | bytes 1114120 | solution.py:403
  1.4 16.8 %all_to_all.8 = bf16[8,272,128]{2,1,0:T(8,128)(2,1)S(1)} all-to-all(bf16[8,272,128]{2,1,0:T(8,128)(2,1)S(1)} %param.3), channel_id=1, replica_groups=mesh['groups'=2,'role'=2,'seq'=8] {'seq'}, dimensions={0} | all-to-all | bytes 1114112 | tf_op jit(solution)/shard_map/cond/branch_1_fun/all_to_all | solution.py:373
  18.2 0.0 collective-permute-done
  18.2 0.0 copy-done
  18.2 0.0 copy-done.3
  18.2 1.7 %conditional.7 = (s16[4,272,128]{2,1,0:T(8,128)(2,1)S(1)}, s16[8,272,128]{2,1,0:T(8,128)(2,1)S(1)}) conditional(s32[]{:T(128)} %convert_element_type.2, (bf16[16,2,1024]{2,1,0:T(2,128)(2,1)S(1)}, s32[2,16]{1,0:T(2,128)S(1)}, s32[1,16]{1,0:T(1,128)S(1)}, bf16[16,64,128]{2,1,0:T(8,128)(2,1)S(1)}, bf16[512,1024]{1,0:T(8,128)(2,1)S(1)}) %tuple.71, ...), branch_computations={%region_4.0_spmd, %region_5.0_spmd} | conditional | bytes 16 | solution.py:429
  18.2 1.7 %branch_1_fun.4 = (s16[8,272,128]{2,1,0:T(8,128)(2,1)S(1)}, s16[4,272,128]{2,1,0:T(8,128)(2,1)S(1)}) custom-call(s32[2,16]{1,0:T(2,128)S(1)} %get-tuple-element.97.pages_ref, s32[1,2]{1,0:T(1,128)S(1)} %get-tuple-element.98.len_ref, bf16[8,272,128]{2,1,0:T(8,128)(2,1)S(1)} %get-tuple-element.99.recv_ref, bf16[512,1024]{1,0:T(8,128)(2,1)S(1)} %get-tuple-element.100.store_ref), custom_call_target="tpu_custom_call" | custom-call | tf_op jit(solution)/shard_map/cond/branch_1_fun/pallas_call | solution.py:332
  20.0 0.1 collective-permute-start.1
  20.0 0.0 copy-start.1
  20.1 12.8 %conditional.8 = (s16[8,272,128]{2,1,0:T(8,128)(2,1)S(1)}) conditional(s32[]{:T(128)} %convert_element_type.2, () %tuple.45, s16[8,272,128]{2,1,0:T(8,128)(2,1)S(1)} %get-tuple-element.128), branch_computations={%region_6.0_spmd, %region_7.0_spmd} | conditional | bytes 1114120 | solution.py:431
  20.1 12.8 %all_to_all.9 = s16[8,272,128]{2,1,0:T(8,128)(2,1)S(1)} all-to-all(s16[8,272,128]{2,1,0:T(8,128)(2,1)S(1)} %param.7), channel_id=1, replica_groups=mesh['groups'=2,'role'=2,'seq'=8] {'seq'}, dimensions={0} | all-to-all | bytes 1114112 | tf_op jit(solution)/shard_map/cond/branch_1_fun/all_to_all | solution.py:373
  32.8 0.0 collective-permute-done.1
  32.8 0.0 copy-done.1
  32.9 0.8 %conditional.9 = (bf16[1,16,2,4096]{3,2,1,0:T(2,128)(2,1)S(1)}) conditional(s32[]{:T(128)} %convert_element_type.2, (s32[2,16]{1,0:T(2,128)S(1)}, s32[1,16]{1,0:T(1,128)S(1)}, bf16[16,64,128]{2,1,0:T(8,128)(2,1)S(1)}, bf16[512,1024]{1,0:T(8,128)(2,1)S(1)}) %tuple.69, (s32[1,16]{1,0:T(1,128)S(1)}, s16[8,272,128]{2,1,0:T(8,128)(2,1)S(1)}, ...), branch_computations={%region_8.0_spmd, %region_9.0_spmd} | conditional | bytes 8 | solution.py:446
  32.9 0.8 %branch_1_fun.5 = bf16[16,64,128]{2,1,0:T(8,128)(2,1)S(1)} custom-call(s32[1,16]{1,0:T(1,128)S(1)} %get-tuple-element.107.owner_ref, s16[8,272,128]{2,1,0:T(8,128)(2,1)S(1)} %get-tuple-element.108.back_ref, s16[4,272,128]{2,1,0:T(8,128)(2,1)S(1)} %get-tuple-element.109.own_ref), custom_call_target="tpu_custom_call" | custom-call | tf_op jit(solution)/shard_map/cond/branch_1_fun/pallas_call | solution.py:332
  33.7 0.0 copy-start.2
  33.7 0.7 %copy-done.2 = bf16[1,16,2,4096]{3,2,1,0:T(2,128)(2,1)} copy-done((bf16[1,16,2,4096]{3,2,1,0:T(2,128)(2,1)}, bf16[1,16,2,4096]{3,2,1,0:T(2,128)(2,1)S(1)}, u32[]{:S(2)}) %copy-start.2) | copy-done | bytes 262168
Async XLA Ops:
  0.0 18.2 %copy-start = (bf16[1,512,1024]{2,1,0:T(8,128)(2,1)S(1)}, bf16[1,512,1024]{2,1,0:T(8,128)(2,1)}, u32[]{:S(2)}) copy-start(bf16[1,512,1024]{2,1,0:T(8,128)(2,1)} %param.19) | copy-start | bytes 3145732
  1.2 17.0 %collective-permute-start = (bf16[16,64,128]{2,1,0:T(8,128)(2,1)}, bf16[16,64,128]{2,1,0:T(8,128)(2,1)S(1)}, u32[]{:S(2)}, u32[]{:S(2)}) collective-permute-start(bf16[16,64,128]{2,1,0:T(8,128)(2,1)} %bitcast.30), channel_id=1, source_target_pairs={{0,8},{8,0},{1,9},{9,1},{2,10},{10,2},{3,11},{11,3},{4,12},{12,4},... | collective-permute-start | bytes 786440 | tf_op jit(solution)/shard_map/ppermute | solution.py:402
  1.3 16.9 %copy-start.3 = (bf16[16,2,1024]{2,1,0:T(2,128)(2,1)S(1)}, bf16[16,2,1024]{2,1,0:T(2,128)(2,1)}, u32[]{:S(2)}) copy-start(bf16[16,2,1024]{2,1,0:T(2,128)(2,1)} %param.21) | copy-start | bytes 196612
  20.0 12.9 %collective-permute-start.1 = (s16[4,272,128]{2,1,0:T(8,128)(2,1)S(1)}, s16[4,272,128]{2,1,0:T(8,128)(2,1)S(1)}, u32[]{:S(2)}, u32[]{:S(2)}) collective-permute-start(s16[4,272,128]{2,1,0:T(8,128)(2,1)S(1)} %get-tuple-element.129), channel_id=1, source_target_pairs={{0,8},{8,0},{1,9},{9,1},{2,10},{10,2},{3,11},{11,3},{4,12},{12,4},... | collective-permute-start | bytes 835592 | tf_op jit(solution)/shard_map/ppermute | solution.py:430
  20.0 12.8 %copy-start.1 = (bf16[1,16,2,4096]{3,2,1,0:T(2,128)(2,1)S(1)}, bf16[1,16,2,4096]{3,2,1,0:T(2,128)(2,1)}, u32[]{:S(2)}) copy-start(bf16[1,16,2,4096]{3,2,1,0:T(2,128)(2,1)} %param.20) | copy-start | bytes 786436
  33.7 0.7 %copy-start.2 = (bf16[1,16,2,4096]{3,2,1,0:T(2,128)(2,1)}, bf16[1,16,2,4096]{3,2,1,0:T(2,128)(2,1)S(1)}, u32[]{:S(2)}) copy-start(bf16[1,16,2,4096]{3,2,1,0:T(2,128)(2,1)S(1)} %get-tuple-element.160) | copy-start | bytes 786436

commit v8 on v7

--- a/solution.py
+++ b/solution.py
@@ -80,10 +80,14 @@
         move.wait()
 
 
-def idle_kernel(*refs):
-    tables, (out_ref, *copies) = refs[: len(refs) // 2], refs[len(refs) // 2 :]
-    out_ref[...] = jnp.zeros_like(out_ref)
-    for table, copy in zip(tables, copies):
+def zero_kernel(*refs):
+    for ref in refs:
+        ref[...] = jnp.zeros_like(ref)
+
+
+def hand_kernel(*refs):
+    half = len(refs) // 2
+    for table, copy in zip(refs[:half], refs[half:]):
         copy[...] = table[...]
 
 
@@ -287,6 +291,22 @@
         out_ref[j, pl.ds(KV_HEADS * head_span, STAT_ROWS), :] = flat[:, j * HEAD_DIM : (j + 1) * HEAD_DIM]
 
 
+def spread_rows(rows):
+    high = rows.astype(jnp.bfloat16)
+    rest = rows - high.astype(jnp.float32)
+    middle = rest.astype(jnp.bfloat16)
+    low = (rest - middle.astype(jnp.float32)).astype(jnp.bfloat16)
+    count = rows.shape[0]
+    shape = (3 * count, count * HEAD_DIM)
+    chosen = iota(shape, 0) % count == iota(shape, 1) // HEAD_DIM
+    return lax.dot_general(
+        jnp.concatenate([high, middle, low], axis=0),
+        jnp.where(chosen, 1.0, 0.0).astype(jnp.bfloat16),
+        (((0,), (0,)), ((), ())),
+        preferred_element_type=jnp.float32,
+    )
+
+
 def merge_kernel(cap, owner_ref, back_ref, own_ref, out_ref, decoded_ref):
     count = out_ref.shape[0]
     rows = count * HEAD_ROWS
@@ -311,8 +331,7 @@
     own_weight, part_weight = jnp.exp(own_top - top), jnp.exp(part_top - top)
     inverse = 1.0 / (own_weight + part_weight)
     weights = [own[KV_HEADS:] * own_weight * inverse, flat[KV_HEADS:] * part_weight * inverse]
-    weights.append(jnp.zeros((HEAD_DIM - 2 * KV_HEADS, rows), jnp.float32))
-    weights = jnp.concatenate(weights, axis=0).T
+    weights = spread_rows(jnp.concatenate(weights, axis=0))
     for r in range(count):
         span = slice(r * HEAD_ROWS, (r + 1) * HEAD_ROWS)
         for g in range(KV_HEADS):
@@ -320,8 +339,9 @@
             part = back_ref[names[r], pl.ds(start, HEAD_ROWS), :].astype(jnp.int32).astype(jnp.float32)
             own_start = g * head_span + r % cap * HEAD_ROWS
             own_part = own_ref[r // cap, pl.ds(own_start, HEAD_ROWS), :].astype(jnp.int32).astype(jnp.float32)
-            merged = own_part * weights[span, g : g + 1]
-            merged = merged + part * weights[span, KV_HEADS + g : KV_HEADS + g + 1]
+            merged = own_part * weights[span, g * HEAD_DIM : (g + 1) * HEAD_DIM]
+            k = KV_HEADS + g
+            merged = merged + part * weights[span, k * HEAD_DIM : (k + 1) * HEAD_DIM]
             out_ref[r, pl.ds(g * HEAD_ROWS, HEAD_ROWS), :] = merged.astype(jnp.bfloat16)
 
 
@@ -358,7 +378,8 @@
     chunk = max(1, min(seq_count, 512 // head_span))
     query_rows = head_rows(queries[0])
     owner_row, parent_row = owner.reshape(1, -1), parent_id.reshape(1, -1)
-    tables = (suffix_pages.T, suffix_len.reshape(1, -1), parent_pages, parent_len.reshape(1, -1))
+    parent_tables = (parent_pages, parent_len.reshape(1, -1))
+    suffix_tables = (suffix_pages.T, suffix_len.reshape(1, -1))
     token_rows = store.shape[0]
 
     sent = jax.ShapeDtypeStruct((seq_count, KV_HEADS * head_span + 16, HEAD_DIM), jnp.bfloat16)
@@ -377,30 +398,39 @@
             1, count, pair, width
         )
 
-    handed = (sent, *(jax.ShapeDtypeStruct(t.shape, t.dtype) for t in (owner_row, *tables)))
-
-    def send_queries(query_rows):
-        packed, *copies = call(
+    def like(arrays):
+        return tuple(jax.ShapeDtypeStruct(a.shape, a.dtype) for a in arrays)
+
+    def zeros(shapes):
+        return tuple(jnp.zeros(a.shape, a.dtype) for a in shapes)
+
+    handed = (sent, *like((owner_row, *parent_tables)))
+
+    def pack(query_rows):
+        return call(
             functools.partial(pack_kernel, cap),
             handed,
-            (query_rows, owner_row, parent_row, *tables),
+            (query_rows, owner_row, parent_row, *parent_tables),
             [
                 pltpu.VMEM(query_rows.shape, jnp.bfloat16),
                 pltpu.VMEM(parent_row.shape, jnp.int32),
                 pltpu.VMEM((seq_count, 16, HEAD_DIM), jnp.float32),
-                pltpu.SemaphoreType.DMA((3 + len(tables),)),
+                pltpu.SemaphoreType.DMA((3 + len(parent_tables),)),
             ],
             in_space=pl.ANY,
         )
-        return packed, *copies
-
-    def idle(query_rows):
-        return call(idle_kernel, handed, (owner_row, *tables), [])
-
-    packed, owner_row, *tables = lax.cond(decoding, send_queries, idle, query_rows)
+
+    packed, owner_row, *parent_tables = lax.cond(decoding, pack, lambda _: call(zero_kernel, handed, (), []), query_rows)
     query_after, packed = lax.optimization_barrier((query_rows, packed))
     decode_query = lax.ppermute(query_after, "role", [(0, 1), (1, 0)])
-    received = lax.cond(decoding, exchange, lambda block: jnp.zeros_like(block), packed)
+
+    def send(packed):
+        return exchange(packed), *zeros(suffix_tables)
+
+    def hand_on(packed):
+        return jnp.zeros_like(packed), *call(hand_kernel, like(suffix_tables), suffix_tables, [])
+
+    received, *suffix_tables = lax.cond(decoding, send, hand_on, packed)
 
     def answer_queries(received, decode_query):
         parents, page_count = parent_pages.shape
@@ -408,7 +438,7 @@
         return call(
             functools.partial(parent_kernel, cap, chunk),
             (answer, own_part),
-            (*tables[2:], received, store),
+            (*parent_tables, received, store),
             [
                 pltpu.VMEM(own_part.shape, jnp.int16),
                 pltpu.VMEM(beside, jnp.bfloat16),
@@ -422,7 +452,7 @@
         return call(
             functools.partial(local_kernel, cap),
             (answer, own_part),
-            (*tables[:2], decode_query, store, head_rows(step_kv)),
+            (*suffix_tables, decode_query, store, head_rows(step_kv)),
             [bias],
         )
 
@@ -441,7 +471,7 @@
         )
 
     def prefill(back, own, query_rows):
-        return tokens_of(call(prefill_kernel, result, (*tables[:2], query_rows, store), [bias]))
+        return tokens_of(call(prefill_kernel, result, (*suffix_tables, query_rows, store), [bias]))
 
     return lax.cond(decoding, merge, prefill, back, own, query_rows)
 

time: 34.6 us -> 33.9 us (0.980)
  blocking collectives: 29.6 us -> 29.2 us
    all_to_all x2, blocking collectives: 29.6 us -> 29.2 us  [exchange(): return lax.all_to_all(block, 'seq', split_axis=0, concat_axis=0, tiled=True)]
where the time goes in v8:
time: 33.9 us; the launch traced here: 33.7 us
  blocking collectives  29.2 us (86%)
  Pallas kernels  3.52 us (10%)
  local copies, waits for them, and re-layouts  0.72 us (2%)
    all_to_all x2, blocking collectives, exchange(): return lax.all_to_all(block, 'seq', split_axis=0, concat_axis=0, tiled=True)  29.2 us
    pallas_call x3, Pallas kernels, call(): pl.pallas_call(kernel, out_shape=out_shape, in_specs=[take] * len(arrays)...  3.52 us
    unnamed x8, local copies, waits for them, and re-layouts  0.71 us
  transfers between devices with their start and end apart: 2, of which 0 were waited for; matrix products, arithmetic and copies ran while one was open for 0% of the time, Pallas kernels for 0%

profile of v8, /device:TPU:1, one launch (start us, length us, event | category | flops | bytes accessed | tf_op | source)
XLA Modules:
  0.0 33.7 jit_solution(17906452131023600385)
XLA Ops:
  0.0 0.0 copy-start
  0.0 1.2 %conditional.5 = ((bf16[8,272,128]{2,1,0:T(8,128)(2,1)S(1)}, s32[1,16]{1,0:T(1,128)S(1)}, s32[2,16]{1,0:T(2,128)S(1)}, s32[1,2]{1,0:T(1,128)S(1)})) conditional(s32[]{:T(128)} %convert_element_type.2, () %tuple.45, (s32[16,1]{0,1:T(1,128)}, s32[16]{0:T(128)}, s32[2]{0:T(128)}, bf16[16,64,128]{2,1,0:T(8,128)(2,1)}, s32[2,16]{1,0:T(2,128)}) %tuple.70), branch_computations={%region_0.0_spmd, %region_1.0_spmd} | conditional | bytes 8 | solution.py:423
  0.0 1.2 %branch_1_fun.3 = (bf16[8,272,128]{2,1,0:T(8,128)(2,1)S(1)}, s32[1,16]{1,0:T(1,128)S(1)}, s32[2,16]{1,0:T(2,128)S(1)}, s32[1,2]{1,0:T(1,128)S(1)}) custom-call(bf16[16,64,128]{2,1,0:T(8,128)(2,1)} %get-tuple-element.68.query_hbm, s32[1,16]{1,0:T(1,128)} %bitcast.35, s32[1,16]{1,0:T(1,128)} %bitcast.36, s32[2,16]{1,0:T(2,128)} %get-tuple-element.126.refs_0_, ...), custom_call_target="tpu_custom_call" | custom-call | tf_op jit(solution)/shard_map/cond/branch_1_fun/pallas_call | solution.py:352
  1.2 0.1 collective-permute-start
  1.3 0.0 copy-start.3
  1.3 16.5 %conditional.6 = (bf16[8,272,128]{2,1,0:T(8,128)(2,1)S(1)}, s32[2,16]{1,0:T(2,128)S(1)}, s32[1,16]{1,0:T(1,128)S(1)}) conditional(s32[]{:T(128)} %convert_element_type.2, (s32[16]{0:T(128)}, s32[2,16]{1,0:T(2,128)}) %tuple.74, bf16[8,272,128]{2,1,0:T(8,128)(2,1)S(1)} %get-tuple-element.109), branch_computations={%region_2.0_spmd, %region_3.0_spmd} | conditional | bytes 1114336 | solution.py:433
  1.3 16.4 %all_to_all.8 = bf16[8,272,128]{2,1,0:T(8,128)(2,1)S(1)} all-to-all(bf16[8,272,128]{2,1,0:T(8,128)(2,1)S(1)} %param.3), channel_id=1, replica_groups=mesh['groups'=2,'role'=2,'seq'=8] {'seq'}, dimensions={0} | all-to-all | bytes 1114112 | tf_op jit(solution)/shard_map/cond/branch_1_fun/all_to_all | solution.py:394
  17.8 0.0 collective-permute-done
  17.8 0.0 copy-done
  17.8 0.0 copy-done.3
  17.8 1.7 %conditional.7 = (s16[4,272,128]{2,1,0:T(8,128)(2,1)S(1)}, s16[8,272,128]{2,1,0:T(8,128)(2,1)S(1)}) conditional(s32[]{:T(128)} %convert_element_type.2, (bf16[16,2,1024]{2,1,0:T(2,128)(2,1)S(1)}, s32[2,16]{1,0:T(2,128)S(1)}, s32[1,16]{1,0:T(1,128)S(1)}, bf16[16,64,128]{2,1,0:T(8,128)(2,1)S(1)}, bf16[512,1024]{1,0:T(8,128)(2,1)S(1)}) %tuple.73, ...), branch_computations={%region_4.0_spmd, %region_5.0_spmd} | conditional | bytes 16 | solution.py:459
  17.8 1.7 %branch_1_fun.4 = (s16[8,272,128]{2,1,0:T(8,128)(2,1)S(1)}, s16[4,272,128]{2,1,0:T(8,128)(2,1)S(1)}) custom-call(s32[2,16]{1,0:T(2,128)S(1)} %get-tuple-element.84.pages_ref, s32[1,2]{1,0:T(1,128)S(1)} %get-tuple-element.85.len_ref, bf16[8,272,128]{2,1,0:T(8,128)(2,1)S(1)} %get-tuple-element.86.recv_ref, bf16[512,1024]{1,0:T(8,128)(2,1)S(1)} %get-tuple-element.87.store_ref), custom_call_target="tpu_custom_call" | custom-call | tf_op jit(solution)/shard_map/cond/branch_1_fun/pallas_call | solution.py:352
  19.6 0.1 collective-permute-start.1
  19.6 0.0 copy-start.1
  19.6 12.8 %conditional.8 = (s16[8,272,128]{2,1,0:T(8,128)(2,1)S(1)}) conditional(s32[]{:T(128)} %convert_element_type.2, () %tuple.49, s16[8,272,128]{2,1,0:T(8,128)(2,1)S(1)} %get-tuple-element.117), branch_computations={%region_6.0_spmd, %region_7.0_spmd} | conditional | bytes 1114120 | solution.py:461
  19.7 12.8 %all_to_all.9 = s16[8,272,128]{2,1,0:T(8,128)(2,1)S(1)} all-to-all(s16[8,272,128]{2,1,0:T(8,128)(2,1)S(1)} %param.7), channel_id=1, replica_groups=mesh['groups'=2,'role'=2,'seq'=8] {'seq'}, dimensions={0} | all-to-all | bytes 1114112 | tf_op jit(solution)/shard_map/cond/branch_1_fun/all_to_all | solution.py:394
  32.4 0.0 collective-permute-done.1
  32.4 0.0 copy-done.1
  32.4 0.6 %conditional.9 = (bf16[1,16,2,4096]{3,2,1,0:T(2,128)(2,1)S(1)}) conditional(s32[]{:T(128)} %convert_element_type.2, (s32[2,16]{1,0:T(2,128)S(1)}, s32[1,16]{1,0:T(1,128)S(1)}, bf16[16,64,128]{2,1,0:T(8,128)(2,1)S(1)}, bf16[512,1024]{1,0:T(8,128)(2,1)S(1)}) %tuple.71, (s32[1,16]{1,0:T(1,128)S(1)}, s16[8,272,128]{2,1,0:T(8,128)(2,1)S(1)}, ...), branch_computations={%region_8.0_spmd, %region_9.0_spmd} | conditional | bytes 8 | solution.py:476
  32.4 0.6 %branch_1_fun.5 = bf16[16,64,128]{2,1,0:T(8,128)(2,1)S(1)} custom-call(s32[1,16]{1,0:T(1,128)S(1)} %get-tuple-element.94.owner_ref, s16[8,272,128]{2,1,0:T(8,128)(2,1)S(1)} %get-tuple-element.95.back_ref, s16[4,272,128]{2,1,0:T(8,128)(2,1)S(1)} %get-tuple-element.96.own_ref), custom_call_target="tpu_custom_call" | custom-call | tf_op jit(solution)/shard_map/cond/branch_1_fun/pallas_call | solution.py:352
  33.0 0.0 copy-start.2
  33.0 0.7 %copy-done.2 = bf16[1,16,2,4096]{3,2,1,0:T(2,128)(2,1)} copy-done((bf16[1,16,2,4096]{3,2,1,0:T(2,128)(2,1)}, bf16[1,16,2,4096]{3,2,1,0:T(2,128)(2,1)S(1)}, u32[]{:S(2)}) %copy-start.2) | copy-done | bytes 262168
  (2 shorter events, 0.0 us)
Async XLA Ops:
  0.0 17.8 %copy-start = (bf16[1,512,1024]{2,1,0:T(8,128)(2,1)S(1)}, bf16[1,512,1024]{2,1,0:T(8,128)(2,1)}, u32[]{:S(2)}) copy-start(bf16[1,512,1024]{2,1,0:T(8,128)(2,1)} %param.19) | copy-start | bytes 3145732
  1.2 16.6 %collective-permute-start = (bf16[16,64,128]{2,1,0:T(8,128)(2,1)}, bf16[16,64,128]{2,1,0:T(8,128)(2,1)S(1)}, u32[]{:S(2)}, u32[]{:S(2)}) collective-permute-start(bf16[16,64,128]{2,1,0:T(8,128)(2,1)} %bitcast.30), channel_id=1, source_target_pairs={{0,8},{8,0},{1,9},{9,1},{2,10},{10,2},{3,11},{11,3},{4,12},{12,4},... | collective-permute-start | bytes 786440 | tf_op jit(solution)/shard_map/ppermute | solution.py:425
  1.3 16.5 %copy-start.3 = (bf16[16,2,1024]{2,1,0:T(2,128)(2,1)S(1)}, bf16[16,2,1024]{2,1,0:T(2,128)(2,1)}, u32[]{:S(2)}) copy-start(bf16[16,2,1024]{2,1,0:T(2,128)(2,1)} %param.21) | copy-start | bytes 196612
  19.6 12.9 %collective-permute-start.1 = (s16[4,272,128]{2,1,0:T(8,128)(2,1)S(1)}, s16[4,272,128]{2,1,0:T(8,128)(2,1)S(1)}, u32[]{:S(2)}, u32[]{:S(2)}) collective-permute-start(s16[4,272,128]{2,1,0:T(8,128)(2,1)S(1)} %get-tuple-element.118), channel_id=1, source_target_pairs={{0,8},{8,0},{1,9},{9,1},{2,10},{10,2},{3,11},{11,3},{4,12},{12,4},... | collective-permute-start | bytes 835592 | tf_op jit(solution)/shard_map/ppermute | solution.py:460
  19.6 12.8 %copy-start.1 = (bf16[1,16,2,4096]{3,2,1,0:T(2,128)(2,1)S(1)}, bf16[1,16,2,4096]{3,2,1,0:T(2,128)(2,1)}, u32[]{:S(2)}) copy-start(bf16[1,16,2,4096]{3,2,1,0:T(2,128)(2,1)} %param.20) | copy-start | bytes 786436
  33.0 0.7 %copy-start.2 = (bf16[1,16,2,4096]{3,2,1,0:T(2,128)(2,1)}, bf16[1,16,2,4096]{3,2,1,0:T(2,128)(2,1)S(1)}, u32[]{:S(2)}) copy-start(bf16[1,16,2,4096]{3,2,1,0:T(2,128)(2,1)S(1)} %get-tuple-element.158) | copy-start | bytes 786436

commit v9 on v8

--- a/solution.py
+++ b/solution.py
@@ -21,6 +21,7 @@
 CODE_TOP = 32600.0
 LOG2_E = 1.4426950408889634
 VMEM_BYTES = 48 * 1024 * 1024
+PREFILL_VMEM_BYTES = (64 * 1024 - 1150) * 1024
 
 NT = (((1,), (1,)), ((), ()))
 
@@ -257,8 +258,10 @@
     step_bias = jnp.where(seen, 0.0, MASKED).astype(jnp.bfloat16)
     pad = jnp.zeros((step_pad, HEAD_DIM), jnp.bfloat16)
 
+    step_tiles = [step_ref[r] for r in range(count)]
+
     def step_rows(c):
-        return jnp.concatenate([step_ref[r, 2 * c : 2 * c + 2, :] for r in range(count)] + [pad], axis=0)
+        return jnp.concatenate([step[2 * c : 2 * c + 2, :] for step in step_tiles] + [pad], axis=0)
 
     pick = own_pick(count)
     lanes = iota((rows, HEAD_DIM), 1)
@@ -307,8 +310,14 @@
     )
 
 
-def merge_kernel(cap, owner_ref, back_ref, own_ref, out_ref, decoded_ref):
+def merge_kernel(cap, owner_ref, back_ref, own_ref, out_hbm, out_ref, decoded_ref, sems):
     count = out_ref.shape[0]
+    step = count // sems.shape[0]
+
+    def put(k):
+        part = pl.ds(k * step, step)
+        return pltpu.make_async_copy(out_ref.at[part], out_hbm.at[part], sems.at[k])
+
     rows = count * HEAD_ROWS
     head_span = cap * HEAD_ROWS
     stat_span = pl.ds(KV_HEADS * head_span, STAT_ROWS)
@@ -343,9 +352,13 @@
             k = KV_HEADS + g
             merged = merged + part * weights[span, k * HEAD_DIM : (k + 1) * HEAD_DIM]
             out_ref[r, pl.ds(g * HEAD_ROWS, HEAD_ROWS), :] = merged.astype(jnp.bfloat16)
-
-
-def call(kernel, out_shape, arrays, scratch, cost=None, in_space=pltpu.VMEM, out_space=pltpu.VMEM):
+        if (r + 1) % step == 0:
+            put(r // step).start()
+    for k in range(count // step):
+        put(k).wait()
+
+
+def call(kernel, out_shape, arrays, scratch, cost=None, in_space=pltpu.VMEM, out_space=pltpu.VMEM, grant=VMEM_BYTES):
     take = pl.BlockSpec(memory_space=in_space)
     if not isinstance(out_space, tuple):
         out_space = jax.tree.map(lambda _: out_space, out_shape)
@@ -356,7 +369,7 @@
         out_specs=jax.tree.map(lambda space: pl.BlockSpec(memory_space=space), out_space),
         cost_estimate=cost,
         scratch_shapes=scratch,
-        compiler_params=pltpu.CompilerParams(vmem_limit_bytes=VMEM_BYTES),
+        compiler_params=pltpu.CompilerParams(vmem_limit_bytes=grant),
     )(*arrays)
 
 
@@ -466,12 +479,17 @@
                 functools.partial(merge_kernel, cap),
                 result,
                 (owner_row, back, own),
-                [pltpu.VMEM((seq_count, 2 * KV_HEADS, HEAD_DIM), jnp.float32)],
+                [
+                    pltpu.VMEM(result.shape, jnp.bfloat16),
+                    pltpu.VMEM((seq_count, 2 * KV_HEADS, HEAD_DIM), jnp.float32),
+                    pltpu.SemaphoreType.DMA((4 if count % 4 == 0 else 1,)),
+                ],
+                out_space=pl.ANY,
             )
         )
 
     def prefill(back, own, query_rows):
-        return tokens_of(call(prefill_kernel, result, (*suffix_tables, query_rows, store), [bias]))
+        return tokens_of(call(prefill_kernel, result, (*suffix_tables, query_rows, store), [bias], grant=PREFILL_VMEM_BYTES))
 
     return lax.cond(decoding, merge, prefill, back, own, query_rows)
 

time: 33.9 us -> 33.7 us (level)
  local copies, waits for them, and re-layouts: 0.72 us -> 0.01 us
  Pallas kernels: 3.52 us -> 4.19 us
    unnamed x8 -> x4, local copies, waits for them, and re-layouts: 0.71 us -> 0.01 us
    pallas_call x3, Pallas kernels: 3.52 us -> 4.19 us  [call(): pl.pallas_call(kernel, out_shape=out_shape, in_specs=[take] * len(arrays)...]
where the time goes in v9:
time: 33.7 us; the launch traced here: 33.6 us
  blocking collectives  29.1 us (86%)
  Pallas kernels  4.19 us (12%)
    all_to_all x2, blocking collectives, exchange(): return lax.all_to_all(block, 'seq', split_axis=0, concat_axis=0, tiled=True)  29.1 us
    pallas_call x3, Pallas kernels, call(): pl.pallas_call(kernel, out_shape=out_shape, in_specs=[take] * len(arrays)...  4.19 us
  transfers between devices with their start and end apart: 2, of which 0 were waited for; matrix products, arithmetic and copies ran while one was open for 0% of the time, Pallas kernels for 0%

profile of v9, /device:TPU:1, one launch (start us, length us, event | category | flops | bytes accessed | tf_op | source)
XLA Modules:
  0.0 33.6 jit_solution(6656078499987039314)
XLA Ops:
  0.0 0.0 copy-start
  0.0 1.2 %conditional.5 = ((bf16[8,272,128]{2,1,0:T(8,128)(2,1)S(1)}, s32[1,16]{1,0:T(1,128)S(1)}, s32[2,16]{1,0:T(2,128)S(1)}, s32[1,2]{1,0:T(1,128)S(1)})) conditional(s32[]{:T(128)} %convert_element_type.2, () %tuple.45, (s32[16,1]{0,1:T(1,128)}, s32[16]{0:T(128)}, s32[2]{0:T(128)}, bf16[16,64,128]{2,1,0:T(8,128)(2,1)}, s32[2,16]{1,0:T(2,128)}) %tuple.70), branch_computations={%region_0.0_spmd, %region_1.0_spmd} | conditional | bytes 8 | solution.py:436
  0.0 1.2 %branch_1_fun.3 = (bf16[8,272,128]{2,1,0:T(8,128)(2,1)S(1)}, s32[1,16]{1,0:T(1,128)S(1)}, s32[2,16]{1,0:T(2,128)S(1)}, s32[1,2]{1,0:T(1,128)S(1)}) custom-call(bf16[16,64,128]{2,1,0:T(8,128)(2,1)} %get-tuple-element.68.query_hbm, s32[1,16]{1,0:T(1,128)} %bitcast.35, s32[1,16]{1,0:T(1,128)} %bitcast.36, s32[2,16]{1,0:T(2,128)} %get-tuple-element.126.refs_0_, ...), custom_call_target="tpu_custom_call" | custom-call | tf_op jit(solution)/shard_map/cond/branch_1_fun/pallas_call | solution.py:365
  1.2 0.1 collective-permute-start
  1.3 0.0 copy-start.1
  1.3 16.5 %conditional.6 = (bf16[8,272,128]{2,1,0:T(8,128)(2,1)S(1)}, s32[2,16]{1,0:T(2,128)S(1)}, s32[1,16]{1,0:T(1,128)S(1)}) conditional(s32[]{:T(128)} %convert_element_type.2, (s32[16]{0:T(128)}, s32[2,16]{1,0:T(2,128)}) %tuple.73, bf16[8,272,128]{2,1,0:T(8,128)(2,1)S(1)} %get-tuple-element.109), branch_computations={%region_2.0_spmd, %region_3.0_spmd} | conditional | bytes 1114336 | solution.py:446
  1.3 16.4 %all_to_all.8 = bf16[8,272,128]{2,1,0:T(8,128)(2,1)S(1)} all-to-all(bf16[8,272,128]{2,1,0:T(8,128)(2,1)S(1)} %param.3), channel_id=1, replica_groups=mesh['groups'=2,'role'=2,'seq'=8] {'seq'}, dimensions={0} | all-to-all | bytes 1114112 | tf_op jit(solution)/shard_map/cond/branch_1_fun/all_to_all | solution.py:407
  17.8 0.0 collective-permute-done
  17.8 0.0 copy-done
  17.8 0.0 copy-done.1
  17.8 1.7 %conditional.7 = (s16[4,272,128]{2,1,0:T(8,128)(2,1)S(1)}, s16[8,272,128]{2,1,0:T(8,128)(2,1)S(1)}) conditional(s32[]{:T(128)} %convert_element_type.2, (bf16[16,2,1024]{2,1,0:T(2,128)(2,1)S(1)}, s32[2,16]{1,0:T(2,128)S(1)}, s32[1,16]{1,0:T(1,128)S(1)}, bf16[16,64,128]{2,1,0:T(8,128)(2,1)S(1)}, bf16[512,1024]{1,0:T(8,128)(2,1)S(1)}) %tuple.72, ...), branch_computations={%region_4.0_spmd, %region_5.0_spmd} | conditional | bytes 16 | solution.py:472
  17.8 1.7 %branch_1_fun.4 = (s16[8,272,128]{2,1,0:T(8,128)(2,1)S(1)}, s16[4,272,128]{2,1,0:T(8,128)(2,1)S(1)}) custom-call(s32[2,16]{1,0:T(2,128)S(1)} %get-tuple-element.84.pages_ref, s32[1,2]{1,0:T(1,128)S(1)} %get-tuple-element.85.len_ref, bf16[8,272,128]{2,1,0:T(8,128)(2,1)S(1)} %get-tuple-element.86.recv_ref, bf16[512,1024]{1,0:T(8,128)(2,1)S(1)} %get-tuple-element.87.store_ref), custom_call_target="tpu_custom_call" | custom-call | tf_op jit(solution)/shard_map/cond/branch_1_fun/pallas_call | solution.py:365
  19.6 0.1 collective-permute-start.1
  19.6 12.7 %conditional.8 = (s16[8,272,128]{2,1,0:T(8,128)(2,1)S(1)}) conditional(s32[]{:T(128)} %convert_element_type.2, () %tuple.49, s16[8,272,128]{2,1,0:T(8,128)(2,1)S(1)} %get-tuple-element.117), branch_computations={%region_6.0_spmd, %region_7.0_spmd} | conditional | bytes 1114120 | solution.py:474
  19.7 12.6 %all_to_all.9 = s16[8,272,128]{2,1,0:T(8,128)(2,1)S(1)} all-to-all(s16[8,272,128]{2,1,0:T(8,128)(2,1)S(1)} %param.7), channel_id=1, replica_groups=mesh['groups'=2,'role'=2,'seq'=8] {'seq'}, dimensions={0} | all-to-all | bytes 1114112 | tf_op jit(solution)/shard_map/cond/branch_1_fun/all_to_all | solution.py:407
  32.3 0.0 collective-permute-done.1
  32.3 1.3 %conditional.9 = (bf16[1,16,2,4096]{3,2,1,0:T(2,128)(2,1)}) conditional(s32[]{:T(128)} %convert_element_type.2, (s32[2,16]{1,0:T(2,128)S(1)}, s32[1,16]{1,0:T(1,128)S(1)}, bf16[16,64,128]{2,1,0:T(8,128)(2,1)}, bf16[512,1024]{1,0:T(8,128)(2,1)S(1)}) %tuple.71, (s32[1,16]{1,0:T(1,128)S(1)}, s16[8,272,128]{2,1,0:T(8,128)(2,1)S(1)}, ...), branch_computations={%region_8.0_spmd, %region_9.0_spmd} | conditional | bytes 8 | solution.py:494
  32.3 1.3 %branch_1_fun.5 = bf16[16,64,128]{2,1,0:T(8,128)(2,1)} custom-call(s32[1,16]{1,0:T(1,128)S(1)} %get-tuple-element.94.owner_ref, s16[8,272,128]{2,1,0:T(8,128)(2,1)S(1)} %get-tuple-element.95.back_ref, s16[4,272,128]{2,1,0:T(8,128)(2,1)S(1)} %get-tuple-element.96.own_ref), custom_call_target="tpu_custom_call" | custom-call | tf_op jit(solution)/shard_map/cond/branch_1_fun/pallas_call | solution.py:365
  (2 shorter events, 0.0 us)
Async XLA Ops:
  0.0 17.8 %copy-start = (bf16[1,512,1024]{2,1,0:T(8,128)(2,1)S(1)}, bf16[1,512,1024]{2,1,0:T(8,128)(2,1)}, u32[]{:S(2)}) copy-start(bf16[1,512,1024]{2,1,0:T(8,128)(2,1)} %param.19) | copy-start | bytes 3145732
  1.2 16.6 %collective-permute-start = (bf16[16,64,128]{2,1,0:T(8,128)(2,1)}, bf16[16,64,128]{2,1,0:T(8,128)(2,1)S(1)}, u32[]{:S(2)}, u32[]{:S(2)}) collective-permute-start(bf16[16,64,128]{2,1,0:T(8,128)(2,1)} %bitcast.30), channel_id=1, source_target_pairs={{0,8},{8,0},{1,9},{9,1},{2,10},{10,2},{3,11},{11,3},{4,12},{12,4},... | collective-permute-start | bytes 786440 | tf_op jit(solution)/shard_map/ppermute | solution.py:438
  1.3 16.5 %copy-start.1 = (bf16[16,2,1024]{2,1,0:T(2,128)(2,1)S(1)}, bf16[16,2,1024]{2,1,0:T(2,128)(2,1)}, u32[]{:S(2)}) copy-start(bf16[16,2,1024]{2,1,0:T(2,128)(2,1)} %param.21) | copy-start | bytes 196612
  19.6 12.7 %collective-permute-start.1 = (s16[4,272,128]{2,1,0:T(8,128)(2,1)S(1)}, s16[4,272,128]{2,1,0:T(8,128)(2,1)S(1)}, u32[]{:S(2)}, u32[]{:S(2)}) collective-permute-start(s16[4,272,128]{2,1,0:T(8,128)(2,1)S(1)} %get-tuple-element.118), channel_id=1, source_target_pairs={{0,8},{8,0},{1,9},{9,1},{2,10},{10,2},{3,11},{11,3},{4,12},{12,4},... | collective-permute-start | bytes 835592 | tf_op jit(solution)/shard_map/ppermute | solution.py:473

commit v10 on v9

--- a/solution.py
+++ b/solution.py
@@ -136,14 +136,25 @@
     head_span = cap * HEAD_ROWS
     tokens = page_count * PAGE
     heads = range(KV_HEADS)
-    for p in range(parents):
-        for i in range(page_count):
-            start = pl.multiple_of(pages[p, i] * PAGE, PAGE)
-            page = store_ref[pl.ds(start, PAGE), :]
-            for g in heads:
+    starts = [[pl.multiple_of(pages[p, i] * PAGE, PAGE) for i in range(page_count)] for p in range(parents)]
+
+    def arrange(target_ref, g, column):
+        for p in range(parents):
+            for i in range(page_count):
                 span = (g, pl.ds(i * PAGE, PAGE), pl.ds(p * HEAD_DIM, HEAD_DIM))
-                key_ref[span] = page[:, g * HEAD_DIM : (g + 1) * HEAD_DIM]
-                value_ref[span] = page[:, KEY_WIDTH + g * HEAD_DIM : KEY_WIDTH + (g + 1) * HEAD_DIM]
+                target_ref[span] = store_ref[pl.ds(starts[p][i], PAGE), pl.ds(column, HEAD_DIM)]
+
+    def arrange_keys(g):
+        arrange(key_ref, g, g * HEAD_DIM)
+
+    def arrange_values(g):
+        arrange(value_ref, g, KEY_WIDTH + g * HEAD_DIM)
+
+    at_once = sources == chunk
+    if not at_once:
+        for g in heads:
+            arrange_keys(g)
+            arrange_values(g)
 
     rows = chunk * head_span
     lanes = iota((rows, HEAD_DIM), 1)
@@ -163,6 +174,8 @@
         parent_low = parent.astype(jnp.bfloat16)
 
         def scores_of(g):
+            if at_once:
+                arrange_keys(g)
             query = recv_ref[part, pl.ds(g * head_span, head_span), :].reshape(rows, HEAD_DIM)
             query = jnp.concatenate(
                 [jnp.where(parent_low == p, query, jnp.zeros_like(query)) for p in range(parents)], axis=1
@@ -176,15 +189,22 @@
             return terms.astype(jnp.bfloat16), top, jnp.sum(terms, axis=1, keepdims=True)
 
         def blended_of(g, weights):
+            if at_once:
+                arrange_values(g)
             both = jnp.dot(weights, value_ref[g], preferred_element_type=jnp.float32)
             blended = both[:, :HEAD_DIM]
             for p in range(1, parents):
                 blended = jnp.where(parent == p, both[:, p * HEAD_DIM : (p + 1) * HEAD_DIM], blended)
             return blended
 
-        scores = [scores_of(g) for g in heads]
-        softmaxes = [softmax_of(scores[g]) for g in heads]
-        blends = [blended_of(g, softmaxes[g][0]) for g in heads]
+        scores, softmaxes, blends = {}, {}, {}
+        for g in range(KV_HEADS + 2):
+            if g < KV_HEADS:
+                scores[g] = scores_of(g)
+            if 0 <= g - 1 < KV_HEADS:
+                softmaxes[g - 1] = softmax_of(scores[g - 1])
+            if 0 <= g - 2 < KV_HEADS:
+                blends[g - 2] = blended_of(g - 2, softmaxes[g - 2][0])
         stats = jnp.zeros((rows, HEAD_DIM), jnp.float32)
         for g in heads:
             coded, factor = coded_rows(blends[g])
@@ -193,11 +213,8 @@
                 stats = jnp.where(lanes == k * KV_HEADS + g, value, stats)
         flat = coded_stats(stats)
         for j in range(chunk):
-            piece = flat[:, j * head_span : (j + 1) * head_span]
-            if head_span < HEAD_DIM:
-                piece = jnp.concatenate(
-                    [piece, jnp.zeros((STAT_ROWS, HEAD_DIM - head_span), jnp.int16)], axis=1
-                )
+            first = j * head_span // HEAD_DIM * HEAD_DIM
+            piece = flat[:, first : first + HEAD_DIM]
             out_ref[c * chunk + j, pl.ds(KV_HEADS * head_span, STAT_ROWS), :] = piece
         return carry
 
@@ -325,13 +342,14 @@
     own = jnp.concatenate([decoded_stats(own_ref[j, stat_span, :]) for j in range(rows // HEAD_DIM)], axis=1)
 
     names, ranks = slot_ranks(owner_ref, cap, back_ref.shape[0])
+    here = lax.rem(lax.axis_index("seq") * head_span, HEAD_DIM)
     per_tile = HEAD_DIM // HEAD_ROWS
     place = iota((2 * KV_HEADS, HEAD_DIM), 1) // HEAD_ROWS
     tiles = []
     for first in range(0, count, per_tile):
         tile = jnp.zeros((2 * KV_HEADS, HEAD_DIM), jnp.float32)
         for r in range(first, min(first + per_tile, count)):
-            shift = lax.rem((r - first) * HEAD_ROWS - ranks[r] * HEAD_ROWS + HEAD_DIM, HEAD_DIM)
+            shift = lax.rem((r - first) * HEAD_ROWS - ranks[r] * HEAD_ROWS - here + 2 * HEAD_DIM, HEAD_DIM)
             tile = jnp.where(place == r - first, pltpu.roll(decoded_ref[names[r]], shift, 1), tile)
         tiles.append(tile)
     flat = jnp.concatenate(tiles, axis=1)[:, :rows]

time: 33.7 us -> 33.6 us (level)
  no operation moved by 1% of the time
where the time goes in v10:
time: 33.6 us; the launch traced here: 33.4 us
  blocking collectives  29.1 us (87%)
  Pallas kernels  4.04 us (12%)
    all_to_all x2, blocking collectives, exchange(): return lax.all_to_all(block, 'seq', split_axis=0, concat_axis=0, tiled=True)  29.1 us
    pallas_call x3, Pallas kernels, call(): pl.pallas_call(kernel, out_shape=out_shape, in_specs=[take] * len(arrays)...  4.04 us
  transfers between devices with their start and end apart: 2, of which 0 were waited for; matrix products, arithmetic and copies ran while one was open for 0% of the time, Pallas kernels for 0%

profile of v10, /device:TPU:1, one launch (start us, length us, event | category | flops | bytes accessed | tf_op | source)
XLA Modules:
  0.0 33.4 jit_solution(10722894909465507859)
XLA Ops:
  0.0 0.0 copy-start
  0.0 1.2 %conditional.5 = ((bf16[8,272,128]{2,1,0:T(8,128)(2,1)S(1)}, s32[1,16]{1,0:T(1,128)S(1)}, s32[2,16]{1,0:T(2,128)S(1)}, s32[1,2]{1,0:T(1,128)S(1)})) conditional(s32[]{:T(128)} %convert_element_type.2, () %tuple.45, (s32[16,1]{0,1:T(1,128)}, s32[16]{0:T(128)}, s32[2]{0:T(128)}, bf16[16,64,128]{2,1,0:T(8,128)(2,1)}, s32[2,16]{1,0:T(2,128)}) %tuple.70), branch_computations={%region_0.0_spmd, %region_1.0_spmd} | conditional | bytes 8 | solution.py:454
  0.0 1.2 %branch_1_fun.3 = (bf16[8,272,128]{2,1,0:T(8,128)(2,1)S(1)}, s32[1,16]{1,0:T(1,128)S(1)}, s32[2,16]{1,0:T(2,128)S(1)}, s32[1,2]{1,0:T(1,128)S(1)}) custom-call(bf16[16,64,128]{2,1,0:T(8,128)(2,1)} %get-tuple-element.68.query_hbm, s32[1,16]{1,0:T(1,128)} %bitcast.35, s32[1,16]{1,0:T(1,128)} %bitcast.36, s32[2,16]{1,0:T(2,128)} %get-tuple-element.126.refs_0_, ...), custom_call_target="tpu_custom_call" | custom-call | tf_op jit(solution)/shard_map/cond/branch_1_fun/pallas_call | solution.py:383
  1.2 0.1 collective-permute-start
  1.3 0.0 copy-start.1
  1.3 16.5 %conditional.6 = (bf16[8,272,128]{2,1,0:T(8,128)(2,1)S(1)}, s32[2,16]{1,0:T(2,128)S(1)}, s32[1,16]{1,0:T(1,128)S(1)}) conditional(s32[]{:T(128)} %convert_element_type.2, (s32[16]{0:T(128)}, s32[2,16]{1,0:T(2,128)}) %tuple.73, bf16[8,272,128]{2,1,0:T(8,128)(2,1)S(1)} %get-tuple-element.109), branch_computations={%region_2.0_spmd, %region_3.0_spmd} | conditional | bytes 1114336 | solution.py:464
  1.3 16.4 %all_to_all.8 = bf16[8,272,128]{2,1,0:T(8,128)(2,1)S(1)} all-to-all(bf16[8,272,128]{2,1,0:T(8,128)(2,1)S(1)} %param.3), channel_id=1, replica_groups=mesh['groups'=2,'role'=2,'seq'=8] {'seq'}, dimensions={0} | all-to-all | bytes 1114112 | tf_op jit(solution)/shard_map/cond/branch_1_fun/all_to_all | solution.py:425
  17.8 0.0 collective-permute-done
  17.8 0.0 copy-done
  17.8 0.0 copy-done.1
  17.8 1.6 %conditional.7 = (s16[4,272,128]{2,1,0:T(8,128)(2,1)S(1)}, s16[8,272,128]{2,1,0:T(8,128)(2,1)S(1)}) conditional(s32[]{:T(128)} %convert_element_type.2, (bf16[16,2,1024]{2,1,0:T(2,128)(2,1)S(1)}, s32[2,16]{1,0:T(2,128)S(1)}, s32[1,16]{1,0:T(1,128)S(1)}, bf16[16,64,128]{2,1,0:T(8,128)(2,1)S(1)}, bf16[512,1024]{1,0:T(8,128)(2,1)S(1)}) %tuple.72, ...), branch_computations={%region_4.0_spmd, %region_5.0_spmd} | conditional | bytes 16 | solution.py:490
  17.8 1.6 %branch_1_fun.4 = (s16[8,272,128]{2,1,0:T(8,128)(2,1)S(1)}, s16[4,272,128]{2,1,0:T(8,128)(2,1)S(1)}) custom-call(s32[2,16]{1,0:T(2,128)S(1)} %get-tuple-element.84.pages_ref, s32[1,2]{1,0:T(1,128)S(1)} %get-tuple-element.85.len_ref, bf16[8,272,128]{2,1,0:T(8,128)(2,1)S(1)} %get-tuple-element.86.recv_ref, bf16[512,1024]{1,0:T(8,128)(2,1)S(1)} %get-tuple-element.87.store_ref), custom_call_target="tpu_custom_call" | custom-call | tf_op jit(solution)/shard_map/cond/branch_1_fun/pallas_call | solution.py:383
  19.4 0.1 collective-permute-start.1
  19.5 12.7 %conditional.8 = (s16[8,272,128]{2,1,0:T(8,128)(2,1)S(1)}) conditional(s32[]{:T(128)} %convert_element_type.2, () %tuple.49, s16[8,272,128]{2,1,0:T(8,128)(2,1)S(1)} %get-tuple-element.117), branch_computations={%region_6.0_spmd, %region_7.0_spmd} | conditional | bytes 1114120 | solution.py:492
  19.5 12.6 %all_to_all.9 = s16[8,272,128]{2,1,0:T(8,128)(2,1)S(1)} all-to-all(s16[8,272,128]{2,1,0:T(8,128)(2,1)S(1)} %param.7), channel_id=1, replica_groups=mesh['groups'=2,'role'=2,'seq'=8] {'seq'}, dimensions={0} | all-to-all | bytes 1114112 | tf_op jit(solution)/shard_map/cond/branch_1_fun/all_to_all | solution.py:425
  32.1 0.0 collective-permute-done.1
  32.1 1.3 %conditional.9 = (bf16[1,16,2,4096]{3,2,1,0:T(2,128)(2,1)}) conditional(s32[]{:T(128)} %convert_element_type.2, (s32[2,16]{1,0:T(2,128)S(1)}, s32[1,16]{1,0:T(1,128)S(1)}, bf16[16,64,128]{2,1,0:T(8,128)(2,1)}, bf16[512,1024]{1,0:T(8,128)(2,1)S(1)}) %tuple.71, (s32[1,16]{1,0:T(1,128)S(1)}, s16[8,272,128]{2,1,0:T(8,128)(2,1)S(1)}, ...), branch_computations={%region_8.0_spmd, %region_9.0_spmd} | conditional | bytes 8 | solution.py:512
  32.1 1.3 %branch_1_fun.5 = bf16[16,64,128]{2,1,0:T(8,128)(2,1)} custom-call(s32[1,16]{1,0:T(1,128)S(1)} %get-tuple-element.94.owner_ref, s16[8,272,128]{2,1,0:T(8,128)(2,1)S(1)} %get-tuple-element.95.back_ref, s16[4,272,128]{2,1,0:T(8,128)(2,1)S(1)} %get-tuple-element.96.own_ref), custom_call_target="tpu_custom_call" | custom-call | tf_op jit(solution)/shard_map/cond/branch_1_fun/pallas_call | solution.py:383
  (2 shorter events, 0.0 us)
Async XLA Ops:
  0.0 17.8 %copy-start = (bf16[1,512,1024]{2,1,0:T(8,128)(2,1)S(1)}, bf16[1,512,1024]{2,1,0:T(8,128)(2,1)}, u32[]{:S(2)}) copy-start(bf16[1,512,1024]{2,1,0:T(8,128)(2,1)} %param.19) | copy-start | bytes 3145732
  1.2 16.6 %collective-permute-start = (bf16[16,64,128]{2,1,0:T(8,128)(2,1)}, bf16[16,64,128]{2,1,0:T(8,128)(2,1)S(1)}, u32[]{:S(2)}, u32[]{:S(2)}) collective-permute-start(bf16[16,64,128]{2,1,0:T(8,128)(2,1)} %bitcast.30), channel_id=1, source_target_pairs={{0,8},{8,0},{1,9},{9,1},{2,10},{10,2},{3,11},{11,3},{4,12},{12,4},... | collective-permute-start | bytes 786440 | tf_op jit(solution)/shard_map/ppermute | solution.py:456
  1.3 16.5 %copy-start.1 = (bf16[16,2,1024]{2,1,0:T(2,128)(2,1)S(1)}, bf16[16,2,1024]{2,1,0:T(2,128)(2,1)}, u32[]{:S(2)}) copy-start(bf16[16,2,1024]{2,1,0:T(2,128)(2,1)} %param.21) | copy-start | bytes 196612
  19.4 12.7 %collective-permute-start.1 = (s16[4,272,128]{2,1,0:T(8,128)(2,1)S(1)}, s16[4,272,128]{2,1,0:T(8,128)(2,1)S(1)}, u32[]{:S(2)}, u32[]{:S(2)}) collective-permute-start(s16[4,272,128]{2,1,0:T(8,128)(2,1)S(1)} %get-tuple-element.118), channel_id=1, source_target_pairs={{0,8},{8,0},{1,9},{9,1},{2,10},{10,2},{3,11},{11,3},{4,12},{12,4},... | collective-permute-start | bytes 835592 | tf_op jit(solution)/shard_map/ppermute | solution.py:491

commit v11 on v10

--- a/solution.py
+++ b/solution.py
@@ -55,7 +55,8 @@
 
 def pack_kernel(cap, query_hbm, owner_hbm, parent_hbm, *refs):
     *refs, query_ref, parent_ref, meta_ref, sems = refs
-    tables, (out_ref, owner_ref, *copies) = refs[: len(refs) // 2 - 1], refs[len(refs) // 2 - 1 :]
+    half = (len(refs) - 3) // 2
+    tables, (out_ref, owner_ref, rank_ref, *copies) = refs[:half], refs[half:]
     moves = [(owner_hbm, owner_ref), (parent_hbm, parent_ref), (query_hbm, query_ref), *zip(tables, copies)]
     moves = [pltpu.make_async_copy(src, dst, sems.at[k]) for k, (src, dst) in enumerate(moves)]
     for move in moves:
@@ -68,6 +69,10 @@
     moves[1].wait()
     parent = parent_ref[...]
     names, ranks = slot_ranks(owner_ref, cap, out_ref.shape[0])
+    table = jnp.zeros(rank_ref.shape, jnp.int32)
+    for r in range(count):
+        table = jnp.where(iota(rank_ref.shape, 1) == r, ranks[r], table)
+    rank_ref[...] = table
     for r in range(count):
         meta_ref[names[r], pl.ds(ranks[r], 1), :] = jnp.full((1, HEAD_DIM), parent[0, r].astype(jnp.float32))
     out_ref[:, pl.ds(KV_HEADS * head_span, 16), :] = meta_ref[...].astype(jnp.bfloat16)
@@ -327,7 +332,7 @@
     )
 
 
-def merge_kernel(cap, owner_ref, back_ref, own_ref, out_hbm, out_ref, decoded_ref, sems):
+def merge_kernel(cap, owner_ref, rank_ref, back_ref, own_ref, out_hbm, out_ref, decoded_ref, sems):
     count = out_ref.shape[0]
     step = count // sems.shape[0]
 
@@ -341,7 +346,8 @@
     decoded_ref[...] = decoded_stats(back_ref[:, stat_span, :])
     own = jnp.concatenate([decoded_stats(own_ref[j, stat_span, :]) for j in range(rows // HEAD_DIM)], axis=1)
 
-    names, ranks = slot_ranks(owner_ref, cap, back_ref.shape[0])
+    names, ranks = owner_ref[...], rank_ref[...]
+    names, ranks = [names[0, r] for r in range(count)], [ranks[0, r] for r in range(count)]
     here = lax.rem(lax.axis_index("seq") * head_span, HEAD_DIM)
     per_tile = HEAD_DIM // HEAD_ROWS
     place = iota((2 * KV_HEADS, HEAD_DIM), 1) // HEAD_ROWS
@@ -435,7 +441,7 @@
     def zeros(shapes):
         return tuple(jnp.zeros(a.shape, a.dtype) for a in shapes)
 
-    handed = (sent, *like((owner_row, *parent_tables)))
+    handed = (sent, *like((owner_row, owner_row, *parent_tables)))
 
     def pack(query_rows):
         return call(
@@ -451,7 +457,7 @@
             in_space=pl.ANY,
         )
 
-    packed, owner_row, *parent_tables = lax.cond(decoding, pack, lambda _: call(zero_kernel, handed, (), []), query_rows)
+    packed, owner_row, rank_row, *parent_tables = lax.cond(decoding, pack, lambda _: call(zero_kernel, handed, (), []), query_rows)
     query_after, packed = lax.optimization_barrier((query_rows, packed))
     decode_query = lax.ppermute(query_after, "role", [(0, 1), (1, 0)])
 
@@ -496,7 +502,7 @@
             call(
                 functools.partial(merge_kernel, cap),
                 result,
-                (owner_row, back, own),
+                (owner_row, rank_row, back, own),
                 [
                     pltpu.VMEM(result.shape, jnp.bfloat16),
                     pltpu.VMEM((seq_count, 2 * KV_HEADS, HEAD_DIM), jnp.float32),

time: 33.6 us -> 33.6 us (level)
  no operation moved by 1% of the time
where the time goes in v11:
time: 33.6 us; the launch traced here: 33.4 us
  blocking collectives  29.1 us (87%)
  Pallas kernels  4.02 us (12%)
    all_to_all x2, blocking collectives, exchange(): return lax.all_to_all(block, 'seq', split_axis=0, concat_axis=0, tiled=True)  29.1 us
    pallas_call x3, Pallas kernels, call(): pl.pallas_call(kernel, out_shape=out_shape, in_specs=[take] * len(arrays)...  4.02 us
  transfers between devices with their start and end apart: 2, of which 0 were waited for; matrix products, arithmetic and copies ran while one was open for 0% of the time, Pallas kernels for 0%

profile of v11, /device:TPU:1, one launch (start us, length us, event | category | flops | bytes accessed | tf_op | source)
XLA Modules:
  0.0 33.4 jit_solution(5345720296271790876)
XLA Ops:
  0.0 0.0 copy-start
  0.0 1.2 %conditional.5 = ((bf16[8,272,128]{2,1,0:T(8,128)(2,1)S(1)}, s32[1,16]{1,0:T(1,128)S(1)}, s32[1,16]{1,0:T(1,128)S(1)}, s32[2,16]{1,0:T(2,128)S(1)}, s32[1,2]{1,0:T(1,128)S(1)})) conditional(s32[]{:T(128)} %convert_element_type.2, () %tuple.45, (s32[16,1]{0,1:T(1,128)}, s32[16]{0:T(128)}, s32[2]{0:T(128)}, bf16[16,64,128]{2,1,0:T(8,128)(2,1)}, ...), branch_computations={%region_0.0_spmd, %region_1.0_spmd} | conditional | bytes 8 | solution.py:460
  0.0 1.2 %branch_1_fun.3 = (bf16[8,272,128]{2,1,0:T(8,128)(2,1)S(1)}, s32[1,16]{1,0:T(1,128)S(1)}, s32[1,16]{1,0:T(1,128)S(1)}, s32[2,16]{1,0:T(2,128)S(1)}, s32[1,2]{1,0:T(1,128)S(1)}) custom-call(bf16[16,64,128]{2,1,0:T(8,128)(2,1)} %get-tuple-element.70.query_hbm, s32[1,16]{1,0:T(1,128)} %bitcast.35, s32[1,16]{1,0:T(1,128)} %bitcast.36, ...), custom_call_target="tpu_custom_call" | custom-call | tf_op jit(solution)/shard_map/cond/branch_1_fun/pallas_call | solution.py:389
  1.2 0.1 collective-permute-start
  1.3 0.0 copy-start.1
  1.3 16.5 %conditional.6 = (bf16[8,272,128]{2,1,0:T(8,128)(2,1)S(1)}, s32[2,16]{1,0:T(2,128)S(1)}, s32[1,16]{1,0:T(1,128)S(1)}) conditional(s32[]{:T(128)} %convert_element_type.2, (s32[16]{0:T(128)}, s32[2,16]{1,0:T(2,128)}) %tuple.73, bf16[8,272,128]{2,1,0:T(8,128)(2,1)S(1)} %get-tuple-element.113), branch_computations={%region_2.0_spmd, %region_3.0_spmd} | conditional | bytes 1114336 | solution.py:470
  1.3 16.4 %all_to_all.8 = bf16[8,272,128]{2,1,0:T(8,128)(2,1)S(1)} all-to-all(bf16[8,272,128]{2,1,0:T(8,128)(2,1)S(1)} %param.3), channel_id=1, replica_groups=mesh['groups'=2,'role'=2,'seq'=8] {'seq'}, dimensions={0} | all-to-all | bytes 1114112 | tf_op jit(solution)/shard_map/cond/branch_1_fun/all_to_all | solution.py:431
  17.8 0.0 collective-permute-done
  17.8 0.0 copy-done
  17.8 0.0 copy-done.1
  17.8 1.6 %conditional.7 = (s16[4,272,128]{2,1,0:T(8,128)(2,1)S(1)}, s16[8,272,128]{2,1,0:T(8,128)(2,1)S(1)}) conditional(s32[]{:T(128)} %convert_element_type.2, (bf16[16,2,1024]{2,1,0:T(2,128)(2,1)S(1)}, s32[2,16]{1,0:T(2,128)S(1)}, s32[1,16]{1,0:T(1,128)S(1)}, bf16[16,64,128]{2,1,0:T(8,128)(2,1)S(1)}, bf16[512,1024]{1,0:T(8,128)(2,1)S(1)}) %tuple.72, ...), branch_computations={%region_4.0_spmd, %region_5.0_spmd} | conditional | bytes 16 | solution.py:496
  17.8 1.6 %branch_1_fun.4 = (s16[8,272,128]{2,1,0:T(8,128)(2,1)S(1)}, s16[4,272,128]{2,1,0:T(8,128)(2,1)S(1)}) custom-call(s32[2,16]{1,0:T(2,128)S(1)} %get-tuple-element.86.pages_ref, s32[1,2]{1,0:T(1,128)S(1)} %get-tuple-element.87.len_ref, bf16[8,272,128]{2,1,0:T(8,128)(2,1)S(1)} %get-tuple-element.88.recv_ref, bf16[512,1024]{1,0:T(8,128)(2,1)S(1)} %get-tuple-element.89.store_ref), custom_call_target="tpu_custom_call" | custom-call | tf_op jit(solution)/shard_map/cond/branch_1_fun/pallas_call | solution.py:389
  19.4 0.1 collective-permute-start.1
  19.5 12.7 %conditional.8 = (s16[8,272,128]{2,1,0:T(8,128)(2,1)S(1)}) conditional(s32[]{:T(128)} %convert_element_type.2, () %tuple.49, s16[8,272,128]{2,1,0:T(8,128)(2,1)S(1)} %get-tuple-element.122), branch_computations={%region_6.0_spmd, %region_7.0_spmd} | conditional | bytes 1114120 | solution.py:498
  19.5 12.6 %all_to_all.9 = s16[8,272,128]{2,1,0:T(8,128)(2,1)S(1)} all-to-all(s16[8,272,128]{2,1,0:T(8,128)(2,1)S(1)} %param.7), channel_id=1, replica_groups=mesh['groups'=2,'role'=2,'seq'=8] {'seq'}, dimensions={0} | all-to-all | bytes 1114112 | tf_op jit(solution)/shard_map/cond/branch_1_fun/all_to_all | solution.py:431
  32.1 0.0 collective-permute-done.1
  32.1 1.3 %conditional.9 = (bf16[1,16,2,4096]{3,2,1,0:T(2,128)(2,1)}) conditional(s32[]{:T(128)} %convert_element_type.2, (s32[2,16]{1,0:T(2,128)S(1)}, s32[1,16]{1,0:T(1,128)S(1)}, bf16[16,64,128]{2,1,0:T(8,128)(2,1)}, bf16[512,1024]{1,0:T(8,128)(2,1)S(1)}) %tuple.71, (s32[1,16]{1,0:T(1,128)S(1)}, s32[1,16]{1,0:T(1,128)S(1)}, ...), branch_computations={%region_8.0_spmd, %region_9.0_spmd} | conditional | bytes 8 | solution.py:518
  32.1 1.3 %branch_1_fun.5 = bf16[16,64,128]{2,1,0:T(8,128)(2,1)} custom-call(s32[1,16]{1,0:T(1,128)S(1)} %get-tuple-element.96.owner_ref, s32[1,16]{1,0:T(1,128)S(1)} %get-tuple-element.97.rank_ref, s16[8,272,128]{2,1,0:T(8,128)(2,1)S(1)} %get-tuple-element.98.back_ref, s16[4,272,128]{2,1,0:T(8,128)(2,1)S(1)} %get-tuple-element.99.own_ref), custom_call_target="tpu_custom_call" | custom-call | tf_op jit(solution)/shard_map/cond/branch_1_fun/pallas_call | solution.py:389
  (2 shorter events, 0.0 us)
Async XLA Ops:
  0.0 17.8 %copy-start = (bf16[1,512,1024]{2,1,0:T(8,128)(2,1)S(1)}, bf16[1,512,1024]{2,1,0:T(8,128)(2,1)}, u32[]{:S(2)}) copy-start(bf16[1,512,1024]{2,1,0:T(8,128)(2,1)} %param.19) | copy-start | bytes 3145732
  1.2 16.6 %collective-permute-start = (bf16[16,64,128]{2,1,0:T(8,128)(2,1)}, bf16[16,64,128]{2,1,0:T(8,128)(2,1)S(1)}, u32[]{:S(2)}, u32[]{:S(2)}) collective-permute-start(bf16[16,64,128]{2,1,0:T(8,128)(2,1)} %bitcast.30), channel_id=1, source_target_pairs={{0,8},{8,0},{1,9},{9,1},{2,10},{10,2},{3,11},{11,3},{4,12},{12,4},... | collective-permute-start | bytes 786440 | tf_op jit(solution)/shard_map/ppermute | solution.py:462
  1.3 16.5 %copy-start.1 = (bf16[16,2,1024]{2,1,0:T(2,128)(2,1)S(1)}, bf16[16,2,1024]{2,1,0:T(2,128)(2,1)}, u32[]{:S(2)}) copy-start(bf16[16,2,1024]{2,1,0:T(2,128)(2,1)} %param.21) | copy-start | bytes 196612
  19.4 12.7 %collective-permute-start.1 = (s16[4,272,128]{2,1,0:T(8,128)(2,1)S(1)}, s16[4,272,128]{2,1,0:T(8,128)(2,1)S(1)}, u32[]{:S(2)}, u32[]{:S(2)}) collective-permute-start(s16[4,272,128]{2,1,0:T(8,128)(2,1)S(1)} %get-tuple-element.123), channel_id=1, source_target_pairs={{0,8},{8,0},{1,9},{9,1},{2,10},{10,2},{3,11},{11,3},{4,12},{12,4},... | collective-permute-start | bytes 835592 | tf_op jit(solution)/shard_map/ppermute | solution.py:497

commit v12 on v10

--- a/solution.py
+++ b/solution.py
@@ -198,13 +198,12 @@
             return blended
 
         scores, softmaxes, blends = {}, {}, {}
-        for g in range(KV_HEADS + 2):
-            if g < KV_HEADS:
-                scores[g] = scores_of(g)
-            if 0 <= g - 1 < KV_HEADS:
-                softmaxes[g - 1] = softmax_of(scores[g - 1])
-            if 0 <= g - 2 < KV_HEADS:
-                blends[g - 2] = blended_of(g - 2, softmaxes[g - 2][0])
+        for g in heads:
+            scores[g] = scores_of(g)
+        for g in heads:
+            softmaxes[g] = softmax_of(scores[g])
+        for g in heads:
+            blends[g] = blended_of(g, softmaxes[g][0])
         stats = jnp.zeros((rows, HEAD_DIM), jnp.float32)
         for g in heads:
             coded, factor = coded_rows(blends[g])

time: 33.6 us -> 33.6 us (level)
  no operation moved by 1% of the time
where the time goes in v12:
time: 33.6 us; the launch traced here: 33.4 us
  blocking collectives  29.1 us (87%)
  Pallas kernels  4.07 us (12%)
    all_to_all x2, blocking collectives, exchange(): return lax.all_to_all(block, 'seq', split_axis=0, concat_axis=0, tiled=True)  29.1 us
    pallas_call x3, Pallas kernels, call(): pl.pallas_call(kernel, out_shape=out_shape, in_specs=[take] * len(arrays)...  4.07 us
  transfers between devices with their start and end apart: 2, of which 0 were waited for; matrix products, arithmetic and copies ran while one was open for 0% of the time, Pallas kernels for 0%

profile of v12, /device:TPU:1, one launch (start us, length us, event | category | flops | bytes accessed | tf_op | source)
XLA Modules:
  0.0 33.4 jit_solution(9063037853949233253)
XLA Ops:
  0.0 0.0 copy-start
  0.0 1.2 %conditional.5 = ((bf16[8,272,128]{2,1,0:T(8,128)(2,1)S(1)}, s32[1,16]{1,0:T(1,128)S(1)}, s32[2,16]{1,0:T(2,128)S(1)}, s32[1,2]{1,0:T(1,128)S(1)})) conditional(s32[]{:T(128)} %convert_element_type.2, () %tuple.45, (s32[16,1]{0,1:T(1,128)}, s32[16]{0:T(128)}, s32[2]{0:T(128)}, bf16[16,64,128]{2,1,0:T(8,128)(2,1)}, s32[2,16]{1,0:T(2,128)}) %tuple.70), branch_computations={%region_0.0_spmd, %region_1.0_spmd} | conditional | bytes 8 | solution.py:453
  0.0 1.2 %branch_1_fun.3 = (bf16[8,272,128]{2,1,0:T(8,128)(2,1)S(1)}, s32[1,16]{1,0:T(1,128)S(1)}, s32[2,16]{1,0:T(2,128)S(1)}, s32[1,2]{1,0:T(1,128)S(1)}) custom-call(bf16[16,64,128]{2,1,0:T(8,128)(2,1)} %get-tuple-element.68.query_hbm, s32[1,16]{1,0:T(1,128)} %bitcast.35, s32[1,16]{1,0:T(1,128)} %bitcast.36, s32[2,16]{1,0:T(2,128)} %get-tuple-element.126.refs_0_, ...), custom_call_target="tpu_custom_call" | custom-call | tf_op jit(solution)/shard_map/cond/branch_1_fun/pallas_call | solution.py:382
  1.2 0.1 collective-permute-start
  1.3 0.0 copy-start.1
  1.3 16.5 %conditional.6 = (bf16[8,272,128]{2,1,0:T(8,128)(2,1)S(1)}, s32[2,16]{1,0:T(2,128)S(1)}, s32[1,16]{1,0:T(1,128)S(1)}) conditional(s32[]{:T(128)} %convert_element_type.2, (s32[16]{0:T(128)}, s32[2,16]{1,0:T(2,128)}) %tuple.73, bf16[8,272,128]{2,1,0:T(8,128)(2,1)S(1)} %get-tuple-element.109), branch_computations={%region_2.0_spmd, %region_3.0_spmd} | conditional | bytes 1114336 | solution.py:463
  1.3 16.4 %all_to_all.8 = bf16[8,272,128]{2,1,0:T(8,128)(2,1)S(1)} all-to-all(bf16[8,272,128]{2,1,0:T(8,128)(2,1)S(1)} %param.3), channel_id=1, replica_groups=mesh['groups'=2,'role'=2,'seq'=8] {'seq'}, dimensions={0} | all-to-all | bytes 1114112 | tf_op jit(solution)/shard_map/cond/branch_1_fun/all_to_all | solution.py:424
  17.8 0.0 collective-permute-done
  17.8 0.0 copy-done
  17.8 0.0 copy-done.1
  17.8 1.6 %conditional.7 = (s16[4,272,128]{2,1,0:T(8,128)(2,1)S(1)}, s16[8,272,128]{2,1,0:T(8,128)(2,1)S(1)}) conditional(s32[]{:T(128)} %convert_element_type.2, (bf16[16,2,1024]{2,1,0:T(2,128)(2,1)S(1)}, s32[2,16]{1,0:T(2,128)S(1)}, s32[1,16]{1,0:T(1,128)S(1)}, bf16[16,64,128]{2,1,0:T(8,128)(2,1)S(1)}, bf16[512,1024]{1,0:T(8,128)(2,1)S(1)}) %tuple.72, ...), branch_computations={%region_4.0_spmd, %region_5.0_spmd} | conditional | bytes 16 | solution.py:489
  17.8 1.6 %branch_1_fun.4 = (s16[8,272,128]{2,1,0:T(8,128)(2,1)S(1)}, s16[4,272,128]{2,1,0:T(8,128)(2,1)S(1)}) custom-call(s32[2,16]{1,0:T(2,128)S(1)} %get-tuple-element.84.pages_ref, s32[1,2]{1,0:T(1,128)S(1)} %get-tuple-element.85.len_ref, bf16[8,272,128]{2,1,0:T(8,128)(2,1)S(1)} %get-tuple-element.86.recv_ref, bf16[512,1024]{1,0:T(8,128)(2,1)S(1)} %get-tuple-element.87.store_ref), custom_call_target="tpu_custom_call" | custom-call | tf_op jit(solution)/shard_map/cond/branch_1_fun/pallas_call | solution.py:382
  19.4 0.1 collective-permute-start.1
  19.5 12.7 %conditional.8 = (s16[8,272,128]{2,1,0:T(8,128)(2,1)S(1)}) conditional(s32[]{:T(128)} %convert_element_type.2, () %tuple.49, s16[8,272,128]{2,1,0:T(8,128)(2,1)S(1)} %get-tuple-element.117), branch_computations={%region_6.0_spmd, %region_7.0_spmd} | conditional | bytes 1114120 | solution.py:491
  19.5 12.6 %all_to_all.9 = s16[8,272,128]{2,1,0:T(8,128)(2,1)S(1)} all-to-all(s16[8,272,128]{2,1,0:T(8,128)(2,1)S(1)} %param.7), channel_id=1, replica_groups=mesh['groups'=2,'role'=2,'seq'=8] {'seq'}, dimensions={0} | all-to-all | bytes 1114112 | tf_op jit(solution)/shard_map/cond/branch_1_fun/all_to_all | solution.py:424
  32.2 0.0 collective-permute-done.1
  32.2 1.3 %conditional.9 = (bf16[1,16,2,4096]{3,2,1,0:T(2,128)(2,1)}) conditional(s32[]{:T(128)} %convert_element_type.2, (s32[2,16]{1,0:T(2,128)S(1)}, s32[1,16]{1,0:T(1,128)S(1)}, bf16[16,64,128]{2,1,0:T(8,128)(2,1)}, bf16[512,1024]{1,0:T(8,128)(2,1)S(1)}) %tuple.71, (s32[1,16]{1,0:T(1,128)S(1)}, s16[8,272,128]{2,1,0:T(8,128)(2,1)S(1)}, ...), branch_computations={%region_8.0_spmd, %region_9.0_spmd} | conditional | bytes 8 | solution.py:511
  32.2 1.3 %branch_1_fun.5 = bf16[16,64,128]{2,1,0:T(8,128)(2,1)} custom-call(s32[1,16]{1,0:T(1,128)S(1)} %get-tuple-element.94.owner_ref, s16[8,272,128]{2,1,0:T(8,128)(2,1)S(1)} %get-tuple-element.95.back_ref, s16[4,272,128]{2,1,0:T(8,128)(2,1)S(1)} %get-tuple-element.96.own_ref), custom_call_target="tpu_custom_call" | custom-call | tf_op jit(solution)/shard_map/cond/branch_1_fun/pallas_call | solution.py:382
  (2 shorter events, 0.0 us)
Async XLA Ops:
  0.0 17.8 %copy-start = (bf16[1,512,1024]{2,1,0:T(8,128)(2,1)S(1)}, bf16[1,512,1024]{2,1,0:T(8,128)(2,1)}, u32[]{:S(2)}) copy-start(bf16[1,512,1024]{2,1,0:T(8,128)(2,1)} %param.19) | copy-start | bytes 3145732
  1.2 16.6 %collective-permute-start = (bf16[16,64,128]{2,1,0:T(8,128)(2,1)}, bf16[16,64,128]{2,1,0:T(8,128)(2,1)S(1)}, u32[]{:S(2)}, u32[]{:S(2)}) collective-permute-start(bf16[16,64,128]{2,1,0:T(8,128)(2,1)} %bitcast.30), channel_id=1, source_target_pairs={{0,8},{8,0},{1,9},{9,1},{2,10},{10,2},{3,11},{11,3},{4,12},{12,4},... | collective-permute-start | bytes 786440 | tf_op jit(solution)/shard_map/ppermute | solution.py:455
  1.3 16.5 %copy-start.1 = (bf16[16,2,1024]{2,1,0:T(2,128)(2,1)S(1)}, bf16[16,2,1024]{2,1,0:T(2,128)(2,1)}, u32[]{:S(2)}) copy-start(bf16[16,2,1024]{2,1,0:T(2,128)(2,1)} %param.21) | copy-start | bytes 196612
  19.4 12.7 %collective-permute-start.1 = (s16[4,272,128]{2,1,0:T(8,128)(2,1)S(1)}, s16[4,272,128]{2,1,0:T(8,128)(2,1)S(1)}, u32[]{:S(2)}, u32[]{:S(2)}) collective-permute-start(s16[4,272,128]{2,1,0:T(8,128)(2,1)S(1)} %get-tuple-element.118), channel_id=1, source_target_pairs={{0,8},{8,0},{1,9},{9,1},{2,10},{10,2},{3,11},{11,3},{4,12},{12,4},... | collective-permute-start | bytes 835592 | tf_op jit(solution)/shard_map/ppermute | solution.py:490
